TPU v7x, 1024 devices: a whole 8x8x8 slice. The times are simulated.
1024 devices in a mesh: rep: 32 (over x_hi, z), fsdp: 32 (over x_lo, y, core).
Axes of the slice: x: 8 (x_hi: 4, x_lo: 2; x = x_hi * 2 + x_lo), y: 8, z: 8, core: 2. Of those that a mesh axis runs over, the one named last changes fastest.
Arguments:
- acts: bfloat16 [32, 8192, 2048], P('rep', 'fsdp'), may hold values from -6 to 6
- grad_out: bfloat16 [32, 8192, 1024], P('rep', 'fsdp'), may hold values from -0.13258252 to 0.13258252
- inner_weight: float32 [32, 2048, 1024], P('rep', 'fsdp'), may hold values from -0.03 to 0.03
- first_moment: float32 [32, 2048, 1024], P('rep', 'fsdp'), may hold values from -6 to 6
- second_moment: float32 [32, 2048, 1024], P('rep', 'fsdp'), may hold values from 0.1 to 10
- outer_weight: float32 [2048, 1024], P(('fsdp', 'rep')), may hold values from -0.03 to 0.03
- outer_momentum: float32 [2048, 1024], P(('fsdp', 'rep')), may hold values from -0.0006 to 0.0006
Outputs:
- outer_next: float32 [2048, 1024], P(('fsdp', 'rep'))
- momentum_next: float32 [2048, 1024], P(('fsdp', 'rep'))
- weight_next: bfloat16 [2048, 1024], P('fsdp')
All inputs are finite; a program needn't handle non-finite values.
Results may differ from a plain program's by a relative error of at most 0.008.
Values may be sent and summed in bfloat16 or wider, within the bound.
No kernel may reach another device: no remote copies, remote signals or barrier semaphores. Data moves between devices by JAX's collectives and lax.ppermute only.
A program may use at most 32 MiB of HBM per device.

v0:
```python
import jax
import jax.numpy as jnp
from jax import lax
from jax.sharding import PartitionSpec as P

INNER_STEP = 500


def shards(acts, grad_out, inner_weight, first_moment, second_moment, outer_weight, outer_momentum):
    tokens = acts[0]
    cotangent = grad_out[0]
    grad = lax.psum_scatter(
        lax.dot_general(
            tokens, cotangent, (((0,), (0,)), ((), ())), preferred_element_type=jnp.float32
        ).astype(jnp.bfloat16),
        "fsdp",
        scatter_dimension=0,
        tiled=True,
    ).astype(jnp.float32)
    first = 0.9 * first_moment[0] + 0.1 * grad
    second = 0.95 * second_moment[0] + 0.05 * grad * grad
    first_hat = first / (1.0 - 0.9**INNER_STEP)
    second_hat = second / (1.0 - 0.95**INNER_STEP)
    inner_new = inner_weight[0] * (1.0 - 0.0004 * 0.1) - 0.0004 * first_hat / (
        jnp.sqrt(second_hat) + 1e-08
    )
    replicas = lax.axis_size("rep")
    summed = lax.psum_scatter(inner_new, "rep", scatter_dimension=0, tiled=True)
    pseudo = outer_weight - summed / replicas
    momentum_next = 0.9 * outer_momentum + pseudo
    outer_next = outer_weight - 0.7 * (pseudo + 0.9 * momentum_next)
    weight_next = lax.all_gather(outer_next.astype(jnp.bfloat16), "rep", axis=0, tiled=True)
    return (outer_next, momentum_next, weight_next)


def solution(mesh):
    placed = (
        P("rep", "fsdp", None),
        P("rep", "fsdp", None),
        P("rep", "fsdp", None),
        P("rep", "fsdp", None),
        P("rep", "fsdp", None),
        P(("fsdp", "rep"), None),
        P(("fsdp", "rep"), None),
    )
    return jax.shard_map(
        shards,
        mesh=mesh,
        in_specs=placed,
        out_specs=(P(("fsdp", "rep"), None), P(("fsdp", "rep"), None), P("fsdp", None)),
        check_vma=False,
    )
```

profile of v0, /device:TPU:16, one launch (start us, length us, event | category | flops | bytes accessed | tf_op | source)
XLA Modules:
  0.0 563.1 jit_solution(5312899298882462067)
XLA Ops:
  7.2 0.0 copy-start
  7.2 0.0 reduce-scatter.2.cloned.1.call-start
  7.2 1.2 copy-done
  8.4 4.3 convolution_convert_fusion
  12.7 0.0 copy-start.1
  12.7 0.0 copy-start.2
  12.7 0.0 copy-start.3
  12.7 0.0 copy-start.4
  12.7 0.0 copy-start.5
  12.7 0.0 reduce-scatter.2.cloned.1.call-update
  12.7 0.0 all-reduce.3.cloned.1.call-start
  12.8 134.6 %reduce-scatter.2.cloned.1.call-done = bf16[64,1024]{1,0:T(8,128)(2,1)} async-done(((bf16[2048,1024]{1,0:T(8,128)(2,1)}), bf16[64,1024]{1,0:T(8,128)(2,1)}) %reduce-scatter.2.cloned.1.call-update) | async-done | bytes 131088 | tf_op jit(solution)/shard_map/reduce_scatter | solution.py:12
  147.3 0.0 copy-done.1
  147.3 0.0 copy-done.2
  147.3 0.0 copy-done.3
  147.3 1.8 fusion.5
  149.1 0.0 all-reduce.3.cloned.1.call-update
  149.1 1.3 dynamic-slice
  151.1 322.0 %all-reduce.3.cloned.1.call-done = f32[64,1024]{1,0:T(8,128)} async-done(((f32[64,1024]{1,0:T(8,128)}), f32[64,1024]{1,0:T(8,128)}) %all-reduce.3.cloned.1.call-update) | async-done | bytes 262160
  473.1 0.0 copy-done.4
  473.1 0.0 copy-done.5
  473.1 1.4 convert_bitcast_fusion
  474.5 81.1 %all-gather = bf16[32,2,1024]{2,1,0:T(2,128)(2,1)S(1)} all-gather(bf16[1,2,1024]{2,1,0:T(2,128)(2,1)S(1)} %get-tuple-element.3), channel_id=1, replica_groups=mesh['rep'=32,'fsdp'=32] {'rep'}, dimensions={0}, use_global_device_ids=true | all-gather | bytes 135168 | tf_op jit(solution)/shard_map/all_gather | solution.py:32
  555.6 0.7 reshape.13
Async XLA Ops:
  7.2 1.2 copy-start
  7.2 140.1 %reduce-scatter.2.cloned.1.call-start = ((), (), s32[]{:S(2)}) async-start(), calls=%async_computation.1 | async-start | bytes 4325376 | tf_op jit(solution)/shard_map/reduce_scatter | solution.py:12
  12.7 134.7 %copy-start.1 = (f32[1,64,1024]{2,1,0:T(8,128)S(1)}, f32[1,64,1024]{2,1,0:T(8,128)}, u32[]{:S(2)}) copy-start(f32[1,64,1024]{2,1,0:T(8,128)} %param.11) | copy-start | bytes 786436
  12.7 134.7 %copy-start.2 = (f32[1,64,1024]{2,1,0:T(8,128)S(1)}, f32[1,64,1024]{2,1,0:T(8,128)}, u32[]{:S(2)}) copy-start(f32[1,64,1024]{2,1,0:T(8,128)} %param.10) | copy-start | bytes 786436
  12.7 134.7 %copy-start.3 = (f32[1,64,1024]{2,1,0:T(8,128)S(1)}, f32[1,64,1024]{2,1,0:T(8,128)}, u32[]{:S(2)}) copy-start(f32[1,64,1024]{2,1,0:T(8,128)} %param.9) | copy-start | bytes 786436
  12.7 460.4 %copy-start.4 = (f32[2,1024]{1,0:T(2,128)S(1)}, f32[2,1024]{1,0:T(2,128)}, u32[]{:S(2)}) copy-start(f32[2,1024]{1,0:T(2,128)} %param.12) | copy-start | bytes 24580
  12.7 460.4 %copy-start.5 = (f32[2,1024]{1,0:T(2,128)S(1)}, f32[2,1024]{1,0:T(2,128)}, u32[]{:S(2)}) copy-start(f32[2,1024]{1,0:T(2,128)} %param.13) | copy-start | bytes 24580
  12.7 460.4 %all-reduce.3.cloned.1.call-start = ((), (), s32[]{:S(2)}) async-start(), calls=%async_computation.2 | async-start | bytes 524288
Sparse Core Ops, SparseCore 0:
  12.8 134.4 reduce-scatter.1
  150.8 322.2 all-reduce.2
where the time goes:
time: 563 us
  waiting for transfers between devices  457 us (81%)
  blocking collectives  81.1 us (14%)
  between operations  14.7 us (3%)
    unnamed x3, waiting for transfers between devices  322 us
    reduce_scatter x1, waiting for transfers between devices, shards(): lax.psum_scatter(lax.dot_general(tokens, cotangent, (((0,), (0,)), ((), (...  135 us
    all_gather x1, blocking collectives, shards(): lax.all_gather(outer_next.astype(jnp.bfloat16), 'rep', axis=0, tiled=True)  81.1 us
  transfers between devices with their start and end apart: 2, of which 2 were waited for; matrix products, arithmetic and copies ran while one was open for 0% of the time, Pallas kernels for 0%

commit v1 on v0

v1 whole, which is shorter than its diff:
```python
import jax
import jax.numpy as jnp
from jax import lax
from jax.sharding import Mesh, PartitionSpec as P

INNER_STEP = 500
AXES = ("xh", "z", "xl", "y", "core")
SIZES = (4, 8, 2, 8, 2)
REP = ("xh", "z")
FSDP = ("xl", "y", "core")


def shards(acts, grad_out, inner_weight, first_moment, second_moment, outer_weight, outer_momentum):
    core = lax.axis_index("core")
    chips = lax.axis_size(("xl", "y"))
    replicas = lax.axis_size(REP)
    rows, cols = inner_weight.shape[1:]
    own = rows // replicas

    with jax.named_scope("grad_product"):
        partial = lax.dot_general(
            acts[0], grad_out[0], (((0,), (0,)), ((), ())), preferred_element_type=jnp.float32
        ).astype(jnp.bfloat16).reshape(chips, 2, rows, cols)
    with jax.named_scope("core_sum"):
        keep = lax.dynamic_index_in_dim(partial, core, 1, keepdims=False)
        give = lax.dynamic_index_in_dim(partial, 1 - core, 1, keepdims=False)
        got = lax.ppermute(give, "core", [(0, 1), (1, 0)])
        chip_sum = (keep.astype(jnp.float32) + got.astype(jnp.float32)).astype(jnp.bfloat16)
    with jax.named_scope("grad_exchange"):
        pieces = lax.all_to_all(chip_sum, ("xl", "y"), 0, 0, tiled=True)
        grad = jnp.sum(pieces.astype(jnp.float32), axis=0)

    with jax.named_scope("adamw"):
        first = 0.9 * first_moment[0] + 0.1 * grad
        second = 0.95 * second_moment[0] + 0.05 * grad * grad
        first_hat = first / (1.0 - 0.9**INNER_STEP)
        second_hat = second / (1.0 - 0.95**INNER_STEP)
        inner_new = inner_weight[0] * (1.0 - 0.0004 * 0.1) - 0.0004 * first_hat / (
            jnp.sqrt(second_hat) + 1e-08
        )
        inner_new = lax.optimization_barrier(inner_new)
    with jax.named_scope("replica_sum"):
        pieces = lax.all_to_all(inner_new.reshape(replicas, own, cols), REP, 0, 0, tiled=True)
        summed = jnp.sum(pieces, axis=0)
    with jax.named_scope("outer_step"):
        pseudo = outer_weight - summed / replicas
        momentum_next = 0.9 * outer_momentum + pseudo
        outer_next = outer_weight - 0.7 * (pseudo + 0.9 * momentum_next)
    with jax.named_scope("row_gather"):
        new = outer_next.astype(jnp.bfloat16).reshape(1, own * cols // 128, 128)
        copies = jnp.broadcast_to(new, (replicas,) + new.shape[1:])
        weight_next = lax.all_to_all(copies, REP, 0, 0, tiled=True).reshape(rows, cols)
    return (outer_next, momentum_next, weight_next)


def solution(mesh, sizes=SIZES):
    grid = Mesh(mesh.devices.reshape(sizes), AXES)
    split = P(REP, FSDP, None)
    outer = P(FSDP + REP, None)
    return jax.shard_map(
        shards,
        mesh=grid,
        in_specs=(split, split, split, split, split, outer, outer),
        out_specs=(outer, outer, P(FSDP, None)),
        check_vma=False,
    )
```

time: 563 us -> 130 us (0.23)
  waiting for transfers between devices: 457 us -> 4.34 us
  blocking collectives: 81.1 us -> 111 us
  between operations: 14.7 us -> 0.77 us
    unnamed x3 -> x0, waiting for transfers between devices: 322 us -> none
    reduce_scatter x1 -> x0, waiting for transfers between devices: 135 us -> none  [shards(): lax.psum_scatter(lax.dot_general(tokens, cotangent, (((0,), (0,)), ((), (...]
    all_to_all x0 -> x3, blocking collectives: none -> 111 us  [the longest x1 65.5 us: shards(): pieces = lax.all_to_all(chip_sum, ('xl', 'y'), 0, 0, tiled=True)]
    all_gather x1 -> x0, blocking collectives: 81.1 us -> none  [shards(): lax.all_gather(outer_next.astype(jnp.bfloat16), 'rep', axis=0, tiled=True)]
  transfers between devices with their start and end apart: 2 -> 1, of which waited for: 2 -> 1; matrix products, arithmetic and copies ran while one was open for 0% -> 0% of each run, Pallas kernels for 0% -> 0%
where the time goes in v1:
time: 130 us; the launch traced here: 129 us
  blocking collectives  111 us (85%)
  local copies, waits for them, and re-layouts  5.6 us (4%)
  waiting for transfers between devices  4.34 us (3%)
  other arithmetic  3.85 us (3%)
  matrix products  2.32 us (2%)
  starting transfers between devices  1.91 us (1%)
    all_to_all x1, blocking collectives, shards(): pieces = lax.all_to_all(chip_sum, ('xl', 'y'), 0, 0, tiled=True)  65.5 us
    all_to_all x1, blocking collectives, shards(): lax.all_to_all(inner_new.reshape(replicas, own, cols), REP, 0, 0, tiled=T...  27.2 us
    all_to_all x1, blocking collectives, shards(): lax.all_to_all(copies, REP, 0, 0, tiled=True).reshape(rows, cols)  17.9 us
    ppermute x1, waiting for transfers between devices, shards(): got = lax.ppermute(give, 'core', [(0, 1), (1, 0)])  4.34 us
    unnamed x14, local copies, waits for them, and re-layouts  3.19 us
  transfers between devices with their start and end apart: 1, of which 1 were waited for; matrix products, arithmetic and copies ran while one was open for 0% of the time, Pallas kernels for 0%

profile of v1, /device:TPU:16, one launch (start us, length us, event | category | flops | bytes accessed | tf_op | source)
XLA Modules:
  0.0 129.3 jit_solution(9906169317724766079)
XLA Ops:
  0.6 0.0 copy-start
  0.6 1.2 copy-done
  1.9 2.3 %convolution_convert_fusion = bf16[2048,1024]{1,0:T(8,128)(2,1)S(1)} fusion(bf16[1,256,2048]{2,1,0:T(8,128)(2,1)S(1)} %copy-done, bf16[1,256,1024]{2,1,0:T(8,128)(2,1)} %param.8), kind=kOutput, calls=%fused_computation.3 | convolution fusion | flops 1075838976 | bytes 5767168 | tf_op jit(solution)/shard_map/grad_product/dot_general | solution.py:21
  4.2 0.0 copy-start.1
  4.2 1.9 %copy-done.1 = bf16[2048,1024]{1,0:T(8,128)(2,1)} copy-done((bf16[2048,1024]{1,0:T(8,128)(2,1)}, bf16[2048,1024]{1,0:T(8,128)(2,1)S(1)}, u32[]{:S(2)}) %copy-start.1) | copy-done | bytes 4194328
  6.1 1.5 %dynamic-slice_bitcast_fusion = bf16[16,64,1024]{2,1,0:T(8,128)(2,1)} fusion(bf16[16,2,64,1024]{3,2,1,0:T(8,128)(2,1)S(1)} %bitcast.22, s32[]{:T(128)S(6)} %select_n.8), kind=kLoop, calls=%fused_computation.4 | loop fusion | bytes 4194308 | tf_op jit(solution)/shard_map/core_sum/jit(dynamic_index_in_dim)/squeeze | solution.py:26
  7.7 1.9 %collective-permute-start = (bf16[16,64,1024]{2,1,0:T(8,128)(2,1)}, bf16[16,64,1024]{2,1,0:T(8,128)(2,1)S(1)}, u32[]{:S(2)}, u32[]{:S(2)}) collective-permute-start(bf16[16,64,1024]{2,1,0:T(8,128)(2,1)} %dynamic-slice_bitcast_fusion), channel_id=1, source_target_pairs={{0,1},{1,0},{2,3},{3,2},{4,5},{5,4},{6,7},{7,6},{8,9},{9,8},{10,11... | collective-permute-start | bytes 6291464 | tf_op jit(solution)/shard_map/core_sum/ppermute | solution.py:27
  9.6 4.3 %collective-permute-done = bf16[16,64,1024]{2,1,0:T(8,128)(2,1)S(1)} collective-permute-done((bf16[16,64,1024]{2,1,0:T(8,128)(2,1)}, bf16[16,64,1024]{2,1,0:T(8,128)(2,1)S(1)}, u32[]{:S(2)}, u32[]{:S(2)}) %collective-permute-start) | collective-permute-done | bytes 2097184 | tf_op jit(solution)/shard_map/core_sum/ppermute | solution.py:27
  13.9 2.5 %fusion = bf16[16,64,1024]{2,1,0:T(8,128)(2,1)S(1)} fusion(bf16[16,64,1024]{2,1,0:T(8,128)(2,1)S(1)} %collective-permute-done, bf16[16,2,64,1024]{3,2,1,0:T(8,128)(2,1)} %bitcast.23, s32[]{:T(128)S(6)} %select_n.7), kind=kLoop, calls=%fused_computation.1 | loop fusion | flops 4194304 | bytes 6291460 | tf_op jit(solution)/shard_map/core_sum/convert_element_type | solution.py:28
  16.5 0.0 copy-start.2
  16.5 0.0 copy-start.3
  16.5 0.0 copy-start.4
  16.5 0.0 copy-start.5
  16.5 0.0 copy-start.6
  16.5 65.5 %all_to_all.15 = bf16[16,64,1024]{2,1,0:T(8,128)(2,1)S(1)} all-to-all(bf16[16,64,1024]{2,1,0:T(8,128)(2,1)S(1)} %fusion), channel_id=1, replica_groups=mesh['xh'=4,'z'=8,'xl'=2,'y'=8,'core'=2] {'xl','y'}, dimensions={0} | all-to-all | bytes 4194304 | tf_op jit(solution)/shard_map/grad_exchange/all_to_all | solution.py:30
  82.0 0.4 convert_reduce_fusion
  82.4 0.0 copy-done.2
  82.4 0.0 copy-done.3
  82.4 0.0 copy-done.4
  82.4 0.2 fusion.7
  82.6 0.1 reshape.26
  82.8 27.2 %all_to_all.16 = f32[32,2,1024]{2,1,0:T(2,128)S(1)} all-to-all(f32[32,2,1024]{2,1,0:T(2,128)S(1)} %reshape.26), channel_id=1, replica_groups=mesh['xh'=4,'z'=8,'xl'=2,'y'=8,'core'=2] {'xh','z'}, dimensions={0} | all-to-all | bytes 524288 | tf_op jit(solution)/shard_map/replica_sum/all_to_all | solution.py:43
  109.9 0.1 reduce_sum.19
  110.0 0.0 copy-done.5
  110.0 0.0 copy-done.6
  110.1 0.6 fusion.9
  110.7 17.9 %all_to_all.17 = bf16[32,16,128]{2,1,0:T(8,128)(2,1)S(1)} all-to-all(bf16[32,16,128]{2,1,0:T(8,128)(2,1)S(1)} %broadcast_in_dim.8), channel_id=1, replica_groups=mesh['xh'=4,'z'=8,'xl'=2,'y'=8,'core'=2] {'xh','z'}, dimensions={0} | all-to-all | bytes 262144 | tf_op jit(solution)/shard_map/row_gather/all_to_all | solution.py:52
  128.6 0.7 reshape.27
  (2 shorter events, 0.0 us)
Async XLA Ops:
  0.6 1.2 copy-start
  4.2 1.9 %copy-start.1 = (bf16[2048,1024]{1,0:T(8,128)(2,1)}, bf16[2048,1024]{1,0:T(8,128)(2,1)S(1)}, u32[]{:S(2)}) copy-start(bf16[2048,1024]{1,0:T(8,128)(2,1)S(1)} %convolution_convert_fusion) | copy-start | bytes 12582916
  7.7 6.3 %collective-permute-start = (bf16[16,64,1024]{2,1,0:T(8,128)(2,1)}, bf16[16,64,1024]{2,1,0:T(8,128)(2,1)S(1)}, u32[]{:S(2)}, u32[]{:S(2)}) collective-permute-start(bf16[16,64,1024]{2,1,0:T(8,128)(2,1)} %dynamic-slice_bitcast_fusion), channel_id=1, source_target_pairs={{0,1},{1,0},{2,3},{3,2},{4,5},{5,4},{6,7},{7,6},{8,9},{9,8},{10,11... | collective-permute-start | bytes 6291464 | tf_op jit(solution)/shard_map/core_sum/ppermute | solution.py:27
  16.5 65.9 %copy-start.2 = (f32[1,64,1024]{2,1,0:T(8,128)S(1)}, f32[1,64,1024]{2,1,0:T(8,128)}, u32[]{:S(2)}) copy-start(f32[1,64,1024]{2,1,0:T(8,128)} %param.11) | copy-start | bytes 786436
  16.5 65.9 %copy-start.3 = (f32[1,64,1024]{2,1,0:T(8,128)S(1)}, f32[1,64,1024]{2,1,0:T(8,128)}, u32[]{:S(2)}) copy-start(f32[1,64,1024]{2,1,0:T(8,128)} %param.10) | copy-start | bytes 786436
  16.5 65.9 %copy-start.4 = (f32[1,64,1024]{2,1,0:T(8,128)S(1)}, f32[1,64,1024]{2,1,0:T(8,128)}, u32[]{:S(2)}) copy-start(f32[1,64,1024]{2,1,0:T(8,128)} %param.9) | copy-start | bytes 786436
  16.5 93.5 %copy-start.5 = (f32[2,1024]{1,0:T(2,128)S(1)}, f32[2,1024]{1,0:T(2,128)}, u32[]{:S(2)}) copy-start(f32[2,1024]{1,0:T(2,128)} %param.12) | copy-start | bytes 24580
  16.5 93.5 %copy-start.6 = (f32[2,1024]{1,0:T(2,128)S(1)}, f32[2,1024]{1,0:T(2,128)}, u32[]{:S(2)}) copy-start(f32[2,1024]{1,0:T(2,128)} %param.13) | copy-start | bytes 24580

commit v2 on v1

v2 whole, which is shorter than its diff:
```python
import jax
import jax.numpy as jnp
from jax import lax
from jax.experimental import pallas as pl
from jax.experimental.pallas import tpu as pltpu
from jax.sharding import Mesh, PartitionSpec as P

INNER_STEP = 500
AXES = ("xh", "z", "xl", "y", "core")
SIZES = (4, 8, 2, 8, 2)
REP = ("xh", "z")
FSDP = ("xl", "y", "core")
RING = 8


def product_kernel(offsets, place, acts, cot, acts_peer, cot_peer, *outs):
    xl, y, core = place[0], place[1], place[2]
    lane = lax.broadcasted_iota(jnp.int32, (1, 128), 1)
    own_side = (lane < 64) == (core == 0)

    def columns(ref, target):
        def block(side):
            start = pl.multiple_of((side * RING + target) * 128, 128)
            return ref[:, pl.ds(start, 128)].astype(jnp.float32)

        near, far = block(xl), block(1 - xl)
        still = jnp.where(core == 0, near, far)
        moved = pltpu.roll(jnp.where(core == 0, far, near), 64, 1)
        return jnp.where(own_side, still, moved).astype(jnp.bfloat16)

    def times(lhs, rhs):
        return lax.dot_general(lhs, rhs, (((0,), (0,)), ((), ())), preferred_element_type=jnp.float32)

    for offset, out in zip(offsets, outs):
        target = lax.rem(y + offset, RING)
        total = times(columns(acts, target), cot[...]) + times(columns(acts_peer, target), cot_peer[...])
        out[...] = total.astype(out.dtype)


def product(offsets, place, acts, cot, acts_peer, cot_peer):
    vmem = pl.BlockSpec(memory_space=pltpu.VMEM)
    cols = cot.shape[1]
    tokens = acts.shape[0]
    return pl.pallas_call(
        lambda *refs: product_kernel(offsets, *refs),
        out_shape=[jax.ShapeDtypeStruct((128, cols), jnp.bfloat16) for _ in offsets],
        in_specs=[pl.BlockSpec(memory_space=pltpu.SMEM)] + [vmem] * 4,
        out_specs=[vmem for _ in offsets],
        compiler_params=pltpu.CompilerParams(vmem_limit_bytes=24 * 1024 * 1024),
        cost_estimate=pl.CostEstimate(
            flops=2 * 128 * len(offsets) * 2 * tokens * cols,
            bytes_accessed=4 * tokens * (2048 + cols),
            transcendentals=0,
        ),
    )(place, acts, cot, acts_peer, cot_peer)


def add(*terms):
    return sum(t.astype(jnp.float32) for t in terms)


def shards(acts, grad_out, inner_weight, first_moment, second_moment, outer_weight, outer_momentum):
    replicas = lax.axis_size(REP)
    rows, cols = inner_weight.shape[1:]
    own = rows // replicas
    bf16 = jnp.bfloat16
    place = jnp.stack([lax.axis_index(a) for a in FSDP])

    with jax.named_scope("core_swap"):
        swap = [(0, 1), (1, 0)]
        acts_peer = lax.ppermute(acts[0], "core", swap)
        cot_peer = lax.ppermute(grad_out[0], "core", swap)
    with jax.named_scope("grad_product"):
        four, three, five = product((4, 3, 5), place, acts[0], grad_out[0], acts_peer, cot_peer)
        two, six, one, seven, zero = product((2, 6, 1, 7, 0), place, acts[0], grad_out[0], acts_peer, cot_peer)
    with jax.named_scope("grad_ring"):
        ring = [(i, (i + 1) % RING) for i in range(RING)]
        back = [(j, i) for i, j in ring]
        up = lax.ppermute(four[:rows], "y", ring)
        down = lax.ppermute(four[rows:], "y", back)
        up = jnp.concatenate([add(three[:rows], up).astype(bf16), three[rows:]])
        down = jnp.concatenate([five[:rows], add(five[rows:], down).astype(bf16)])
        for ahead, behind in ((two, six), (one, seven)):
            up = add(ahead, lax.ppermute(up, "y", ring)).astype(bf16)
            down = add(behind, lax.ppermute(down, "y", back)).astype(bf16)
        up = lax.ppermute(up, "y", ring)
        down = lax.ppermute(down, "y", back)
    with jax.named_scope("grad_pair"):
        other = add(zero[rows:], up[rows:], down[rows:]).astype(bf16)
        other = lax.ppermute(other, "xl", [(0, 1), (1, 0)])
        grad = add(zero[:rows], up[:rows], down[:rows], other)

    with jax.named_scope("adamw"):
        first = 0.9 * first_moment[0] + 0.1 * grad
        second = 0.95 * second_moment[0] + 0.05 * grad * grad
        first_hat = first / (1.0 - 0.9**INNER_STEP)
        second_hat = second / (1.0 - 0.95**INNER_STEP)
        inner_new = inner_weight[0] * (1.0 - 0.0004 * 0.1) - 0.0004 * first_hat / (
            jnp.sqrt(second_hat) + 1e-08
        )
        inner_new = lax.optimization_barrier(inner_new)
    with jax.named_scope("replica_sum"):
        pieces = lax.all_to_all(inner_new.reshape(replicas, own, cols), REP, 0, 0, tiled=True)
        summed = jnp.sum(pieces, axis=0)
    with jax.named_scope("outer_step"):
        pseudo = outer_weight - summed / replicas
        momentum_next = 0.9 * outer_momentum + pseudo
        outer_next = outer_weight - 0.7 * (pseudo + 0.9 * momentum_next)
    with jax.named_scope("row_gather"):
        new = outer_next.astype(bf16).reshape(1, own * cols // 128, 128)
        copies = jnp.broadcast_to(new, (replicas,) + new.shape[1:])
        weight_next = lax.all_to_all(copies, REP, 0, 0, tiled=True).reshape(rows, cols)
    return (outer_next, momentum_next, weight_next)


def solution(mesh, sizes=SIZES):
    grid = Mesh(mesh.devices.reshape(sizes), AXES)
    split = P(REP, FSDP, None)
    outer = P(FSDP + REP, None)
    return jax.shard_map(
        shards,
        mesh=grid,
        in_specs=(split, split, split, split, split, outer, outer),
        out_specs=(outer, outer, P(FSDP, None)),
        check_vma=False,
    )
```

time: 130 us -> 117 us (0.900)
  the two profiles are of different devices: /device:TPU:16 before, /device:TPU:48 now
where the time goes in v2:
time: 117 us; the launch traced here: 116 us
  blocking collectives  48.3 us (41%)
  starting transfers between devices  39.6 us (34%)
  waiting for transfers between devices  18.2 us (16%)
  local copies, waits for them, and re-layouts  3.83 us (3%)
  Pallas kernels  3.67 us (3%)
  other arithmetic  1.47 us (1%)
    all_to_all x1, blocking collectives, shards(): lax.all_to_all(inner_new.reshape(replicas, own, cols), REP, 0, 0, tiled=T...  31.6 us
    all_to_all x1, blocking collectives, shards(): lax.all_to_all(copies, REP, 0, 0, tiled=True).reshape(rows, cols)  16.7 us
    ppermute x2, starting transfers between devices, shards(): up = add(ahead, lax.ppermute(up, 'y', ring)).astype(bf16)  11.2 us
    ppermute x2, starting transfers between devices, shards(): down = add(behind, lax.ppermute(down, 'y', back)).astype(bf16)  8.98 us
    ppermute x1, waiting for transfers between devices, shards(): other = lax.ppermute(other, 'xl', [(0, 1), (1, 0)])  4.93 us
    ppermute x1, starting transfers between devices, shards(): up = lax.ppermute(four[:rows], 'y', ring)  4.84 us
    ppermute x2, waiting for transfers between devices, shards(): up = add(ahead, lax.ppermute(up, 'y', ring)).astype(bf16)  4.79 us
    ppermute x1, starting transfers between devices, shards(): down = lax.ppermute(down, 'y', back)  4.35 us
  transfers between devices with their start and end apart: 11, of which 7 were waited for; matrix products, arithmetic and copies ran while one was open for 0% of the time, Pallas kernels for 2%

profile of v2, /device:TPU:48, one launch (start us, length us, event | category | flops | bytes accessed | tf_op | source)
XLA Modules:
  0.0 115.9 jit_solution(12060989769943863275)
XLA Ops:
  0.6 1.9 %collective-permute-start = (bf16[256,2048]{1,0:T(8,128)(2,1)}, bf16[256,2048]{1,0:T(8,128)(2,1)S(1)}, u32[]{:S(2)}, u32[]{:S(2)}) collective-permute-start(bf16[256,2048]{1,0:T(8,128)(2,1)} %bitcast.15), channel_id=1, source_target_pairs={{0,1},{1,0},{2,3},{3,2},{4,5},{5,4},{6,7},{7,6},{8,9},{9,8},{10,11... | collective-permute-start | bytes 3145736 | tf_op jit(solution)/shard_map/core_swap/ppermute | solution.py:71
  2.6 2.4 %collective-permute-start.1 = (bf16[256,1024]{1,0:T(8,128)(2,1)}, bf16[256,1024]{1,0:T(8,128)(2,1)S(1)}, u32[]{:S(2)}, u32[]{:S(2)}) collective-permute-start(bf16[256,1024]{1,0:T(8,128)(2,1)} %bitcast.18), channel_id=1, source_target_pairs={{0,1},{1,0},{2,3},{3,2},{4,5},{5,4},{6,7},{7,6},{8,9},{9,8},{10,11... | collective-permute-start | bytes 1572872 | tf_op jit(solution)/shard_map/core_swap/ppermute | solution.py:72
  5.0 0.1 pad_add_fusion.refs_0_
  5.1 1.6 %collective-permute-done.1.refs_4_ = bf16[256,1024]{1,0:T(8,128)(2,1)S(1)} collective-permute-done((bf16[256,1024]{1,0:T(8,128)(2,1)}, bf16[256,1024]{1,0:T(8,128)(2,1)S(1)}, u32[]{:S(2)}, u32[]{:S(2)}) %collective-permute-start.1) | collective-permute-done | bytes 524320 | tf_op jit(solution)/shard_map/core_swap/ppermute | solution.py:72
  6.7 1.2 %copy-done = bf16[1,256,2048]{2,1,0:T(8,128)(2,1)S(1)} copy-done((bf16[1,256,2048]{2,1,0:T(8,128)(2,1)S(1)}, bf16[1,256,2048]{2,1,0:T(8,128)(2,1)}, u32[]{:S(2)}) %copy-start) | copy-done | bytes 1048600
  7.9 1.0 copy-done.1
  9.0 1.5 %grad_product.3 = (bf16[128,1024]{1,0:T(8,128)(2,1)S(1)}, bf16[128,1024]{1,0:T(8,128)(2,1)S(1)}, bf16[128,1024]{1,0:T(8,128)(2,1)S(1)}) custom-call(s32[3]{0:T(128)S(1)} %pad_add_fusion.refs_0_, bf16[256,2048]{1,0:T(8,128)(2,1)S(1)} %bitcast.16, bf16[256,1024]{1,0:T(8,128)(2,1)S(1)} %bitcast.19, bf16[256,2048]{1,0:T(8,128)(2,1)S(1)} %collective-permute-done.refs_3_, ...), custom_call_target="tpu_custom_call" | custom-call | flops 402653184 | bytes 3145728 | tf_op jit(solution)/shard_map/grad_product/pallas_call | solution.py:44
  10.6 4.8 %collective-permute-start.2 = (bf16[64,1024]{1,0:T(8,128)(2,1)S(1)}, bf16[64,1024]{1,0:T(8,128)(2,1)S(1)}, u32[]{:S(2)}, u32[]{:S(2)}) collective-permute-start(bf16[64,1024]{1,0:T(8,128)(2,1)S(1)} %get-tuple-element.22), channel_id=1, source_target_pairs={{0,2},{2,4},{4,6},{6,8},{8,10},{10,12},{12,14},{14,0},{1,3},{3,5},... | collective-permute-start | bytes 393224 | tf_op jit(solution)/shard_map/grad_ring/ppermute | solution.py:79
  15.4 1.9 %collective-permute-start.6 = (bf16[64,1024]{1,0:T(8,128)(2,1)S(1)}, bf16[64,1024]{1,0:T(8,128)(2,1)S(1)}, u32[]{:S(2)}, u32[]{:S(2)}) collective-permute-start(bf16[64,1024]{1,0:T(8,128)(2,1)S(1)} %get-tuple-element.23), channel_id=1, source_target_pairs={{2,0},{4,2},{6,4},{8,6},{10,8},{12,10},{14,12},{0,14},{3,1},{5,3},... | collective-permute-start | bytes 393224 | tf_op jit(solution)/shard_map/grad_ring/ppermute | solution.py:80
  17.4 1.3 %collective-permute-done.2 = bf16[64,1024]{1,0:T(8,128)(2,1)S(1)} collective-permute-done((bf16[64,1024]{1,0:T(8,128)(2,1)S(1)}, bf16[64,1024]{1,0:T(8,128)(2,1)S(1)}, u32[]{:S(2)}, u32[]{:S(2)}) %collective-permute-start.2) | collective-permute-done | bytes 131104 | tf_op jit(solution)/shard_map/grad_ring/ppermute | solution.py:79
  18.7 5.6 %collective-permute-start.3 = (bf16[128,1024]{1,0:T(8,128)(2,1)S(1)}, bf16[128,1024]{1,0:T(8,128)(2,1)S(1)}, u32[]{:S(2)}, u32[]{:S(2)}) collective-permute-start(bf16[128,1024]{1,0:T(8,128)(2,1)S(1)} %pad_maximum_fusion), channel_id=1, source_target_pairs={{0,2},{2,4},{4,6},{6,8},{8,10},{10,12},{12,14},{14,0},{1,3},{3,5},... | collective-permute-start | bytes 786440 | tf_op jit(solution)/shard_map/grad_ring/ppermute | solution.py:84
  24.4 1.9 %collective-permute-start.7 = (bf16[128,1024]{1,0:T(8,128)(2,1)S(1)}, bf16[128,1024]{1,0:T(8,128)(2,1)S(1)}, u32[]{:S(2)}, u32[]{:S(2)}) collective-permute-start(bf16[128,1024]{1,0:T(8,128)(2,1)S(1)} %pad_maximum_fusion.1), channel_id=1, source_target_pairs={{2,0},{4,2},{6,4},{8,6},{10,8},{12,10},{14,12},{0,14},{3,1},{5,3},... | collective-permute-start | bytes 786440 | tf_op jit(solution)/shard_map/grad_ring/ppermute | solution.py:85
  26.3 2.1 %grad_product.2 = (bf16[128,1024]{1,0:T(8,128)(2,1)S(1)}, bf16[128,1024]{1,0:T(8,128)(2,1)S(1)}, bf16[128,1024]{1,0:T(8,128)(2,1)S(1)}, bf16[128,1024]{1,0:T(8,128)(2,1)S(1)}, bf16[128,1024]{1,0:T(8,128)(2,1)S(1)}) custom-call(s32[3]{0:T(128)S(1)} %pad_add_fusion.refs_0_, bf16[256,2048]{1,0:T(8,128)(2,1)S(1)} %bitcast.17, bf16[256,1024]{1,0:T(8,128)(2,1)S(1)} %bitcast.20, ...), custom_call_target="tpu_custom_call" | custom-call | flops 671088640 | bytes 3145728 | tf_op jit(solution)/shard_map/grad_product/pallas_call | solution.py:44
  28.5 1.1 collective-permute-done.3
  29.6 0.1 add_convert_fusion.3
  29.6 5.6 %collective-permute-start.4 = (bf16[128,1024]{1,0:T(8,128)(2,1)S(1)}, bf16[128,1024]{1,0:T(8,128)(2,1)S(1)}, u32[]{:S(2)}, u32[]{:S(2)}) collective-permute-start(bf16[128,1024]{1,0:T(8,128)(2,1)S(1)} %add_convert_fusion.3), channel_id=1, source_target_pairs={{0,2},{2,4},{4,6},{6,8},{8,10},{10,12},{12,14},{14,0},{1,3},{3,5},... | collective-permute-start | bytes 786440 | tf_op jit(solution)/shard_map/grad_ring/ppermute | solution.py:84
  35.3 7.1 %collective-permute-start.8 = (bf16[128,1024]{1,0:T(8,128)(2,1)S(1)}, bf16[128,1024]{1,0:T(8,128)(2,1)S(1)}, u32[]{:S(2)}, u32[]{:S(2)}) collective-permute-start(bf16[128,1024]{1,0:T(8,128)(2,1)S(1)} %add_convert_fusion.1), channel_id=1, source_target_pairs={{2,0},{4,2},{6,4},{8,6},{10,8},{12,10},{14,12},{0,14},{3,1},{5,3},... | collective-permute-start | bytes 786440 | tf_op jit(solution)/shard_map/grad_ring/ppermute | solution.py:85
  42.4 3.7 %collective-permute-done.4 = bf16[128,1024]{1,0:T(8,128)(2,1)S(1)} collective-permute-done((bf16[128,1024]{1,0:T(8,128)(2,1)S(1)}, bf16[128,1024]{1,0:T(8,128)(2,1)S(1)}, u32[]{:S(2)}, u32[]{:S(2)}) %collective-permute-start.4) | collective-permute-done | bytes 262176 | tf_op jit(solution)/shard_map/grad_ring/ppermute | solution.py:84
  46.1 1.9 %collective-permute-start.5 = (bf16[128,1024]{1,0:T(8,128)(2,1)S(1)}, bf16[128,1024]{1,0:T(8,128)(2,1)S(1)}, u32[]{:S(2)}, u32[]{:S(2)}) collective-permute-start(bf16[128,1024]{1,0:T(8,128)(2,1)S(1)} %add_convert_fusion.2), channel_id=1, source_target_pairs={{0,2},{2,4},{4,6},{6,8},{8,10},{10,12},{12,14},{14,0},{1,3},{3,5},... | collective-permute-start | bytes 786440 | tf_op jit(solution)/shard_map/grad_ring/ppermute | solution.py:86
  48.2 4.3 %collective-permute-start.9 = (bf16[128,1024]{1,0:T(8,128)(2,1)S(1)}, bf16[128,1024]{1,0:T(8,128)(2,1)S(1)}, u32[]{:S(2)}, u32[]{:S(2)}) collective-permute-start(bf16[128,1024]{1,0:T(8,128)(2,1)S(1)} %add_convert_fusion), channel_id=1, source_target_pairs={{2,0},{4,2},{6,4},{8,6},{10,8},{12,10},{14,12},{0,14},{3,1},{5,3},... | collective-permute-start | bytes 786440 | tf_op jit(solution)/shard_map/grad_ring/ppermute | solution.py:87
  52.5 2.8 %collective-permute-done.5 = bf16[128,1024]{1,0:T(8,128)(2,1)S(1)} collective-permute-done((bf16[128,1024]{1,0:T(8,128)(2,1)S(1)}, bf16[128,1024]{1,0:T(8,128)(2,1)S(1)}, u32[]{:S(2)}, u32[]{:S(2)}) %collective-permute-start.5) | collective-permute-done | bytes 262176 | tf_op jit(solution)/shard_map/grad_ring/ppermute | solution.py:86
  55.3 2.8 %collective-permute-done.9 = bf16[128,1024]{1,0:T(8,128)(2,1)S(1)} collective-permute-done((bf16[128,1024]{1,0:T(8,128)(2,1)S(1)}, bf16[128,1024]{1,0:T(8,128)(2,1)S(1)}, u32[]{:S(2)}, u32[]{:S(2)}) %collective-permute-start.9) | collective-permute-done | bytes 262176 | tf_op jit(solution)/shard_map/grad_ring/ppermute | solution.py:87
  58.2 2.1 %collective-permute-start.10 = (bf16[64,1024]{1,0:T(8,128)(2,1)S(1)}, bf16[64,1024]{1,0:T(8,128)(2,1)S(1)}, u32[]{:S(2)}, u32[]{:S(2)}) collective-permute-start(bf16[64,1024]{1,0:T(8,128)(2,1)S(1)} %add_convert_fusion.4), channel_id=1, source_target_pairs={{0,16},{16,0},{1,17},{17,1},{2,18},{18,2},{3,19},{19,3},{4,20},{20... | collective-permute-start | bytes 393224 | tf_op jit(solution)/shard_map/grad_pair/ppermute | solution.py:90
  60.2 4.9 %collective-permute-done.10 = bf16[64,1024]{1,0:T(8,128)(2,1)S(1)} collective-permute-done((bf16[64,1024]{1,0:T(8,128)(2,1)S(1)}, bf16[64,1024]{1,0:T(8,128)(2,1)S(1)}, u32[]{:S(2)}, u32[]{:S(2)}) %collective-permute-start.10) | collective-permute-done | bytes 131104 | tf_op jit(solution)/shard_map/grad_pair/ppermute | solution.py:90
  65.2 0.2 fusion.4
  65.4 0.1 reshape.20
  65.6 31.6 %all_to_all.10 = f32[32,2,1024]{2,1,0:T(2,128)S(1)} all-to-all(f32[32,2,1024]{2,1,0:T(2,128)S(1)} %reshape.20), channel_id=1, replica_groups=mesh['xh'=4,'z'=8,'xl'=2,'y'=8,'core'=2] {'xh','z'}, dimensions={0} | all-to-all | bytes 524288 | tf_op jit(solution)/shard_map/replica_sum/all_to_all | solution.py:103
  97.2 0.1 reduce_sum.9
  97.3 0.6 copy-done.5
  97.9 0.6 fusion.6
  98.5 16.7 %all_to_all.11 = bf16[32,16,128]{2,1,0:T(8,128)(2,1)S(1)} all-to-all(bf16[32,16,128]{2,1,0:T(8,128)(2,1)S(1)} %broadcast_in_dim.8), channel_id=1, replica_groups=mesh['xh'=4,'z'=8,'xl'=2,'y'=8,'core'=2] {'xh','z'}, dimensions={0} | all-to-all | bytes 262144 | tf_op jit(solution)/shard_map/row_gather/all_to_all | solution.py:112
  115.2 0.7 reshape.21
  (28 shorter events, 0.5 us)
Async XLA Ops:
  0.6 6.1 %collective-permute-start = (bf16[256,2048]{1,0:T(8,128)(2,1)}, bf16[256,2048]{1,0:T(8,128)(2,1)S(1)}, u32[]{:S(2)}, u32[]{:S(2)}) collective-permute-start(bf16[256,2048]{1,0:T(8,128)(2,1)} %bitcast.15), channel_id=1, source_target_pairs={{0,1},{1,0},{2,3},{3,2},{4,5},{5,4},{6,7},{7,6},{8,9},{9,8},{10,11... | collective-permute-start | bytes 3145736 | tf_op jit(solution)/shard_map/core_swap/ppermute | solution.py:71
  2.6 4.1 %collective-permute-start.1 = (bf16[256,1024]{1,0:T(8,128)(2,1)}, bf16[256,1024]{1,0:T(8,128)(2,1)S(1)}, u32[]{:S(2)}, u32[]{:S(2)}) collective-permute-start(bf16[256,1024]{1,0:T(8,128)(2,1)} %bitcast.18), channel_id=1, source_target_pairs={{0,1},{1,0},{2,3},{3,2},{4,5},{5,4},{6,7},{7,6},{8,9},{9,8},{10,11... | collective-permute-start | bytes 1572872 | tf_op jit(solution)/shard_map/core_swap/ppermute | solution.py:72
  6.7 1.2 %copy-start = (bf16[1,256,2048]{2,1,0:T(8,128)(2,1)S(1)}, bf16[1,256,2048]{2,1,0:T(8,128)(2,1)}, u32[]{:S(2)}) copy-start(bf16[1,256,2048]{2,1,0:T(8,128)(2,1)} %param.7) | copy-start | bytes 3145732
  7.9 1.0 copy-start.1
  10.6 8.1 %collective-permute-start.2 = (bf16[64,1024]{1,0:T(8,128)(2,1)S(1)}, bf16[64,1024]{1,0:T(8,128)(2,1)S(1)}, u32[]{:S(2)}, u32[]{:S(2)}) collective-permute-start(bf16[64,1024]{1,0:T(8,128)(2,1)S(1)} %get-tuple-element.22), channel_id=1, source_target_pairs={{0,2},{2,4},{4,6},{6,8},{8,10},{10,12},{12,14},{14,0},{1,3},{3,5},... | collective-permute-start | bytes 393224 | tf_op jit(solution)/shard_map/grad_ring/ppermute | solution.py:79
  15.4 8.9 %collective-permute-start.6 = (bf16[64,1024]{1,0:T(8,128)(2,1)S(1)}, bf16[64,1024]{1,0:T(8,128)(2,1)S(1)}, u32[]{:S(2)}, u32[]{:S(2)}) collective-permute-start(bf16[64,1024]{1,0:T(8,128)(2,1)S(1)} %get-tuple-element.23), channel_id=1, source_target_pairs={{2,0},{4,2},{6,4},{8,6},{10,8},{12,10},{14,12},{0,14},{3,1},{5,3},... | collective-permute-start | bytes 393224 | tf_op jit(solution)/shard_map/grad_ring/ppermute | solution.py:80
  18.7 10.9 %collective-permute-start.3 = (bf16[128,1024]{1,0:T(8,128)(2,1)S(1)}, bf16[128,1024]{1,0:T(8,128)(2,1)S(1)}, u32[]{:S(2)}, u32[]{:S(2)}) collective-permute-start(bf16[128,1024]{1,0:T(8,128)(2,1)S(1)} %pad_maximum_fusion), channel_id=1, source_target_pairs={{0,2},{2,4},{4,6},{6,8},{8,10},{10,12},{12,14},{14,0},{1,3},{3,5},... | collective-permute-start | bytes 786440 | tf_op jit(solution)/shard_map/grad_ring/ppermute | solution.py:84
  24.4 10.8 %collective-permute-start.7 = (bf16[128,1024]{1,0:T(8,128)(2,1)S(1)}, bf16[128,1024]{1,0:T(8,128)(2,1)S(1)}, u32[]{:S(2)}, u32[]{:S(2)}) collective-permute-start(bf16[128,1024]{1,0:T(8,128)(2,1)S(1)} %pad_maximum_fusion.1), channel_id=1, source_target_pairs={{2,0},{4,2},{6,4},{8,6},{10,8},{12,10},{14,12},{0,14},{3,1},{5,3},... | collective-permute-start | bytes 786440 | tf_op jit(solution)/shard_map/grad_ring/ppermute | solution.py:85
  29.6 16.4 %collective-permute-start.4 = (bf16[128,1024]{1,0:T(8,128)(2,1)S(1)}, bf16[128,1024]{1,0:T(8,128)(2,1)S(1)}, u32[]{:S(2)}, u32[]{:S(2)}) collective-permute-start(bf16[128,1024]{1,0:T(8,128)(2,1)S(1)} %add_convert_fusion.3), channel_id=1, source_target_pairs={{0,2},{2,4},{4,6},{6,8},{8,10},{10,12},{12,14},{14,0},{1,3},{3,5},... | collective-permute-start | bytes 786440 | tf_op jit(solution)/shard_map/grad_ring/ppermute | solution.py:84
  35.3 12.7 %collective-permute-start.8 = (bf16[128,1024]{1,0:T(8,128)(2,1)S(1)}, bf16[128,1024]{1,0:T(8,128)(2,1)S(1)}, u32[]{:S(2)}, u32[]{:S(2)}) collective-permute-start(bf16[128,1024]{1,0:T(8,128)(2,1)S(1)} %add_convert_fusion.1), channel_id=1, source_target_pairs={{2,0},{4,2},{6,4},{8,6},{10,8},{12,10},{14,12},{0,14},{3,1},{5,3},... | collective-permute-start | bytes 786440 | tf_op jit(solution)/shard_map/grad_ring/ppermute | solution.py:85
  46.1 9.1 %collective-permute-start.5 = (bf16[128,1024]{1,0:T(8,128)(2,1)S(1)}, bf16[128,1024]{1,0:T(8,128)(2,1)S(1)}, u32[]{:S(2)}, u32[]{:S(2)}) collective-permute-start(bf16[128,1024]{1,0:T(8,128)(2,1)S(1)} %add_convert_fusion.2), channel_id=1, source_target_pairs={{0,2},{2,4},{4,6},{6,8},{8,10},{10,12},{12,14},{14,0},{1,3},{3,5},... | collective-permute-start | bytes 786440 | tf_op jit(solution)/shard_map/grad_ring/ppermute | solution.py:86
  48.1 17.1 %copy-start.4 = (f32[1,64,1024]{2,1,0:T(8,128)S(1)}, f32[1,64,1024]{2,1,0:T(8,128)}, u32[]{:S(2)}) copy-start(f32[1,64,1024]{2,1,0:T(8,128)} %param.9) | copy-start | bytes 786436
  48.2 9.9 %collective-permute-start.9 = (bf16[128,1024]{1,0:T(8,128)(2,1)S(1)}, bf16[128,1024]{1,0:T(8,128)(2,1)S(1)}, u32[]{:S(2)}, u32[]{:S(2)}) collective-permute-start(bf16[128,1024]{1,0:T(8,128)(2,1)S(1)} %add_convert_fusion), channel_id=1, source_target_pairs={{2,0},{4,2},{6,4},{8,6},{10,8},{12,10},{14,12},{0,14},{3,1},{5,3},... | collective-permute-start | bytes 786440 | tf_op jit(solution)/shard_map/grad_ring/ppermute | solution.py:87
  58.1 7.1 %copy-start.2 = (f32[1,64,1024]{2,1,0:T(8,128)S(1)}, f32[1,64,1024]{2,1,0:T(8,128)}, u32[]{:S(2)}) copy-start(f32[1,64,1024]{2,1,0:T(8,128)} %param.11) | copy-start | bytes 786436
  58.1 7.1 %copy-start.3 = (f32[1,64,1024]{2,1,0:T(8,128)S(1)}, f32[1,64,1024]{2,1,0:T(8,128)}, u32[]{:S(2)}) copy-start(f32[1,64,1024]{2,1,0:T(8,128)} %param.10) | copy-start | bytes 786436
  58.2 7.0 %collective-permute-start.10 = (bf16[64,1024]{1,0:T(8,128)(2,1)S(1)}, bf16[64,1024]{1,0:T(8,128)(2,1)S(1)}, u32[]{:S(2)}, u32[]{:S(2)}) collective-permute-start(bf16[64,1024]{1,0:T(8,128)(2,1)S(1)} %add_convert_fusion.4), channel_id=1, source_target_pairs={{0,16},{16,0},{1,17},{17,1},{2,18},{18,2},{3,19},{19,3},{4,20},{20... | collective-permute-start | bytes 393224 | tf_op jit(solution)/shard_map/grad_pair/ppermute | solution.py:90
  97.2 0.7 copy-start.5
  97.2 0.7 copy-start.6

commit v3 on v2

v3 whole, which is shorter than its diff:
```python
import jax
import jax.numpy as jnp
from jax import lax
from jax.experimental import pallas as pl
from jax.experimental.pallas import tpu as pltpu
from jax.sharding import Mesh, PartitionSpec as P

INNER_STEP = 500
AXES = ("xh", "z", "xl", "y", "core")
SIZES = (4, 8, 2, 8, 2)
REP = ("xh", "z")
FSDP = ("xl", "y", "core")
RING = 8
OUTER_GAIN = 0.7 * 1.9


def product_kernel(offsets, place, acts, cot, *refs):
    xl, y, core = place[0], place[1], place[2]
    before, outs = refs[: -len(offsets)], refs[-len(offsets) :]
    lane = lax.broadcasted_iota(jnp.int32, (1, 128), 1)
    own_side = (lane < 64) == (core == 0)

    def columns(target):
        def block(side):
            start = pl.multiple_of((side * RING + target) * 128, 128)
            return acts[:, pl.ds(start, 128)].astype(jnp.float32)

        near, far = block(xl), block(1 - xl)
        still = jnp.where(core == 0, near, far)
        moved = pltpu.roll(jnp.where(core == 0, far, near), 64, 1)
        return jnp.where(own_side, still, moved).astype(jnp.bfloat16)

    for i, offset in enumerate(offsets):
        target = lax.rem(y + jnp.where(core == 0, offset, RING - offset), RING)
        total = lax.dot_general(
            columns(target), cot[...], (((0,), (0,)), ((), ())), preferred_element_type=jnp.float32
        )
        if before:
            total = total + before[i][...]
        outs[i][...] = total.astype(outs[i].dtype)


def product(offsets, dtype, place, acts, cot, *before):
    vmem = pl.BlockSpec(memory_space=pltpu.VMEM)
    tokens, cols = cot.shape
    return pl.pallas_call(
        lambda *refs: product_kernel(offsets, *refs),
        out_shape=[jax.ShapeDtypeStruct((128, cols), dtype) for _ in offsets],
        in_specs=[pl.BlockSpec(memory_space=pltpu.SMEM)] + [vmem] * (2 + len(before)),
        out_specs=[vmem for _ in offsets],
        compiler_params=pltpu.CompilerParams(vmem_limit_bytes=24 * 1024 * 1024),
        cost_estimate=pl.CostEstimate(
            flops=2 * 128 * len(offsets) * tokens * cols,
            bytes_accessed=2 * tokens * (acts.shape[1] + cols),
            transcendentals=0,
        ),
    )(place, acts, cot, *before)


def add(*terms):
    return sum(t.astype(jnp.float32) for t in terms)


def shards(acts, grad_out, inner_weight, first_moment, second_moment, outer_weight, outer_momentum):
    replicas = lax.axis_size(REP)
    high, deep = lax.axis_size("xh"), lax.axis_size("z")
    rows, cols = inner_weight.shape[1:]
    own = rows // replicas
    bf16 = jnp.bfloat16
    place = jnp.stack([lax.axis_index(a) for a in FSDP])

    with jax.named_scope("core_swap"):
        swap = [(0, 1), (1, 0)]
        acts_peer = lax.ppermute(acts[0], "core", swap)
        cot_peer = lax.ppermute(grad_out[0], "core", swap)
    with jax.named_scope("grad_product"):
        mine = product(range(RING), jnp.float32, place, acts[0], grad_out[0])
        farthest = product((RING - 1,), bf16, place, acts_peer, cot_peer, mine[-1])
        blocks = product(range(RING - 1), bf16, place, acts_peer, cot_peer, *mine[:-1])
    with jax.named_scope("grad_ring"):
        hop = [(2 * i, 2 * ((i + 1) % RING)) for i in range(RING)]
        hop += [(2 * ((i + 1) % RING) + 1, 2 * i + 1) for i in range(RING)]
        running = farthest[0]
        for block in blocks[:0:-1]:
            running = add(block, lax.ppermute(running, ("y", "core"), hop)).astype(bf16)
        running = lax.ppermute(running, ("y", "core"), hop)
    with jax.named_scope("grad_pair"):
        other = add(blocks[0][rows:], running[rows:]).astype(bf16)
        other = lax.ppermute(other, "xl", [(0, 1), (1, 0)])
        grad = add(blocks[0][:rows], running[:rows], other)

    with jax.named_scope("adamw"):
        first = 0.9 * first_moment[0] + 0.1 * grad
        second = 0.95 * second_moment[0] + 0.05 * grad * grad
        first_hat = first / (1.0 - 0.9**INNER_STEP)
        second_hat = second / (1.0 - 0.95**INNER_STEP)
        inner_new = inner_weight[0] * (1.0 - 0.0004 * 0.1) - 0.0004 * first_hat / (
            jnp.sqrt(second_hat) + 1e-08
        )
        inner_new = lax.optimization_barrier(inner_new)
    with jax.named_scope("replica_sum"):
        pieces = inner_new.reshape(high, deep, own, cols).transpose(1, 0, 2, 3)
        pieces = lax.all_to_all(pieces.reshape(deep, high * own, cols), "z", 0, 0, tiled=True)
        term = (-0.33 * outer_weight - 0.567 * outer_momentum) * (replicas / OUTER_GAIN)
        mine_here = (jnp.arange(high) == lax.axis_index("xh")).reshape(high, 1, 1)
        total = jnp.sum(pieces, axis=0) + jnp.where(mine_here, term, 0.0).reshape(high * own, cols)
        step = 1
        while step < high:
            total = total + lax.ppermute(total, "xh", [(i, i ^ step) for i in range(high)])
            step *= 2
    with jax.named_scope("row_gather"):
        new = (total * (OUTER_GAIN / replicas)).astype(bf16)
        copies = jnp.broadcast_to(new, (deep,) + new.shape)
        weight_next = lax.all_to_all(copies, "z", 0, 0, tiled=True)
        weight_next = weight_next.reshape(deep, high, own, cols).transpose(1, 0, 2, 3).reshape(rows, cols)
    with jax.named_scope("outer_step"):
        here = jnp.sum(jnp.where(mine_here, total.reshape(high, own, cols), 0.0), axis=0)
        pseudo = outer_weight - (here - term) / replicas
        momentum_next = 0.9 * outer_momentum + pseudo
        outer_next = outer_weight - 0.7 * (pseudo + 0.9 * momentum_next)
    return (outer_next, momentum_next, weight_next)


def solution(mesh, sizes=SIZES):
    grid = Mesh(mesh.devices.reshape(sizes), AXES)
    split = P(REP, FSDP, None)
    outer = P(FSDP + REP, None)
    return jax.shard_map(
        shards,
        mesh=grid,
        in_specs=(split, split, split, split, split, outer, outer),
        out_specs=(outer, outer, P(FSDP, None)),
        check_vma=False,
    )
```

time: 117 us -> 145 us (1.24)
  the two profiles are of different devices: /device:TPU:48 before, /device:TPU:8 now
where the time goes in v3:
time: 145 us
  waiting for transfers between devices  85.7 us (59%)
  starting transfers between devices  46.8 us (32%)
  local copies, waits for them, and re-layouts  5.18 us (4%)
  Pallas kernels  4.53 us (3%)
  other arithmetic  1.58 us (1%)
    ppermute x6, waiting for transfers between devices, shards(): running = add(block, lax.ppermute(running, ('y', 'core'), hop)).astype(bf16)  42.8 us
    all_to_all x1, starting transfers between devices, shards(): lax.all_to_all(pieces.reshape(deep, high * own, cols), 'z', 0, 0, tiled=T...  16.8 us
    ppermute x6, starting transfers between devices, shards(): running = add(block, lax.ppermute(running, ('y', 'core'), hop)).astype(bf16)  13.2 us
    ppermute x2, waiting for transfers between devices, shards(): lax.ppermute(total, 'xh', [(i, i ^ step) for i in range(high)])  12.5 us
    all_to_all x1, waiting for transfers between devices, shards(): lax.all_to_all(pieces.reshape(deep, high * own, cols), 'z', 0, 0, tiled=T...  10.2 us
    all_to_all x1, waiting for transfers between devices, shards(): weight_next = lax.all_to_all(copies, 'z', 0, 0, tiled=True)  8.28 us
    ppermute x1, waiting for transfers between devices, shards(): running = lax.ppermute(running, ('y', 'core'), hop)  7.55 us
    pallas_call x3, Pallas kernels, product(): pl.pallas_call(lambda *refs: product_kernel(offsets, *refs), out_shape=[j...  4.53 us
  transfers between devices with their start and end apart: 14, of which 12 were waited for; matrix products, arithmetic and copies ran while one was open for 1% of the time, Pallas kernels for 3%

profile of v3, /device:TPU:8, one launch (start us, length us, event | category | flops | bytes accessed | tf_op | source)
XLA Modules:
  0.0 144.7 jit_solution(9951298792929715503)
XLA Ops:
  0.6 1.9 %collective-permute-start = (bf16[256,2048]{1,0:T(8,128)(2,1)}, bf16[256,2048]{1,0:T(8,128)(2,1)S(1)}, u32[]{:S(2)}, u32[]{:S(2)}) collective-permute-start(bf16[256,2048]{1,0:T(8,128)(2,1)} %bitcast.21), channel_id=1, source_target_pairs={{0,1},{1,0},{2,3},{3,2},{4,5},{5,4},{6,7},{7,6},{8,9},{9,8},{10,11... | collective-permute-start | bytes 3145736 | tf_op jit(solution)/shard_map/core_swap/ppermute | solution.py:74
  2.6 2.4 %collective-permute-start.1 = (bf16[256,1024]{1,0:T(8,128)(2,1)}, bf16[256,1024]{1,0:T(8,128)(2,1)S(1)}, u32[]{:S(2)}, u32[]{:S(2)}) collective-permute-start(bf16[256,1024]{1,0:T(8,128)(2,1)} %bitcast.23), channel_id=1, source_target_pairs={{0,1},{1,0},{2,3},{3,2},{4,5},{5,4},{6,7},{7,6},{8,9},{9,8},{10,11... | collective-permute-start | bytes 1572872 | tf_op jit(solution)/shard_map/core_swap/ppermute | solution.py:75
  5.1 1.2 copy-done
  6.3 1.0 copy-done.1
  7.3 1.8 %grad_product.3 = (f32[128,1024]{1,0:T(8,128)S(1)}, f32[128,1024]{1,0:T(8,128)S(1)}, f32[128,1024]{1,0:T(8,128)S(1)}, f32[128,1024]{1,0:T(8,128)S(1)}, f32[128,1...) custom-call(s32[3]{0:T(128)S(1)} %pad_add_fusion.refs_0_, ...), custom_call_target="tpu_custom_call" | custom-call | flops 536870912 | bytes 1572864 | tf_op jit(solution)/shard_map/grad_product/pallas_call | solution.py:46
  9.2 0.9 grad_product.5
  10.1 3.6 %collective-permute-start.2 = (bf16[128,1024]{1,0:T(8,128)(2,1)S(1)}, bf16[128,1024]{1,0:T(8,128)(2,1)S(1)}, u32[]{:S(2)}, u32[]{:S(2)}) collective-permute-start(bf16[128,1024]{1,0:T(8,128)(2,1)S(1)} %grad_product.5), channel_id=1, source_target_pairs={{0,2},{2,4},{4,6},{6,8},{8,10},{10,12},{12,14},{14,0},{3,1},{5,3},... | collective-permute-start | bytes 786440 | tf_op jit(solution)/shard_map/grad_ring/ppermute | solution.py:85
  13.7 1.8 %grad_product.4 = (bf16[128,1024]{1,0:T(8,128)(2,1)S(1)}, bf16[128,1024]{1,0:T(8,128)(2,1)S(1)}, bf16[128,1024]{1,0:T(8,128)(2,1)S(1)}, bf16[128,1024]{1,0:T(8,1...) custom-call(s32[3]{0:T(128)S(1)} %pad_add_fusion.refs_0_, ...), custom_call_target="tpu_custom_call" | custom-call | flops 469762048 | bytes 1572864 | tf_op jit(solution)/shard_map/grad_product/pallas_call | solution.py:46
  15.5 5.1 %collective-permute-done.2 = bf16[128,1024]{1,0:T(8,128)(2,1)S(1)} collective-permute-done((bf16[128,1024]{1,0:T(8,128)(2,1)S(1)}, bf16[128,1024]{1,0:T(8,128)(2,1)S(1)}, u32[]{:S(2)}, u32[]{:S(2)}) %collective-permute-start.2) | collective-permute-done | bytes 262176 | tf_op jit(solution)/shard_map/grad_ring/ppermute | solution.py:85
  20.7 1.9 %collective-permute-start.3 = (bf16[128,1024]{1,0:T(8,128)(2,1)S(1)}, bf16[128,1024]{1,0:T(8,128)(2,1)S(1)}, u32[]{:S(2)}, u32[]{:S(2)}) collective-permute-start(bf16[128,1024]{1,0:T(8,128)(2,1)S(1)} %add_convert_fusion.5), channel_id=1, source_target_pairs={{0,2},{2,4},{4,6},{6,8},{8,10},{10,12},{12,14},{14,0},{3,1},{5,3},... | collective-permute-start | bytes 786440 | tf_op jit(solution)/shard_map/grad_ring/ppermute | solution.py:85
  22.6 7.5 %collective-permute-done.3 = bf16[128,1024]{1,0:T(8,128)(2,1)S(1)} collective-permute-done((bf16[128,1024]{1,0:T(8,128)(2,1)S(1)}, bf16[128,1024]{1,0:T(8,128)(2,1)S(1)}, u32[]{:S(2)}, u32[]{:S(2)}) %collective-permute-start.3) | collective-permute-done | bytes 262176 | tf_op jit(solution)/shard_map/grad_ring/ppermute | solution.py:85
  30.2 1.9 %collective-permute-start.4 = (bf16[128,1024]{1,0:T(8,128)(2,1)S(1)}, bf16[128,1024]{1,0:T(8,128)(2,1)S(1)}, u32[]{:S(2)}, u32[]{:S(2)}) collective-permute-start(bf16[128,1024]{1,0:T(8,128)(2,1)S(1)} %add_convert_fusion.4), channel_id=1, source_target_pairs={{0,2},{2,4},{4,6},{6,8},{8,10},{10,12},{12,14},{14,0},{3,1},{5,3},... | collective-permute-start | bytes 786440 | tf_op jit(solution)/shard_map/grad_ring/ppermute | solution.py:85
  32.1 7.5 %collective-permute-done.4 = bf16[128,1024]{1,0:T(8,128)(2,1)S(1)} collective-permute-done((bf16[128,1024]{1,0:T(8,128)(2,1)S(1)}, bf16[128,1024]{1,0:T(8,128)(2,1)S(1)}, u32[]{:S(2)}, u32[]{:S(2)}) %collective-permute-start.4) | collective-permute-done | bytes 262176 | tf_op jit(solution)/shard_map/grad_ring/ppermute | solution.py:85
  39.8 1.9 %collective-permute-start.5 = (bf16[128,1024]{1,0:T(8,128)(2,1)S(1)}, bf16[128,1024]{1,0:T(8,128)(2,1)S(1)}, u32[]{:S(2)}, u32[]{:S(2)}) collective-permute-start(bf16[128,1024]{1,0:T(8,128)(2,1)S(1)} %add_convert_fusion.3), channel_id=1, source_target_pairs={{0,2},{2,4},{4,6},{6,8},{8,10},{10,12},{12,14},{14,0},{3,1},{5,3},... | collective-permute-start | bytes 786440 | tf_op jit(solution)/shard_map/grad_ring/ppermute | solution.py:85
  41.7 7.5 %collective-permute-done.5 = bf16[128,1024]{1,0:T(8,128)(2,1)S(1)} collective-permute-done((bf16[128,1024]{1,0:T(8,128)(2,1)S(1)}, bf16[128,1024]{1,0:T(8,128)(2,1)S(1)}, u32[]{:S(2)}, u32[]{:S(2)}) %collective-permute-start.5) | collective-permute-done | bytes 262176 | tf_op jit(solution)/shard_map/grad_ring/ppermute | solution.py:85
  49.3 1.9 %collective-permute-start.6 = (bf16[128,1024]{1,0:T(8,128)(2,1)S(1)}, bf16[128,1024]{1,0:T(8,128)(2,1)S(1)}, u32[]{:S(2)}, u32[]{:S(2)}) collective-permute-start(bf16[128,1024]{1,0:T(8,128)(2,1)S(1)} %add_convert_fusion.2), channel_id=1, source_target_pairs={{0,2},{2,4},{4,6},{6,8},{8,10},{10,12},{12,14},{14,0},{3,1},{5,3},... | collective-permute-start | bytes 786440 | tf_op jit(solution)/shard_map/grad_ring/ppermute | solution.py:85
  51.2 7.5 %collective-permute-done.6 = bf16[128,1024]{1,0:T(8,128)(2,1)S(1)} collective-permute-done((bf16[128,1024]{1,0:T(8,128)(2,1)S(1)}, bf16[128,1024]{1,0:T(8,128)(2,1)S(1)}, u32[]{:S(2)}, u32[]{:S(2)}) %collective-permute-start.6) | collective-permute-done | bytes 262176 | tf_op jit(solution)/shard_map/grad_ring/ppermute | solution.py:85
  58.8 1.9 %collective-permute-start.7 = (bf16[128,1024]{1,0:T(8,128)(2,1)S(1)}, bf16[128,1024]{1,0:T(8,128)(2,1)S(1)}, u32[]{:S(2)}, u32[]{:S(2)}) collective-permute-start(bf16[128,1024]{1,0:T(8,128)(2,1)S(1)} %add_convert_fusion.1), channel_id=1, source_target_pairs={{0,2},{2,4},{4,6},{6,8},{8,10},{10,12},{12,14},{14,0},{3,1},{5,3},... | collective-permute-start | bytes 786440 | tf_op jit(solution)/shard_map/grad_ring/ppermute | solution.py:85
  60.8 7.5 %collective-permute-done.7 = bf16[128,1024]{1,0:T(8,128)(2,1)S(1)} collective-permute-done((bf16[128,1024]{1,0:T(8,128)(2,1)S(1)}, bf16[128,1024]{1,0:T(8,128)(2,1)S(1)}, u32[]{:S(2)}, u32[]{:S(2)}) %collective-permute-start.7) | collective-permute-done | bytes 262176 | tf_op jit(solution)/shard_map/grad_ring/ppermute | solution.py:85
  68.4 2.1 %collective-permute-start.8 = (bf16[128,1024]{1,0:T(8,128)(2,1)S(1)}, bf16[128,1024]{1,0:T(8,128)(2,1)S(1)}, u32[]{:S(2)}, u32[]{:S(2)}) collective-permute-start(bf16[128,1024]{1,0:T(8,128)(2,1)S(1)} %add_convert_fusion), channel_id=1, source_target_pairs={{0,2},{2,4},{4,6},{6,8},{8,10},{10,12},{12,14},{14,0},{3,1},{5,3},... | collective-permute-start | bytes 786440 | tf_op jit(solution)/shard_map/grad_ring/ppermute | solution.py:86
  70.5 7.5 %collective-permute-done.8 = bf16[128,1024]{1,0:T(8,128)(2,1)S(1)} collective-permute-done((bf16[128,1024]{1,0:T(8,128)(2,1)S(1)}, bf16[128,1024]{1,0:T(8,128)(2,1)S(1)}, u32[]{:S(2)}, u32[]{:S(2)}) %collective-permute-start.8) | collective-permute-done | bytes 262176 | tf_op jit(solution)/shard_map/grad_ring/ppermute | solution.py:86
  78.1 2.5 %collective-permute-start.9 = (bf16[64,1024]{1,0:T(8,128)(2,1)S(1)}, bf16[64,1024]{1,0:T(8,128)(2,1)S(1)}, u32[]{:S(2)}, u32[]{:S(2)}) collective-permute-start(bf16[64,1024]{1,0:T(8,128)(2,1)S(1)} %add_convert_fusion.6), channel_id=1, source_target_pairs={{0,16},{16,0},{1,17},{17,1},{2,18},{18,2},{3,19},{19,3},{4,20},{20... | collective-permute-start | bytes 393224 | tf_op jit(solution)/shard_map/grad_pair/ppermute | solution.py:89
  80.6 4.4 %collective-permute-done.9 = bf16[64,1024]{1,0:T(8,128)(2,1)S(1)} collective-permute-done((bf16[64,1024]{1,0:T(8,128)(2,1)S(1)}, bf16[64,1024]{1,0:T(8,128)(2,1)S(1)}, u32[]{:S(2)}, u32[]{:S(2)}) %collective-permute-start.9) | collective-permute-done | bytes 131104 | tf_op jit(solution)/shard_map/grad_pair/ppermute | solution.py:89
  85.4 0.9 copy.14
  86.3 16.8 %all-to-all-start = ((f32[8,8,1024]{2,1,0:T(8,128)}), f32[8,8,1024]{2,1,0:T(8,128)S(1)}, u32[]{:S(2)}, u32[]{:S(2)}) async-start(f32[8,8,1024]{2,1,0:T(8,128)} %copy.14), calls=%async_computation | async-start | bytes 524288 | tf_op jit(solution)/shard_map/replica_sum/all_to_all | solution.py:103
  103.3 10.2 %all-to-all-done = f32[8,8,1024]{2,1,0:T(8,128)S(1)} async-done(((f32[8,8,1024]{2,1,0:T(8,128)}), f32[8,8,1024]{2,1,0:T(8,128)S(1)}, u32[]{:S(2)}, u32[]{:S(2)}) %all-to-all-start) | async-done | bytes 262176 | tf_op jit(solution)/shard_map/replica_sum/all_to_all | solution.py:103
  113.7 2.5 %collective-permute-start.10 = (f32[8,1024]{1,0:T(8,128)S(1)}, f32[8,1024]{1,0:T(8,128)S(1)}, u32[]{:S(2)}, u32[]{:S(2)}) collective-permute-start(f32[8,1024]{1,0:T(8,128)S(1)} %select_add_fusion), channel_id=1, source_target_pairs={{0,256},{256,0},{512,768},{768,512},{1,257},{257,1},{513,769},{769... | collective-permute-start | bytes 98312 | tf_op jit(solution)/shard_map/replica_sum/ppermute | solution.py:109
  116.2 4.5 %collective-permute-done.10 = f32[8,1024]{1,0:T(8,128)S(1)} collective-permute-done((f32[8,1024]{1,0:T(8,128)S(1)}, f32[8,1024]{1,0:T(8,128)S(1)}, u32[]{:S(2)}, u32[]{:S(2)}) %collective-permute-start.10) | collective-permute-done | bytes 32800 | tf_op jit(solution)/shard_map/replica_sum/ppermute | solution.py:109
  120.7 2.0 %collective-permute-start.11 = (f32[8,1024]{1,0:T(8,128)S(1)}, f32[8,1024]{1,0:T(8,128)S(1)}, u32[]{:S(2)}, u32[]{:S(2)}) collective-permute-start(f32[8,1024]{1,0:T(8,128)S(1)} %add.68), channel_id=1, source_target_pairs={{0,512},{256,768},{512,0},{768,256},{1,513},{257,769},{513,1},{769... | collective-permute-start | bytes 98312 | tf_op jit(solution)/shard_map/replica_sum/ppermute | solution.py:109
  122.7 7.9 %collective-permute-done.11 = f32[8,1024]{1,0:T(8,128)S(1)} collective-permute-done((f32[8,1024]{1,0:T(8,128)S(1)}, f32[8,1024]{1,0:T(8,128)S(1)}, u32[]{:S(2)}, u32[]{:S(2)}) %collective-permute-start.11) | collective-permute-done | bytes 32800 | tf_op jit(solution)/shard_map/replica_sum/ppermute | solution.py:109
  131.3 3.4 %all-to-all-start.1 = ((bf16[8,8,1024]{2,1,0:T(8,128)(2,1)}), bf16[8,8,1024]{2,1,0:T(8,128)(2,1)S(1)}, u32[]{:S(2)}, u32[]{:S(2)}) async-start(bf16[8,8,1024]{2,1,0:T(8,128)(2,1)} %broadcast_in_dim.45), calls=%async_computation.1 | async-start | bytes 262144 | tf_op jit(solution)/shard_map/row_gather/all_to_all | solution.py:114
  135.4 8.3 %all-to-all-done.1 = bf16[8,8,1024]{2,1,0:T(8,128)(2,1)S(1)} async-done(((bf16[8,8,1024]{2,1,0:T(8,128)(2,1)}), bf16[8,8,1024]{2,1,0:T(8,128)(2,1)S(1)}, u32[]{:S(2)}, u32[]{:S(2)}) %all-to-all-start.1) | async-done | bytes 131104 | tf_op jit(solution)/shard_map/row_gather/all_to_all | solution.py:114
  (42 shorter events, 3.6 us)
Async XLA Ops:
  0.6 8.5 %collective-permute-start = (bf16[256,2048]{1,0:T(8,128)(2,1)}, bf16[256,2048]{1,0:T(8,128)(2,1)S(1)}, u32[]{:S(2)}, u32[]{:S(2)}) collective-permute-start(bf16[256,2048]{1,0:T(8,128)(2,1)} %bitcast.21), channel_id=1, source_target_pairs={{0,1},{1,0},{2,3},{3,2},{4,5},{5,4},{6,7},{7,6},{8,9},{9,8},{10,11... | collective-permute-start | bytes 3145736 | tf_op jit(solution)/shard_map/core_swap/ppermute | solution.py:74
  2.6 6.6 %collective-permute-start.1 = (bf16[256,1024]{1,0:T(8,128)(2,1)}, bf16[256,1024]{1,0:T(8,128)(2,1)S(1)}, u32[]{:S(2)}, u32[]{:S(2)}) collective-permute-start(bf16[256,1024]{1,0:T(8,128)(2,1)} %bitcast.23), channel_id=1, source_target_pairs={{0,1},{1,0},{2,3},{3,2},{4,5},{5,4},{6,7},{7,6},{8,9},{9,8},{10,11... | collective-permute-start | bytes 1572872 | tf_op jit(solution)/shard_map/core_swap/ppermute | solution.py:75
  5.1 1.2 copy-start
  6.3 1.0 copy-start.1
  10.1 10.5 %collective-permute-start.2 = (bf16[128,1024]{1,0:T(8,128)(2,1)S(1)}, bf16[128,1024]{1,0:T(8,128)(2,1)S(1)}, u32[]{:S(2)}, u32[]{:S(2)}) collective-permute-start(bf16[128,1024]{1,0:T(8,128)(2,1)S(1)} %grad_product.5), channel_id=1, source_target_pairs={{0,2},{2,4},{4,6},{6,8},{8,10},{10,12},{12,14},{14,0},{3,1},{5,3},... | collective-permute-start | bytes 786440 | tf_op jit(solution)/shard_map/grad_ring/ppermute | solution.py:85
  20.7 9.5 %collective-permute-start.3 = (bf16[128,1024]{1,0:T(8,128)(2,1)S(1)}, bf16[128,1024]{1,0:T(8,128)(2,1)S(1)}, u32[]{:S(2)}, u32[]{:S(2)}) collective-permute-start(bf16[128,1024]{1,0:T(8,128)(2,1)S(1)} %add_convert_fusion.5), channel_id=1, source_target_pairs={{0,2},{2,4},{4,6},{6,8},{8,10},{10,12},{12,14},{14,0},{3,1},{5,3},... | collective-permute-start | bytes 786440 | tf_op jit(solution)/shard_map/grad_ring/ppermute | solution.py:85
  30.2 9.5 %collective-permute-start.4 = (bf16[128,1024]{1,0:T(8,128)(2,1)S(1)}, bf16[128,1024]{1,0:T(8,128)(2,1)S(1)}, u32[]{:S(2)}, u32[]{:S(2)}) collective-permute-start(bf16[128,1024]{1,0:T(8,128)(2,1)S(1)} %add_convert_fusion.4), channel_id=1, source_target_pairs={{0,2},{2,4},{4,6},{6,8},{8,10},{10,12},{12,14},{14,0},{3,1},{5,3},... | collective-permute-start | bytes 786440 | tf_op jit(solution)/shard_map/grad_ring/ppermute | solution.py:85
  39.8 9.5 %collective-permute-start.5 = (bf16[128,1024]{1,0:T(8,128)(2,1)S(1)}, bf16[128,1024]{1,0:T(8,128)(2,1)S(1)}, u32[]{:S(2)}, u32[]{:S(2)}) collective-permute-start(bf16[128,1024]{1,0:T(8,128)(2,1)S(1)} %add_convert_fusion.3), channel_id=1, source_target_pairs={{0,2},{2,4},{4,6},{6,8},{8,10},{10,12},{12,14},{14,0},{3,1},{5,3},... | collective-permute-start | bytes 786440 | tf_op jit(solution)/shard_map/grad_ring/ppermute | solution.py:85
  49.3 9.5 %collective-permute-start.6 = (bf16[128,1024]{1,0:T(8,128)(2,1)S(1)}, bf16[128,1024]{1,0:T(8,128)(2,1)S(1)}, u32[]{:S(2)}, u32[]{:S(2)}) collective-permute-start(bf16[128,1024]{1,0:T(8,128)(2,1)S(1)} %add_convert_fusion.2), channel_id=1, source_target_pairs={{0,2},{2,4},{4,6},{6,8},{8,10},{10,12},{12,14},{14,0},{3,1},{5,3},... | collective-permute-start | bytes 786440 | tf_op jit(solution)/shard_map/grad_ring/ppermute | solution.py:85
  58.8 9.5 %collective-permute-start.7 = (bf16[128,1024]{1,0:T(8,128)(2,1)S(1)}, bf16[128,1024]{1,0:T(8,128)(2,1)S(1)}, u32[]{:S(2)}, u32[]{:S(2)}) collective-permute-start(bf16[128,1024]{1,0:T(8,128)(2,1)S(1)} %add_convert_fusion.1), channel_id=1, source_target_pairs={{0,2},{2,4},{4,6},{6,8},{8,10},{10,12},{12,14},{14,0},{3,1},{5,3},... | collective-permute-start | bytes 786440 | tf_op jit(solution)/shard_map/grad_ring/ppermute | solution.py:85
  68.3 16.6 %copy-start.3 = (f32[1,64,1024]{2,1,0:T(8,128)S(1)}, f32[1,64,1024]{2,1,0:T(8,128)}, u32[]{:S(2)}) copy-start(f32[1,64,1024]{2,1,0:T(8,128)} %param.10) | copy-start | bytes 786436
  68.3 16.6 %copy-start.4 = (f32[1,64,1024]{2,1,0:T(8,128)S(1)}, f32[1,64,1024]{2,1,0:T(8,128)}, u32[]{:S(2)}) copy-start(f32[1,64,1024]{2,1,0:T(8,128)} %param.9) | copy-start | bytes 786436
  68.4 16.5 %copy-start.2 = (f32[1,64,1024]{2,1,0:T(8,128)S(1)}, f32[1,64,1024]{2,1,0:T(8,128)}, u32[]{:S(2)}) copy-start(f32[1,64,1024]{2,1,0:T(8,128)} %param.11) | copy-start | bytes 786436
  68.4 9.6 %collective-permute-start.8 = (bf16[128,1024]{1,0:T(8,128)(2,1)S(1)}, bf16[128,1024]{1,0:T(8,128)(2,1)S(1)}, u32[]{:S(2)}, u32[]{:S(2)}) collective-permute-start(bf16[128,1024]{1,0:T(8,128)(2,1)S(1)} %add_convert_fusion), channel_id=1, source_target_pairs={{0,2},{2,4},{4,6},{6,8},{8,10},{10,12},{12,14},{14,0},{3,1},{5,3},... | collective-permute-start | bytes 786440 | tf_op jit(solution)/shard_map/grad_ring/ppermute | solution.py:86
  78.1 6.9 %collective-permute-start.9 = (bf16[64,1024]{1,0:T(8,128)(2,1)S(1)}, bf16[64,1024]{1,0:T(8,128)(2,1)S(1)}, u32[]{:S(2)}, u32[]{:S(2)}) collective-permute-start(bf16[64,1024]{1,0:T(8,128)(2,1)S(1)} %add_convert_fusion.6), channel_id=1, source_target_pairs={{0,16},{16,0},{1,17},{17,1},{2,18},{18,2},{3,19},{19,3},{4,20},{20... | collective-permute-start | bytes 393224 | tf_op jit(solution)/shard_map/grad_pair/ppermute | solution.py:89
  86.3 16.8 %copy-start.5 = (f32[2,1024]{1,0:T(2,128)S(1)}, f32[2,1024]{1,0:T(2,128)}, u32[]{:S(2)}) copy-start(f32[2,1024]{1,0:T(2,128)} %param.12) | copy-start | bytes 24580
  86.3 16.8 %copy-start.6 = (f32[2,1024]{1,0:T(2,128)S(1)}, f32[2,1024]{1,0:T(2,128)}, u32[]{:S(2)}) copy-start(f32[2,1024]{1,0:T(2,128)} %param.13) | copy-start | bytes 24580
  86.3 27.3 %all-to-all-start = ((f32[8,8,1024]{2,1,0:T(8,128)}), f32[8,8,1024]{2,1,0:T(8,128)S(1)}, u32[]{:S(2)}, u32[]{:S(2)}) async-start(f32[8,8,1024]{2,1,0:T(8,128)} %copy.14), calls=%async_computation | async-start | bytes 524288 | tf_op jit(solution)/shard_map/replica_sum/all_to_all | solution.py:103
  113.7 7.0 %collective-permute-start.10 = (f32[8,1024]{1,0:T(8,128)S(1)}, f32[8,1024]{1,0:T(8,128)S(1)}, u32[]{:S(2)}, u32[]{:S(2)}) collective-permute-start(f32[8,1024]{1,0:T(8,128)S(1)} %select_add_fusion), channel_id=1, source_target_pairs={{0,256},{256,0},{512,768},{768,512},{1,257},{257,1},{513,769},{769... | collective-permute-start | bytes 98312 | tf_op jit(solution)/shard_map/replica_sum/ppermute | solution.py:109
  120.7 9.9 %collective-permute-start.11 = (f32[8,1024]{1,0:T(8,128)S(1)}, f32[8,1024]{1,0:T(8,128)S(1)}, u32[]{:S(2)}, u32[]{:S(2)}) collective-permute-start(f32[8,1024]{1,0:T(8,128)S(1)} %add.68), channel_id=1, source_target_pairs={{0,512},{256,768},{512,0},{768,256},{1,513},{257,769},{513,1},{769... | collective-permute-start | bytes 98312 | tf_op jit(solution)/shard_map/replica_sum/ppermute | solution.py:109
  131.3 12.4 %all-to-all-start.1 = ((bf16[8,8,1024]{2,1,0:T(8,128)(2,1)}), bf16[8,8,1024]{2,1,0:T(8,128)(2,1)S(1)}, u32[]{:S(2)}, u32[]{:S(2)}) async-start(bf16[8,8,1024]{2,1,0:T(8,128)(2,1)} %broadcast_in_dim.45), calls=%async_computation.1 | async-start | bytes 262144 | tf_op jit(solution)/shard_map/row_gather/all_to_all | solution.py:114

commit v4 on v2

v4 whole, which is shorter than its diff:
```python
import jax
import jax.numpy as jnp
from jax import lax
from jax.experimental import pallas as pl
from jax.experimental.pallas import tpu as pltpu
from jax.sharding import Mesh, PartitionSpec as P

INNER_STEP = 500
AXES = ("xh", "z", "xl", "y", "core")
SIZES = (4, 8, 2, 8, 2)
REP = ("xh", "z")
FSDP = ("xl", "y", "core")
RING = 8


def product_kernel(offsets, place, acts, cot, *refs):
    xl, y, core = place[0], place[1], place[2]
    before, (near, far) = refs[:-2], refs[-2:]
    lane = lax.broadcasted_iota(jnp.int32, (1, 128), 1)
    own_side = (lane < 64) == (core == 0)

    def columns(target):
        def block(side):
            start = pl.multiple_of((side * RING + target) * 128, 128)
            return acts[:, pl.ds(start, 128)].astype(jnp.float32)

        own, other = block(xl), block(1 - xl)
        still = jnp.where(core == 0, own, other)
        moved = pltpu.roll(jnp.where(core == 0, other, own), 64, 1)
        return jnp.where(own_side, still, moved).astype(jnp.bfloat16)

    for i, offset in enumerate(offsets):
        total = lax.dot_general(
            columns(lax.rem(y + offset, RING)), cot[...], (((0,), (0,)), ((), ())),
            preferred_element_type=jnp.float32,
        )
        for out, part, part_before in zip((near, far), (total[:64], total[64:]), before or (None, None)):
            if before:
                part = part + part_before[i]
            out[i] = part.astype(out.dtype)


def product(offsets, dtype, place, acts, cot, *before):
    vmem = pl.BlockSpec(memory_space=pltpu.VMEM)
    tokens, cols = cot.shape
    return pl.pallas_call(
        lambda *refs: product_kernel(offsets, *refs),
        out_shape=[jax.ShapeDtypeStruct((len(offsets), 64, cols), dtype)] * 2,
        in_specs=[pl.BlockSpec(memory_space=pltpu.SMEM)] + [vmem] * (2 + len(before)),
        out_specs=[vmem] * 2,
        compiler_params=pltpu.CompilerParams(vmem_limit_bytes=24 * 1024 * 1024),
        cost_estimate=pl.CostEstimate(
            flops=2 * 128 * len(offsets) * tokens * cols,
            bytes_accessed=2 * tokens * (acts.shape[1] + cols),
            transcendentals=0,
        ),
    )(place, acts, cot, *before)


def add(*terms):
    return sum(t.astype(jnp.float32) for t in terms)


def shards(acts, grad_out, inner_weight, first_moment, second_moment, outer_weight, outer_momentum):
    replicas = lax.axis_size(REP)
    rows, cols = inner_weight.shape[1:]
    own = rows // replicas
    bf16 = jnp.bfloat16
    place = jnp.stack([lax.axis_index(a) for a in FSDP])

    swap = [(0, 1), (1, 0)]
    ring = [(i, (i + 1) % RING) for i in range(RING)]
    back = [(j, i) for i, j in ring]
    with jax.named_scope("core_swap"):
        acts_peer = lax.ppermute(acts[0], "core", swap)
        cot_peer = lax.ppermute(grad_out[0], "core", swap)
    with jax.named_scope("grad_product"):
        early, late = (4, 3, 5), (2, 6, 1, 7, 0)
        mine_early = product(early, jnp.float32, place, acts[0], grad_out[0])
        mine_late = product(late, jnp.float32, place, acts[0], grad_out[0])
        near, far = product(early, bf16, place, acts_peer, cot_peer, *mine_early)
        near_late, far_late = product(late, bf16, place, acts_peer, cot_peer, *mine_late)
    with jax.named_scope("grad_ring"):
        far_late = lax.ppermute(far_late, "xl", swap)
        up = lax.ppermute(near[0], "y", ring)
        down = lax.ppermute(far[0], "y", back)
        up = jnp.concatenate([add(near[1], up).astype(bf16), far[1]])
        down = jnp.concatenate([near[2], add(far[2], down).astype(bf16)])
        up = lax.ppermute(up, "y", ring)
        down = lax.ppermute(down, "y", back)
        up_far = lax.ppermute(up[rows:], "xl", swap)
        down_far = lax.ppermute(down[rows:], "xl", swap)
        up = add(up[:rows], up_far, near_late[0], far_late[0]).astype(bf16)
        down = add(down[:rows], down_far, near_late[1], far_late[1]).astype(bf16)
        up = lax.ppermute(up, "y", ring)
        down = lax.ppermute(down, "y", back)
        up = add(up, near_late[2], far_late[2]).astype(bf16)
        down = add(down, near_late[3], far_late[3]).astype(bf16)
        up = lax.ppermute(up, "y", ring)
        down = lax.ppermute(down, "y", back)
        grad = add(up, down, near_late[4], far_late[4])

    with jax.named_scope("adamw"):
        first = 0.9 * first_moment[0] + 0.1 * grad
        second = 0.95 * second_moment[0] + 0.05 * grad * grad
        first_hat = first / (1.0 - 0.9**INNER_STEP)
        second_hat = second / (1.0 - 0.95**INNER_STEP)
        inner_new = inner_weight[0] * (1.0 - 0.0004 * 0.1) - 0.0004 * first_hat / (
            jnp.sqrt(second_hat) + 1e-08
        )
        inner_new = lax.optimization_barrier(inner_new)
    with jax.named_scope("replica_sum"):
        pieces = lax.all_to_all(inner_new.reshape(replicas, own, cols), REP, 0, 0, tiled=True)
        summed = jnp.sum(pieces, axis=0)
    with jax.named_scope("outer_step"):
        pseudo = outer_weight - summed / replicas
        momentum_next = 0.9 * outer_momentum + pseudo
        outer_next = outer_weight - 0.7 * (pseudo + 0.9 * momentum_next)
    with jax.named_scope("row_gather"):
        new = outer_next.astype(bf16).reshape(1, own * cols // 128, 128)
        copies = jnp.broadcast_to(new, (replicas,) + new.shape[1:])
        weight_next = lax.all_to_all(copies, REP, 0, 0, tiled=True).reshape(rows, cols)
    return (outer_next, momentum_next, weight_next)


def solution(mesh, sizes=SIZES):
    grid = Mesh(mesh.devices.reshape(sizes), AXES)
    split = P(REP, FSDP, None)
    outer = P(FSDP + REP, None)
    return jax.shard_map(
        shards,
        mesh=grid,
        in_specs=(split, split, split, split, split, outer, outer),
        out_specs=(outer, outer, P(FSDP, None)),
        check_vma=False,
    )
```

time: 117 us -> 120 us (1.026)
  the two profiles are of different devices: /device:TPU:48 before, /device:TPU:32 now
where the time goes in v4:
time: 120 us; the launch traced here: 119 us
  starting transfers between devices  48.2 us (40%)
  blocking collectives  47.7 us (40%)
  waiting for transfers between devices  12.6 us (10%)
  Pallas kernels  5.21 us (4%)
  local copies, waits for them, and re-layouts  3.25 us (3%)
  other arithmetic  1.44 us (1%)
    all_to_all x1, blocking collectives, shards(): lax.all_to_all(inner_new.reshape(replicas, own, cols), REP, 0, 0, tiled=T...  31 us
    ppermute x3, starting transfers between devices, shards(): down = lax.ppermute(down, 'y', back)  20.7 us
    all_to_all x1, blocking collectives, shards(): lax.all_to_all(copies, REP, 0, 0, tiled=True).reshape(rows, cols)  16.7 us
    ppermute x3, waiting for transfers between devices, shards(): down = lax.ppermute(down, 'y', back)  7.06 us
    ppermute x3, starting transfers between devices, shards(): up = lax.ppermute(up, 'y', ring)  6.54 us
    pallas_call x4, Pallas kernels, product(): pl.pallas_call(lambda *refs: product_kernel(offsets, *refs), out_shape=[j...  5.21 us
    ppermute x1, starting transfers between devices, shards(): down_far = lax.ppermute(down[rows:], 'xl', swap)  3.77 us
    ppermute x1, starting transfers between devices, shards(): up_far = lax.ppermute(up[rows:], 'xl', swap)  3.64 us
  transfers between devices with their start and end apart: 13, of which 7 were waited for; matrix products, arithmetic and copies ran while one was open for 0% of the time, Pallas kernels for 3%

profile of v4, /device:TPU:32, one launch (start us, length us, event | category | flops | bytes accessed | tf_op | source)
XLA Modules:
  0.0 119.3 jit_solution(17820146581836720266)
XLA Ops:
  0.6 1.9 %collective-permute-start = (bf16[256,2048]{1,0:T(8,128)(2,1)}, bf16[256,2048]{1,0:T(8,128)(2,1)S(1)}, u32[]{:S(2)}, u32[]{:S(2)}) collective-permute-start(bf16[256,2048]{1,0:T(8,128)(2,1)} %bitcast.69), channel_id=1, source_target_pairs={{0,1},{1,0},{2,3},{3,2},{4,5},{5,4},{6,7},{7,6},{8,9},{9,8},{10,11... | collective-permute-start | bytes 3145736 | tf_op jit(solution)/shard_map/core_swap/ppermute | solution.py:75
  2.6 2.4 %collective-permute-start.1 = (bf16[256,1024]{1,0:T(8,128)(2,1)}, bf16[256,1024]{1,0:T(8,128)(2,1)S(1)}, u32[]{:S(2)}, u32[]{:S(2)}) collective-permute-start(bf16[256,1024]{1,0:T(8,128)(2,1)} %bitcast.72), channel_id=1, source_target_pairs={{0,1},{1,0},{2,3},{3,2},{4,5},{5,4},{6,7},{7,6},{8,9},{9,8},{10,11... | collective-permute-start | bytes 1572872 | tf_op jit(solution)/shard_map/core_swap/ppermute | solution.py:76
  5.1 1.2 %copy-done = bf16[1,256,2048]{2,1,0:T(8,128)(2,1)S(1)} copy-done((bf16[1,256,2048]{2,1,0:T(8,128)(2,1)S(1)}, bf16[1,256,2048]{2,1,0:T(8,128)(2,1)}, u32[]{:S(2)}) %copy-start) | copy-done | bytes 1048600
  6.3 1.0 copy-done.1
  7.3 1.1 grad_product.4
  8.5 1.4 %grad_product.6 = (f32[5,64,1024]{2,1,0:T(8,128)S(1)}, f32[5,64,1024]{2,1,0:T(8,128)S(1)}) custom-call(s32[3]{0:T(128)S(1)} %pad_add_fusion.refs_0_, bf16[256,2048]{1,0:T(8,128)(2,1)S(1)} %bitcast.71, bf16[256,1024]{1,0:T(8,128)(2,1)S(1)} %bitcast.74), custom_call_target="tpu_custom_call" | custom-call | flops 335544320 | bytes 1572864 | tf_op jit(solution)/shard_map/grad_product/pallas_call | solution.py:46
  9.9 1.2 grad_product.5
  11.1 2.2 %collective-permute-start.8 = (bf16[64,1024]{1,0:T(8,128)(2,1)S(1)}, bf16[64,1024]{1,0:T(8,128)(2,1)S(1)}, u32[]{:S(2)}, u32[]{:S(2)}) collective-permute-start(bf16[64,1024]{1,0:T(8,128)(2,1)S(1)} %get-tuple-element.29), channel_id=1, source_target_pairs={{2,0},{4,2},{6,4},{8,6},{10,8},{12,10},{14,12},{0,14},{3,1},{5,3},... | collective-permute-start | bytes 393224 | tf_op jit(solution)/shard_map/grad_ring/ppermute | solution.py:86
  13.4 3.6 %collective-permute-start.2 = (bf16[64,1024]{1,0:T(8,128)(2,1)S(1)}, bf16[64,1024]{1,0:T(8,128)(2,1)S(1)}, u32[]{:S(2)}, u32[]{:S(2)}) collective-permute-start(bf16[64,1024]{1,0:T(8,128)(2,1)S(1)} %get-tuple-element.26), channel_id=1, source_target_pairs={{0,2},{2,4},{4,6},{6,8},{8,10},{10,12},{12,14},{14,0},{1,3},{3,5},... | collective-permute-start | bytes 393224 | tf_op jit(solution)/shard_map/grad_ring/ppermute | solution.py:85
  17.0 1.5 %grad_product.7 = (bf16[5,64,1024]{2,1,0:T(8,128)(2,1)S(1)}, bf16[5,64,1024]{2,1,0:T(8,128)(2,1)S(1)}) custom-call(s32[3]{0:T(128)S(1)} %pad_add_fusion.refs_0_, bf16[256,2048]{1,0:T(8,128)(2,1)S(1)} %collective-permute-done.refs_1_, bf16[256,1024]{1,0:T(8,128)(2,1)S(1)} %collective-permute-done.1.refs_2_, f32[5,64,1024]{2,1,0:T(8,128)S(1)} %get-tuple-element.15.refs_3_, ...), custom_call_target="tpu_custom_call" | custom-call | flops 335544320 | bytes 1572864 | tf_op jit(solution)/shard_map/grad_product/pallas_call | solution.py:46
  18.5 3.4 %collective-permute-start.5 = (bf16[5,64,1024]{2,1,0:T(8,128)(2,1)S(1)}, bf16[5,64,1024]{2,1,0:T(8,128)(2,1)S(1)}, u32[]{:S(2)}, u32[]{:S(2)}) collective-permute-start(bf16[5,64,1024]{2,1,0:T(8,128)(2,1)S(1)} %get-tuple-element.18), channel_id=1, source_target_pairs={{0,16},{16,0},{1,17},{17,1},{2,18},{18,2},{3,19},{19,3},{4,20},{20... | collective-permute-start | bytes 1966088 | tf_op jit(solution)/shard_map/grad_ring/ppermute | solution.py:84
  22.0 11.7 %collective-permute-start.9 = (bf16[128,1024]{1,0:T(8,128)(2,1)S(1)}, bf16[128,1024]{1,0:T(8,128)(2,1)S(1)}, u32[]{:S(2)}, u32[]{:S(2)}) collective-permute-start(bf16[128,1024]{1,0:T(8,128)(2,1)S(1)} %pad_maximum_fusion.1), channel_id=1, source_target_pairs={{2,0},{4,2},{6,4},{8,6},{10,8},{12,10},{14,12},{0,14},{3,1},{5,3},... | collective-permute-start | bytes 786440 | tf_op jit(solution)/shard_map/grad_ring/ppermute | solution.py:90
  33.8 1.9 %collective-permute-start.3 = (bf16[128,1024]{1,0:T(8,128)(2,1)S(1)}, bf16[128,1024]{1,0:T(8,128)(2,1)S(1)}, u32[]{:S(2)}, u32[]{:S(2)}) collective-permute-start(bf16[128,1024]{1,0:T(8,128)(2,1)S(1)} %pad_maximum_fusion), channel_id=1, source_target_pairs={{0,2},{2,4},{4,6},{6,8},{8,10},{10,12},{12,14},{14,0},{1,3},{3,5},... | collective-permute-start | bytes 786440 | tf_op jit(solution)/shard_map/grad_ring/ppermute | solution.py:89
  35.7 3.4 %collective-permute-done.9 = bf16[128,1024]{1,0:T(8,128)(2,1)S(1)} collective-permute-done((bf16[128,1024]{1,0:T(8,128)(2,1)S(1)}, bf16[128,1024]{1,0:T(8,128)(2,1)S(1)}, u32[]{:S(2)}, u32[]{:S(2)}) %collective-permute-start.9) | collective-permute-done | bytes 262176 | tf_op jit(solution)/shard_map/grad_ring/ppermute | solution.py:90
  39.2 3.8 %collective-permute-start.10 = (bf16[64,1024]{1,0:T(8,128)(2,1)S(1)}, bf16[64,1024]{1,0:T(8,128)(2,1)S(1)}, u32[]{:S(2)}, u32[]{:S(2)}) collective-permute-start(bf16[64,1024]{1,0:T(8,128)(2,1)S(1)} %slice.85), channel_id=1, source_target_pairs={{0,16},{16,0},{1,17},{17,1},{2,18},{18,2},{3,19},{19,3},{4,20},{20... | collective-permute-start | bytes 393224 | tf_op jit(solution)/shard_map/grad_ring/ppermute | solution.py:92
  43.0 0.4 collective-permute-done.3
  43.3 3.6 %collective-permute-start.4 = (bf16[64,1024]{1,0:T(8,128)(2,1)S(1)}, bf16[64,1024]{1,0:T(8,128)(2,1)S(1)}, u32[]{:S(2)}, u32[]{:S(2)}) collective-permute-start(bf16[64,1024]{1,0:T(8,128)(2,1)S(1)} %slice.81), channel_id=1, source_target_pairs={{0,16},{16,0},{1,17},{17,1},{2,18},{18,2},{3,19},{19,3},{4,20},{20... | collective-permute-start | bytes 393224 | tf_op jit(solution)/shard_map/grad_ring/ppermute | solution.py:91
  47.0 3.2 %collective-permute-done.4 = bf16[64,1024]{1,0:T(8,128)(2,1)S(1)} collective-permute-done((bf16[64,1024]{1,0:T(8,128)(2,1)S(1)}, bf16[64,1024]{1,0:T(8,128)(2,1)S(1)}, u32[]{:S(2)}, u32[]{:S(2)}) %collective-permute-start.4) | collective-permute-done | bytes 131104 | tf_op jit(solution)/shard_map/grad_ring/ppermute | solution.py:91
  50.2 0.2 fusion.9
  50.4 2.2 %collective-permute-start.6 = (bf16[64,1024]{1,0:T(8,128)(2,1)S(1)}, bf16[64,1024]{1,0:T(8,128)(2,1)S(1)}, u32[]{:S(2)}, u32[]{:S(2)}) collective-permute-start(bf16[64,1024]{1,0:T(8,128)(2,1)S(1)} %get-tuple-element.24), channel_id=1, source_target_pairs={{0,2},{2,4},{4,6},{6,8},{8,10},{10,12},{12,14},{14,0},{1,3},{3,5},... | collective-permute-start | bytes 393224 | tf_op jit(solution)/shard_map/grad_ring/ppermute | solution.py:95
  52.6 5.1 %collective-permute-start.11 = (bf16[64,1024]{1,0:T(8,128)(2,1)S(1)}, bf16[64,1024]{1,0:T(8,128)(2,1)S(1)}, u32[]{:S(2)}, u32[]{:S(2)}) collective-permute-start(bf16[64,1024]{1,0:T(8,128)(2,1)S(1)} %get-tuple-element.25), channel_id=1, source_target_pairs={{2,0},{4,2},{6,4},{8,6},{10,8},{12,10},{14,12},{0,14},{3,1},{5,3},... | collective-permute-start | bytes 393224 | tf_op jit(solution)/shard_map/grad_ring/ppermute | solution.py:96
  57.7 1.0 collective-permute-done.6
  58.7 1.5 %collective-permute-done.11 = bf16[64,1024]{1,0:T(8,128)(2,1)S(1)} collective-permute-done((bf16[64,1024]{1,0:T(8,128)(2,1)S(1)}, bf16[64,1024]{1,0:T(8,128)(2,1)S(1)}, u32[]{:S(2)}, u32[]{:S(2)}) %collective-permute-start.11) | collective-permute-done | bytes 131104 | tf_op jit(solution)/shard_map/grad_ring/ppermute | solution.py:96
  60.3 2.4 %collective-permute-start.7 = (bf16[64,1024]{1,0:T(8,128)(2,1)S(1)}, bf16[64,1024]{1,0:T(8,128)(2,1)S(1)}, u32[]{:S(2)}, u32[]{:S(2)}) collective-permute-start(bf16[64,1024]{1,0:T(8,128)(2,1)S(1)} %get-tuple-element.22), channel_id=1, source_target_pairs={{0,2},{2,4},{4,6},{6,8},{8,10},{10,12},{12,14},{14,0},{1,3},{3,5},... | collective-permute-start | bytes 393224 | tf_op jit(solution)/shard_map/grad_ring/ppermute | solution.py:99
  62.7 3.9 %collective-permute-start.12 = (bf16[64,1024]{1,0:T(8,128)(2,1)S(1)}, bf16[64,1024]{1,0:T(8,128)(2,1)S(1)}, u32[]{:S(2)}, u32[]{:S(2)}) collective-permute-start(bf16[64,1024]{1,0:T(8,128)(2,1)S(1)} %get-tuple-element.23), channel_id=1, source_target_pairs={{2,0},{4,2},{6,4},{8,6},{10,8},{12,10},{14,12},{0,14},{3,1},{5,3},... | collective-permute-start | bytes 393224 | tf_op jit(solution)/shard_map/grad_ring/ppermute | solution.py:100
  66.6 1.0 collective-permute-done.7
  67.6 2.1 %collective-permute-done.12 = bf16[64,1024]{1,0:T(8,128)(2,1)S(1)} collective-permute-done((bf16[64,1024]{1,0:T(8,128)(2,1)S(1)}, bf16[64,1024]{1,0:T(8,128)(2,1)S(1)}, u32[]{:S(2)}, u32[]{:S(2)}) %collective-permute-start.12) | collective-permute-done | bytes 131104 | tf_op jit(solution)/shard_map/grad_ring/ppermute | solution.py:100
  69.7 0.2 fusion.4
  70.1 31.0 %all_to_all.10 = f32[32,2,1024]{2,1,0:T(2,128)S(1)} all-to-all(f32[32,2,1024]{2,1,0:T(2,128)S(1)} %reshape.44), channel_id=1, replica_groups=mesh['xh'=4,'z'=8,'xl'=2,'y'=8,'core'=2] {'xh','z'}, dimensions={0} | all-to-all | bytes 524288 | tf_op jit(solution)/shard_map/replica_sum/all_to_all | solution.py:113
  101.2 0.6 fusion.12
  101.9 16.7 %all_to_all.11 = bf16[32,16,128]{2,1,0:T(8,128)(2,1)S(1)} all-to-all(bf16[32,16,128]{2,1,0:T(8,128)(2,1)S(1)} %broadcast_in_dim.8), channel_id=1, replica_groups=mesh['xh'=4,'z'=8,'xl'=2,'y'=8,'core'=2] {'xh','z'}, dimensions={0} | all-to-all | bytes 262144 | tf_op jit(solution)/shard_map/row_gather/all_to_all | solution.py:122
  118.6 0.7 reshape.45
  (32 shorter events, 0.7 us)
Async XLA Ops:
  0.6 9.3 %collective-permute-start = (bf16[256,2048]{1,0:T(8,128)(2,1)}, bf16[256,2048]{1,0:T(8,128)(2,1)S(1)}, u32[]{:S(2)}, u32[]{:S(2)}) collective-permute-start(bf16[256,2048]{1,0:T(8,128)(2,1)} %bitcast.69), channel_id=1, source_target_pairs={{0,1},{1,0},{2,3},{3,2},{4,5},{5,4},{6,7},{7,6},{8,9},{9,8},{10,11... | collective-permute-start | bytes 3145736 | tf_op jit(solution)/shard_map/core_swap/ppermute | solution.py:75
  2.6 7.4 %collective-permute-start.1 = (bf16[256,1024]{1,0:T(8,128)(2,1)}, bf16[256,1024]{1,0:T(8,128)(2,1)S(1)}, u32[]{:S(2)}, u32[]{:S(2)}) collective-permute-start(bf16[256,1024]{1,0:T(8,128)(2,1)} %bitcast.72), channel_id=1, source_target_pairs={{0,1},{1,0},{2,3},{3,2},{4,5},{5,4},{6,7},{7,6},{8,9},{9,8},{10,11... | collective-permute-start | bytes 1572872 | tf_op jit(solution)/shard_map/core_swap/ppermute | solution.py:76
  5.1 1.2 %copy-start = (bf16[1,256,2048]{2,1,0:T(8,128)(2,1)S(1)}, bf16[1,256,2048]{2,1,0:T(8,128)(2,1)}, u32[]{:S(2)}) copy-start(bf16[1,256,2048]{2,1,0:T(8,128)(2,1)} %param.7) | copy-start | bytes 3145732
  6.3 1.0 copy-start.1
  11.1 10.8 %collective-permute-start.8 = (bf16[64,1024]{1,0:T(8,128)(2,1)S(1)}, bf16[64,1024]{1,0:T(8,128)(2,1)S(1)}, u32[]{:S(2)}, u32[]{:S(2)}) collective-permute-start(bf16[64,1024]{1,0:T(8,128)(2,1)S(1)} %get-tuple-element.29), channel_id=1, source_target_pairs={{2,0},{4,2},{6,4},{8,6},{10,8},{12,10},{14,12},{0,14},{3,1},{5,3},... | collective-permute-start | bytes 393224 | tf_op jit(solution)/shard_map/grad_ring/ppermute | solution.py:86
  13.4 20.3 %collective-permute-start.2 = (bf16[64,1024]{1,0:T(8,128)(2,1)S(1)}, bf16[64,1024]{1,0:T(8,128)(2,1)S(1)}, u32[]{:S(2)}, u32[]{:S(2)}) collective-permute-start(bf16[64,1024]{1,0:T(8,128)(2,1)S(1)} %get-tuple-element.26), channel_id=1, source_target_pairs={{0,2},{2,4},{4,6},{6,8},{8,10},{10,12},{12,14},{14,0},{1,3},{3,5},... | collective-permute-start | bytes 393224 | tf_op jit(solution)/shard_map/grad_ring/ppermute | solution.py:85
  18.5 31.7 %collective-permute-start.5 = (bf16[5,64,1024]{2,1,0:T(8,128)(2,1)S(1)}, bf16[5,64,1024]{2,1,0:T(8,128)(2,1)S(1)}, u32[]{:S(2)}, u32[]{:S(2)}) collective-permute-start(bf16[5,64,1024]{2,1,0:T(8,128)(2,1)S(1)} %get-tuple-element.18), channel_id=1, source_target_pairs={{0,16},{16,0},{1,17},{17,1},{2,18},{18,2},{3,19},{19,3},{4,20},{20... | collective-permute-start | bytes 1966088 | tf_op jit(solution)/shard_map/grad_ring/ppermute | solution.py:84
  22.0 17.2 %collective-permute-start.9 = (bf16[128,1024]{1,0:T(8,128)(2,1)S(1)}, bf16[128,1024]{1,0:T(8,128)(2,1)S(1)}, u32[]{:S(2)}, u32[]{:S(2)}) collective-permute-start(bf16[128,1024]{1,0:T(8,128)(2,1)S(1)} %pad_maximum_fusion.1), channel_id=1, source_target_pairs={{2,0},{4,2},{6,4},{8,6},{10,8},{12,10},{14,12},{0,14},{3,1},{5,3},... | collective-permute-start | bytes 786440 | tf_op jit(solution)/shard_map/grad_ring/ppermute | solution.py:90
  33.8 9.6 %collective-permute-start.3 = (bf16[128,1024]{1,0:T(8,128)(2,1)S(1)}, bf16[128,1024]{1,0:T(8,128)(2,1)S(1)}, u32[]{:S(2)}, u32[]{:S(2)}) collective-permute-start(bf16[128,1024]{1,0:T(8,128)(2,1)S(1)} %pad_maximum_fusion), channel_id=1, source_target_pairs={{0,2},{2,4},{4,6},{6,8},{8,10},{10,12},{12,14},{14,0},{1,3},{3,5},... | collective-permute-start | bytes 786440 | tf_op jit(solution)/shard_map/grad_ring/ppermute | solution.py:89
  39.1 30.6 %copy-start.2 = (f32[1,64,1024]{2,1,0:T(8,128)S(1)}, f32[1,64,1024]{2,1,0:T(8,128)}, u32[]{:S(2)}) copy-start(f32[1,64,1024]{2,1,0:T(8,128)} %param.11) | copy-start | bytes 786436
  39.2 30.6 %copy-start.3 = (f32[1,64,1024]{2,1,0:T(8,128)S(1)}, f32[1,64,1024]{2,1,0:T(8,128)}, u32[]{:S(2)}) copy-start(f32[1,64,1024]{2,1,0:T(8,128)} %param.10) | copy-start | bytes 786436
  39.2 30.6 %copy-start.4 = (f32[1,64,1024]{2,1,0:T(8,128)S(1)}, f32[1,64,1024]{2,1,0:T(8,128)}, u32[]{:S(2)}) copy-start(f32[1,64,1024]{2,1,0:T(8,128)} %param.9) | copy-start | bytes 786436
  39.2 7.8 %collective-permute-start.10 = (bf16[64,1024]{1,0:T(8,128)(2,1)S(1)}, bf16[64,1024]{1,0:T(8,128)(2,1)S(1)}, u32[]{:S(2)}, u32[]{:S(2)}) collective-permute-start(bf16[64,1024]{1,0:T(8,128)(2,1)S(1)} %slice.85), channel_id=1, source_target_pairs={{0,16},{16,0},{1,17},{17,1},{2,18},{18,2},{3,19},{19,3},{4,20},{20... | collective-permute-start | bytes 393224 | tf_op jit(solution)/shard_map/grad_ring/ppermute | solution.py:92
  43.3 6.9 %collective-permute-start.4 = (bf16[64,1024]{1,0:T(8,128)(2,1)S(1)}, bf16[64,1024]{1,0:T(8,128)(2,1)S(1)}, u32[]{:S(2)}, u32[]{:S(2)}) collective-permute-start(bf16[64,1024]{1,0:T(8,128)(2,1)S(1)} %slice.81), channel_id=1, source_target_pairs={{0,16},{16,0},{1,17},{17,1},{2,18},{18,2},{3,19},{19,3},{4,20},{20... | collective-permute-start | bytes 393224 | tf_op jit(solution)/shard_map/grad_ring/ppermute | solution.py:91
  50.4 8.3 %collective-permute-start.6 = (bf16[64,1024]{1,0:T(8,128)(2,1)S(1)}, bf16[64,1024]{1,0:T(8,128)(2,1)S(1)}, u32[]{:S(2)}, u32[]{:S(2)}) collective-permute-start(bf16[64,1024]{1,0:T(8,128)(2,1)S(1)} %get-tuple-element.24), channel_id=1, source_target_pairs={{0,2},{2,4},{4,6},{6,8},{8,10},{10,12},{12,14},{14,0},{1,3},{3,5},... | collective-permute-start | bytes 393224 | tf_op jit(solution)/shard_map/grad_ring/ppermute | solution.py:95
  52.6 7.6 %collective-permute-start.11 = (bf16[64,1024]{1,0:T(8,128)(2,1)S(1)}, bf16[64,1024]{1,0:T(8,128)(2,1)S(1)}, u32[]{:S(2)}, u32[]{:S(2)}) collective-permute-start(bf16[64,1024]{1,0:T(8,128)(2,1)S(1)} %get-tuple-element.25), channel_id=1, source_target_pairs={{2,0},{4,2},{6,4},{8,6},{10,8},{12,10},{14,12},{0,14},{3,1},{5,3},... | collective-permute-start | bytes 393224 | tf_op jit(solution)/shard_map/grad_ring/ppermute | solution.py:96
  60.3 7.3 %collective-permute-start.7 = (bf16[64,1024]{1,0:T(8,128)(2,1)S(1)}, bf16[64,1024]{1,0:T(8,128)(2,1)S(1)}, u32[]{:S(2)}, u32[]{:S(2)}) collective-permute-start(bf16[64,1024]{1,0:T(8,128)(2,1)S(1)} %get-tuple-element.22), channel_id=1, source_target_pairs={{0,2},{2,4},{4,6},{6,8},{8,10},{10,12},{12,14},{14,0},{1,3},{3,5},... | collective-permute-start | bytes 393224 | tf_op jit(solution)/shard_map/grad_ring/ppermute | solution.py:99
  62.7 38.5 %copy-start.5 = (f32[2,1024]{1,0:T(2,128)S(1)}, f32[2,1024]{1,0:T(2,128)}, u32[]{:S(2)}) copy-start(f32[2,1024]{1,0:T(2,128)} %param.12) | copy-start | bytes 24580
  62.7 38.5 %copy-start.6 = (f32[2,1024]{1,0:T(2,128)S(1)}, f32[2,1024]{1,0:T(2,128)}, u32[]{:S(2)}) copy-start(f32[2,1024]{1,0:T(2,128)} %param.13) | copy-start | bytes 24580
  62.7 7.0 %collective-permute-start.12 = (bf16[64,1024]{1,0:T(8,128)(2,1)S(1)}, bf16[64,1024]{1,0:T(8,128)(2,1)S(1)}, u32[]{:S(2)}, u32[]{:S(2)}) collective-permute-start(bf16[64,1024]{1,0:T(8,128)(2,1)S(1)} %get-tuple-element.23), channel_id=1, source_target_pairs={{2,0},{4,2},{6,4},{8,6},{10,8},{12,10},{14,12},{0,14},{3,1},{5,3},... | collective-permute-start | bytes 393224 | tf_op jit(solution)/shard_map/grad_ring/ppermute | solution.py:100

commit v5 on v1

v5 whole, which is shorter than its diff:
```python
import jax
import jax.numpy as jnp
from jax import lax
from jax.experimental import pallas as pl
from jax.experimental.pallas import tpu as pltpu
from jax.sharding import Mesh, PartitionSpec as P

INNER_STEP = 500
AXES = ("xh", "z", "xl", "y", "core")
SIZES = (4, 8, 2, 8, 2)
REP = ("xh", "z")
FSDP = ("xl", "y", "core")
RING = 8


def product_kernel(steps, pairs, place, *refs):
    xl, y, core = place[0], place[1], place[2]
    before, outs = refs[2 * pairs : -len(steps)], refs[-len(steps) :]
    lane = lax.broadcasted_iota(jnp.int32, (1, 128), 1)

    for i, step in enumerate(steps):
        to_core = core if step % 2 else 1 - core
        ahead = RING - 1 - step
        target = lax.rem(y + jnp.where(to_core == 1, ahead, RING - ahead), RING)
        own_side = (lane < 64) == (to_core == 0)

        def columns(ref):
            def block(side):
                start = pl.multiple_of((side * RING + target) * 128, 128)
                return ref[:, pl.ds(start, 128)].astype(jnp.float32)

            near, far = block(xl), block(1 - xl)
            still = jnp.where(to_core == 0, near, far)
            moved = pltpu.roll(jnp.where(to_core == 0, far, near), 64, 1)
            return jnp.where(own_side, still, moved).astype(jnp.bfloat16)

        def times(lhs, rhs):
            return lax.dot_general(lhs, rhs, (((0,), (0,)), ((), ())), preferred_element_type=jnp.float32)

        total = sum(times(columns(refs[2 * k]), refs[2 * k + 1][...]) for k in range(pairs))
        if before:
            total = total + before[i][...]
        outs[i][...] = total.astype(outs[i].dtype)


def product(steps, dtype, place, pairs, before=()):
    vmem = pl.BlockSpec(memory_space=pltpu.VMEM)
    operands = [x for pair in pairs for x in pair] + list(before)
    tokens, cols = pairs[0][1].shape
    return pl.pallas_call(
        lambda *refs: product_kernel(steps, len(pairs), *refs),
        out_shape=[jax.ShapeDtypeStruct((128, cols), dtype) for _ in steps],
        in_specs=[pl.BlockSpec(memory_space=pltpu.SMEM)] + [vmem] * len(operands),
        out_specs=[vmem for _ in steps],
        compiler_params=pltpu.CompilerParams(vmem_limit_bytes=24 * 1024 * 1024),
        cost_estimate=pl.CostEstimate(
            flops=2 * 128 * len(steps) * len(pairs) * tokens * cols,
            bytes_accessed=2 * len(pairs) * tokens * (pairs[0][0].shape[1] + cols),
            transcendentals=0,
        ),
    )(place, *operands)


def add(*terms):
    return sum(t.astype(jnp.float32) for t in terms)


def shards(acts, grad_out, inner_weight, first_moment, second_moment, outer_weight, outer_momentum):
    replicas = lax.axis_size(REP)
    rows, cols = inner_weight.shape[1:]
    own = rows // replicas
    bf16 = jnp.bfloat16
    place = jnp.stack([lax.axis_index(a) for a in FSDP])

    swap = [(0, 1), (1, 0)]
    with jax.named_scope("core_swap"):
        acts_peer = lax.ppermute(acts[0], "core", swap)
        cot_peer = lax.ppermute(grad_out[0], "core", swap)
    with jax.named_scope("grad_product"):
        here, peer = (acts[0], grad_out[0]), (acts_peer, cot_peer)
        first_here = product((0,), jnp.float32, place, [here])
        blocks = product((0,), bf16, place, [peer], first_here)
        blocks = [*blocks, *product((1, 2), bf16, place, [here, peer])]
        blocks = [*blocks, *product((3, 4, 5, 6, 7), bf16, place, [here, peer])]
    with jax.named_scope("grad_ring"):
        links = []
        for core in range(2):
            ends = [(2 * y + core, 2 * ((y + 1) % RING) + 1 - core) for y in range(RING)]
            links.append(ends + [(b, a) for a, b in ends])
        running = blocks[0]
        for step in range(1, RING - 1):
            running = add(blocks[step], lax.ppermute(running, ("y", "core"), links[(step - 1) % 2])).astype(bf16)
        running = lax.ppermute(running, ("y", "core"), links[(RING - 2) % 2])
    with jax.named_scope("grad_pair"):
        other = add(blocks[-1][rows:], running[rows:]).astype(bf16)
        other = lax.ppermute(other, "xl", swap)
        grad = add(blocks[-1][:rows], running[:rows], other)

    with jax.named_scope("adamw"):
        first = 0.9 * first_moment[0] + 0.1 * grad
        second = 0.95 * second_moment[0] + 0.05 * grad * grad
        first_hat = first / (1.0 - 0.9**INNER_STEP)
        second_hat = second / (1.0 - 0.95**INNER_STEP)
        inner_new = inner_weight[0] * (1.0 - 0.0004 * 0.1) - 0.0004 * first_hat / (
            jnp.sqrt(second_hat) + 1e-08
        )
        inner_new = lax.optimization_barrier(inner_new)
    with jax.named_scope("replica_sum"):
        pieces = lax.all_to_all(inner_new.reshape(replicas, own, cols), REP, 0, 0, tiled=True)
        summed = jnp.sum(pieces, axis=0)
    with jax.named_scope("outer_step"):
        pseudo = outer_weight - summed / replicas
        momentum_next = 0.9 * outer_momentum + pseudo
        outer_next = outer_weight - 0.7 * (pseudo + 0.9 * momentum_next)
    with jax.named_scope("row_gather"):
        new = outer_next.astype(bf16).reshape(1, own * cols // 128, 128)
        copies = jnp.broadcast_to(new, (replicas,) + new.shape[1:])
        weight_next = lax.all_to_all(copies, REP, 0, 0, tiled=True).reshape(rows, cols)
    return (outer_next, momentum_next, weight_next)


def solution(mesh, sizes=SIZES):
    grid = Mesh(mesh.devices.reshape(sizes), AXES)
    split = P(REP, FSDP, None)
    outer = P(FSDP + REP, None)
    return jax.shard_map(
        shards,
        mesh=grid,
        in_specs=(split, split, split, split, split, outer, outer),
        out_specs=(outer, outer, P(FSDP, None)),
        check_vma=False,
    )
```

time: 130 us -> 133 us (1.023)
  the two profiles are of different devices: /device:TPU:16 before, /device:TPU:1 now
where the time goes in v5:
time: 133 us; the launch traced here: 132 us
  waiting for transfers between devices  46.7 us (35%)
  blocking collectives  40.8 us (31%)
  starting transfers between devices  33.5 us (25%)
  Pallas kernels  5.18 us (4%)
  local copies, waits for them, and re-layouts  3.8 us (3%)
  other arithmetic  1.45 us (1%)
    ppermute x6, waiting for transfers between devices, shards(): lax.ppermute(running, ('y', 'core'), links[(step - 1) % 2])  34.9 us
    all_to_all x1, blocking collectives, shards(): lax.all_to_all(inner_new.reshape(replicas, own, cols), REP, 0, 0, tiled=T...  23.1 us
    all_to_all x1, blocking collectives, shards(): lax.all_to_all(copies, REP, 0, 0, tiled=True).reshape(rows, cols)  17.8 us
    ppermute x1, starting transfers between devices, shards(): acts_peer = lax.ppermute(acts[0], 'core', swap)  16.1 us
    ppermute x6, starting transfers between devices, shards(): lax.ppermute(running, ('y', 'core'), links[(step - 1) % 2])  11.5 us
    ppermute x1, waiting for transfers between devices, shards(): running = lax.ppermute(running, ('y', 'core'), links[(RING - 2) % 2])  6.97 us
    pallas_call x4, Pallas kernels, product(): pl.pallas_call(lambda *refs: product_kernel(steps, len(pairs), *refs), ou...  5.18 us
    ppermute x1, waiting for transfers between devices, shards(): other = lax.ppermute(other, 'xl', swap)  4.86 us
  transfers between devices with their start and end apart: 10, of which 8 were waited for; matrix products, arithmetic and copies ran while one was open for 0% of the time, Pallas kernels for 3%

profile of v5, /device:TPU:1, one launch (start us, length us, event | category | flops | bytes accessed | tf_op | source)
XLA Modules:
  0.0 132.3 jit_solution(10509926148233002387)
XLA Ops:
  0.6 16.1 %collective-permute-start = (bf16[256,2048]{1,0:T(8,128)(2,1)}, bf16[256,2048]{1,0:T(8,128)(2,1)S(1)}, u32[]{:S(2)}, u32[]{:S(2)}) collective-permute-start(bf16[256,2048]{1,0:T(8,128)(2,1)} %bitcast.15), channel_id=1, source_target_pairs={{0,1},{1,0},{2,3},{3,2},{4,5},{5,4},{6,7},{7,6},{8,9},{9,8},{10,11... | collective-permute-start | bytes 3145736 | tf_op jit(solution)/shard_map/core_swap/ppermute | solution.py:77
  16.7 1.9 %collective-permute-start.1 = (bf16[256,1024]{1,0:T(8,128)(2,1)}, bf16[256,1024]{1,0:T(8,128)(2,1)S(1)}, u32[]{:S(2)}, u32[]{:S(2)}) collective-permute-start(bf16[256,1024]{1,0:T(8,128)(2,1)} %bitcast.19), channel_id=1, source_target_pairs={{0,1},{1,0},{2,3},{3,2},{4,5},{5,4},{6,7},{7,6},{8,9},{9,8},{10,11... | collective-permute-start | bytes 1572872 | tf_op jit(solution)/shard_map/core_swap/ppermute | solution.py:78
  18.7 1.2 copy-done
  19.9 1.0 copy-done.2
  21.0 0.9 grad_product.6.refs_3_
  21.9 0.9 grad_product.7
  22.8 1.9 %collective-permute-start.2 = (bf16[128,1024]{1,0:T(8,128)(2,1)S(1)}, bf16[128,1024]{1,0:T(8,128)(2,1)S(1)}, u32[]{:S(2)}, u32[]{:S(2)}) collective-permute-start(bf16[128,1024]{1,0:T(8,128)(2,1)S(1)} %grad_product.7), channel_id=1, source_target_pairs={{0,3},{2,5},{4,7},{6,9},{8,11},{10,13},{12,15},{14,1},{3,0},{5,2},... | collective-permute-start | bytes 786440 | tf_op jit(solution)/shard_map/grad_ring/ppermute | solution.py:92
  24.7 1.3 grad_product.5
  26.1 5.7 %collective-permute-done.2 = bf16[128,1024]{1,0:T(8,128)(2,1)S(1)} collective-permute-done((bf16[128,1024]{1,0:T(8,128)(2,1)S(1)}, bf16[128,1024]{1,0:T(8,128)(2,1)S(1)}, u32[]{:S(2)}, u32[]{:S(2)}) %collective-permute-start.2) | collective-permute-done | bytes 262176 | tf_op jit(solution)/shard_map/grad_ring/ppermute | solution.py:92
  31.8 1.9 %collective-permute-start.3 = (bf16[128,1024]{1,0:T(8,128)(2,1)S(1)}, bf16[128,1024]{1,0:T(8,128)(2,1)S(1)}, u32[]{:S(2)}, u32[]{:S(2)}) collective-permute-start(bf16[128,1024]{1,0:T(8,128)(2,1)S(1)} %add_convert_fusion.5), channel_id=1, source_target_pairs={{1,2},{3,4},{5,6},{7,8},{9,10},{11,12},{13,14},{15,0},{2,1},{4,3},... | collective-permute-start | bytes 786440 | tf_op jit(solution)/shard_map/grad_ring/ppermute | solution.py:92
  33.7 5.9 %collective-permute-done.3 = bf16[128,1024]{1,0:T(8,128)(2,1)S(1)} collective-permute-done((bf16[128,1024]{1,0:T(8,128)(2,1)S(1)}, bf16[128,1024]{1,0:T(8,128)(2,1)S(1)}, u32[]{:S(2)}, u32[]{:S(2)}) %collective-permute-start.3) | collective-permute-done | bytes 262176 | tf_op jit(solution)/shard_map/grad_ring/ppermute | solution.py:92
  39.6 1.9 %collective-permute-start.4 = (bf16[128,1024]{1,0:T(8,128)(2,1)S(1)}, bf16[128,1024]{1,0:T(8,128)(2,1)S(1)}, u32[]{:S(2)}, u32[]{:S(2)}) collective-permute-start(bf16[128,1024]{1,0:T(8,128)(2,1)S(1)} %add_convert_fusion.4), channel_id=1, source_target_pairs={{0,3},{2,5},{4,7},{6,9},{8,11},{10,13},{12,15},{14,1},{3,0},{5,2},... | collective-permute-start | bytes 786440 | tf_op jit(solution)/shard_map/grad_ring/ppermute | solution.py:92
  41.6 2.1 %grad_product.4 = (bf16[128,1024]{1,0:T(8,128)(2,1)S(1)}, bf16[128,1024]{1,0:T(8,128)(2,1)S(1)}, bf16[128,1024]{1,0:T(8,128)(2,1)S(1)}, bf16[128,1024]{1,0:T(8,128)(2,1)S(1)}, bf16[128,1024]{1,0:T(8,128)(2,1)S(1)}) custom-call(s32[3]{0:T(128)S(1)} %pad_add_fusion.refs_0_, bf16[256,2048]{1,0:T(8,128)(2,1)S(1)} %bitcast.18, bf16[256,1024]{1,0:T(8,128)(2,1)S(1)} %bitcast.22, ...), custom_call_target="tpu_custom_call" | custom-call | flops 671088640 | bytes 3145728 | tf_op jit(solution)/shard_map/grad_product/pallas_call | solution.py:50
  43.7 4.9 %collective-permute-done.4 = bf16[128,1024]{1,0:T(8,128)(2,1)S(1)} collective-permute-done((bf16[128,1024]{1,0:T(8,128)(2,1)S(1)}, bf16[128,1024]{1,0:T(8,128)(2,1)S(1)}, u32[]{:S(2)}, u32[]{:S(2)}) %collective-permute-start.4) | collective-permute-done | bytes 262176 | tf_op jit(solution)/shard_map/grad_ring/ppermute | solution.py:92
  48.6 1.9 %collective-permute-start.5 = (bf16[128,1024]{1,0:T(8,128)(2,1)S(1)}, bf16[128,1024]{1,0:T(8,128)(2,1)S(1)}, u32[]{:S(2)}, u32[]{:S(2)}) collective-permute-start(bf16[128,1024]{1,0:T(8,128)(2,1)S(1)} %add_convert_fusion.3), channel_id=1, source_target_pairs={{1,2},{3,4},{5,6},{7,8},{9,10},{11,12},{13,14},{15,0},{2,1},{4,3},... | collective-permute-start | bytes 786440 | tf_op jit(solution)/shard_map/grad_ring/ppermute | solution.py:92
  50.5 5.8 %collective-permute-done.5 = bf16[128,1024]{1,0:T(8,128)(2,1)S(1)} collective-permute-done((bf16[128,1024]{1,0:T(8,128)(2,1)S(1)}, bf16[128,1024]{1,0:T(8,128)(2,1)S(1)}, u32[]{:S(2)}, u32[]{:S(2)}) %collective-permute-start.5) | collective-permute-done | bytes 262176 | tf_op jit(solution)/shard_map/grad_ring/ppermute | solution.py:92
  56.4 1.9 %collective-permute-start.6 = (bf16[128,1024]{1,0:T(8,128)(2,1)S(1)}, bf16[128,1024]{1,0:T(8,128)(2,1)S(1)}, u32[]{:S(2)}, u32[]{:S(2)}) collective-permute-start(bf16[128,1024]{1,0:T(8,128)(2,1)S(1)} %add_convert_fusion.2), channel_id=1, source_target_pairs={{0,3},{2,5},{4,7},{6,9},{8,11},{10,13},{12,15},{14,1},{3,0},{5,2},... | collective-permute-start | bytes 786440 | tf_op jit(solution)/shard_map/grad_ring/ppermute | solution.py:92
  58.3 7.0 %collective-permute-done.6 = bf16[128,1024]{1,0:T(8,128)(2,1)S(1)} collective-permute-done((bf16[128,1024]{1,0:T(8,128)(2,1)S(1)}, bf16[128,1024]{1,0:T(8,128)(2,1)S(1)}, u32[]{:S(2)}, u32[]{:S(2)}) %collective-permute-start.6) | collective-permute-done | bytes 262176 | tf_op jit(solution)/shard_map/grad_ring/ppermute | solution.py:92
  65.4 1.9 %collective-permute-start.7 = (bf16[128,1024]{1,0:T(8,128)(2,1)S(1)}, bf16[128,1024]{1,0:T(8,128)(2,1)S(1)}, u32[]{:S(2)}, u32[]{:S(2)}) collective-permute-start(bf16[128,1024]{1,0:T(8,128)(2,1)S(1)} %add_convert_fusion.1), channel_id=1, source_target_pairs={{1,2},{3,4},{5,6},{7,8},{9,10},{11,12},{13,14},{15,0},{2,1},{4,3},... | collective-permute-start | bytes 786440 | tf_op jit(solution)/shard_map/grad_ring/ppermute | solution.py:92
  67.3 5.8 %collective-permute-done.7 = bf16[128,1024]{1,0:T(8,128)(2,1)S(1)} collective-permute-done((bf16[128,1024]{1,0:T(8,128)(2,1)S(1)}, bf16[128,1024]{1,0:T(8,128)(2,1)S(1)}, u32[]{:S(2)}, u32[]{:S(2)}) %collective-permute-start.7) | collective-permute-done | bytes 262176 | tf_op jit(solution)/shard_map/grad_ring/ppermute | solution.py:92
  73.1 2.1 %collective-permute-start.8 = (bf16[128,1024]{1,0:T(8,128)(2,1)S(1)}, bf16[128,1024]{1,0:T(8,128)(2,1)S(1)}, u32[]{:S(2)}, u32[]{:S(2)}) collective-permute-start(bf16[128,1024]{1,0:T(8,128)(2,1)S(1)} %add_convert_fusion), channel_id=1, source_target_pairs={{0,3},{2,5},{4,7},{6,9},{8,11},{10,13},{12,15},{14,1},{3,0},{5,2},... | collective-permute-start | bytes 786440 | tf_op jit(solution)/shard_map/grad_ring/ppermute | solution.py:93
  75.2 7.0 %collective-permute-done.8 = bf16[128,1024]{1,0:T(8,128)(2,1)S(1)} collective-permute-done((bf16[128,1024]{1,0:T(8,128)(2,1)S(1)}, bf16[128,1024]{1,0:T(8,128)(2,1)S(1)}, u32[]{:S(2)}, u32[]{:S(2)}) %collective-permute-start.8) | collective-permute-done | bytes 262176 | tf_op jit(solution)/shard_map/grad_ring/ppermute | solution.py:93
  82.2 1.9 %collective-permute-start.9 = (bf16[64,1024]{1,0:T(8,128)(2,1)S(1)}, bf16[64,1024]{1,0:T(8,128)(2,1)S(1)}, u32[]{:S(2)}, u32[]{:S(2)}) collective-permute-start(bf16[64,1024]{1,0:T(8,128)(2,1)S(1)} %add_convert_fusion.6), channel_id=1, source_target_pairs={{0,16},{16,0},{1,17},{17,1},{2,18},{18,2},{3,19},{19,3},{4,20},{20... | collective-permute-start | bytes 393224 | tf_op jit(solution)/shard_map/grad_pair/ppermute | solution.py:96
  84.1 4.9 %collective-permute-done.9 = bf16[64,1024]{1,0:T(8,128)(2,1)S(1)} collective-permute-done((bf16[64,1024]{1,0:T(8,128)(2,1)S(1)}, bf16[64,1024]{1,0:T(8,128)(2,1)S(1)}, u32[]{:S(2)}, u32[]{:S(2)}) %collective-permute-start.9) | collective-permute-done | bytes 131104 | tf_op jit(solution)/shard_map/grad_pair/ppermute | solution.py:96
  89.0 0.2 fusion.4
  89.2 0.1 reshape.20
  89.4 23.1 %all_to_all.10 = f32[32,2,1024]{2,1,0:T(2,128)S(1)} all-to-all(f32[32,2,1024]{2,1,0:T(2,128)S(1)} %reshape.20), channel_id=1, replica_groups=mesh['xh'=4,'z'=8,'xl'=2,'y'=8,'core'=2] {'xh','z'}, dimensions={0} | all-to-all | bytes 524288 | tf_op jit(solution)/shard_map/replica_sum/all_to_all | solution.py:109
  112.5 0.1 reduce_sum.9
  112.6 0.6 copy-done.6
  113.2 0.6 fusion.6
  113.8 17.8 %all_to_all.11 = bf16[32,16,128]{2,1,0:T(8,128)(2,1)S(1)} all-to-all(bf16[32,16,128]{2,1,0:T(8,128)(2,1)S(1)} %broadcast_in_dim.8), channel_id=1, replica_groups=mesh['xh'=4,'z'=8,'xl'=2,'y'=8,'core'=2] {'xh','z'}, dimensions={0} | all-to-all | bytes 262144 | tf_op jit(solution)/shard_map/row_gather/all_to_all | solution.py:118
  131.6 0.7 reshape.21
  (25 shorter events, 0.6 us)
Async XLA Ops:
  0.6 21.3 %collective-permute-start = (bf16[256,2048]{1,0:T(8,128)(2,1)}, bf16[256,2048]{1,0:T(8,128)(2,1)S(1)}, u32[]{:S(2)}, u32[]{:S(2)}) collective-permute-start(bf16[256,2048]{1,0:T(8,128)(2,1)} %bitcast.15), channel_id=1, source_target_pairs={{0,1},{1,0},{2,3},{3,2},{4,5},{5,4},{6,7},{7,6},{8,9},{9,8},{10,11... | collective-permute-start | bytes 3145736 | tf_op jit(solution)/shard_map/core_swap/ppermute | solution.py:77
  16.7 5.2 %collective-permute-start.1 = (bf16[256,1024]{1,0:T(8,128)(2,1)}, bf16[256,1024]{1,0:T(8,128)(2,1)S(1)}, u32[]{:S(2)}, u32[]{:S(2)}) collective-permute-start(bf16[256,1024]{1,0:T(8,128)(2,1)} %bitcast.19), channel_id=1, source_target_pairs={{0,1},{1,0},{2,3},{3,2},{4,5},{5,4},{6,7},{7,6},{8,9},{9,8},{10,11... | collective-permute-start | bytes 1572872 | tf_op jit(solution)/shard_map/core_swap/ppermute | solution.py:78
  18.7 1.2 copy-start
  19.9 1.0 copy-start.2
  21.9 2.9 %copy-start.1 = (bf16[1,256,2048]{2,1,0:T(8,128)(2,1)S(1)}, bf16[1,256,2048]{2,1,0:T(8,128)(2,1)}, u32[]{:S(2)}) copy-start(bf16[1,256,2048]{2,1,0:T(8,128)(2,1)} %param.7) | copy-start | bytes 3145732
  22.8 8.9 %collective-permute-start.2 = (bf16[128,1024]{1,0:T(8,128)(2,1)S(1)}, bf16[128,1024]{1,0:T(8,128)(2,1)S(1)}, u32[]{:S(2)}, u32[]{:S(2)}) collective-permute-start(bf16[128,1024]{1,0:T(8,128)(2,1)S(1)} %grad_product.7), channel_id=1, source_target_pairs={{0,3},{2,5},{4,7},{6,9},{8,11},{10,13},{12,15},{14,1},{3,0},{5,2},... | collective-permute-start | bytes 786440 | tf_op jit(solution)/shard_map/grad_ring/ppermute | solution.py:92
  31.8 7.8 %collective-permute-start.3 = (bf16[128,1024]{1,0:T(8,128)(2,1)S(1)}, bf16[128,1024]{1,0:T(8,128)(2,1)S(1)}, u32[]{:S(2)}, u32[]{:S(2)}) collective-permute-start(bf16[128,1024]{1,0:T(8,128)(2,1)S(1)} %add_convert_fusion.5), channel_id=1, source_target_pairs={{1,2},{3,4},{5,6},{7,8},{9,10},{11,12},{13,14},{15,0},{2,1},{4,3},... | collective-permute-start | bytes 786440 | tf_op jit(solution)/shard_map/grad_ring/ppermute | solution.py:92
  39.6 8.9 %collective-permute-start.4 = (bf16[128,1024]{1,0:T(8,128)(2,1)S(1)}, bf16[128,1024]{1,0:T(8,128)(2,1)S(1)}, u32[]{:S(2)}, u32[]{:S(2)}) collective-permute-start(bf16[128,1024]{1,0:T(8,128)(2,1)S(1)} %add_convert_fusion.4), channel_id=1, source_target_pairs={{0,3},{2,5},{4,7},{6,9},{8,11},{10,13},{12,15},{14,1},{3,0},{5,2},... | collective-permute-start | bytes 786440 | tf_op jit(solution)/shard_map/grad_ring/ppermute | solution.py:92
  48.6 7.7 %collective-permute-start.5 = (bf16[128,1024]{1,0:T(8,128)(2,1)S(1)}, bf16[128,1024]{1,0:T(8,128)(2,1)S(1)}, u32[]{:S(2)}, u32[]{:S(2)}) collective-permute-start(bf16[128,1024]{1,0:T(8,128)(2,1)S(1)} %add_convert_fusion.3), channel_id=1, source_target_pairs={{1,2},{3,4},{5,6},{7,8},{9,10},{11,12},{13,14},{15,0},{2,1},{4,3},... | collective-permute-start | bytes 786440 | tf_op jit(solution)/shard_map/grad_ring/ppermute | solution.py:92
  56.4 8.9 %collective-permute-start.6 = (bf16[128,1024]{1,0:T(8,128)(2,1)S(1)}, bf16[128,1024]{1,0:T(8,128)(2,1)S(1)}, u32[]{:S(2)}, u32[]{:S(2)}) collective-permute-start(bf16[128,1024]{1,0:T(8,128)(2,1)S(1)} %add_convert_fusion.2), channel_id=1, source_target_pairs={{0,3},{2,5},{4,7},{6,9},{8,11},{10,13},{12,15},{14,1},{3,0},{5,2},... | collective-permute-start | bytes 786440 | tf_op jit(solution)/shard_map/grad_ring/ppermute | solution.py:92
  65.4 7.7 %collective-permute-start.7 = (bf16[128,1024]{1,0:T(8,128)(2,1)S(1)}, bf16[128,1024]{1,0:T(8,128)(2,1)S(1)}, u32[]{:S(2)}, u32[]{:S(2)}) collective-permute-start(bf16[128,1024]{1,0:T(8,128)(2,1)S(1)} %add_convert_fusion.1), channel_id=1, source_target_pairs={{1,2},{3,4},{5,6},{7,8},{9,10},{11,12},{13,14},{15,0},{2,1},{4,3},... | collective-permute-start | bytes 786440 | tf_op jit(solution)/shard_map/grad_ring/ppermute | solution.py:92
  73.0 16.0 %copy-start.4 = (f32[1,64,1024]{2,1,0:T(8,128)S(1)}, f32[1,64,1024]{2,1,0:T(8,128)}, u32[]{:S(2)}) copy-start(f32[1,64,1024]{2,1,0:T(8,128)} %param.10) | copy-start | bytes 786436
  73.0 16.0 %copy-start.5 = (f32[1,64,1024]{2,1,0:T(8,128)S(1)}, f32[1,64,1024]{2,1,0:T(8,128)}, u32[]{:S(2)}) copy-start(f32[1,64,1024]{2,1,0:T(8,128)} %param.9) | copy-start | bytes 786436
  73.1 15.9 %copy-start.3 = (f32[1,64,1024]{2,1,0:T(8,128)S(1)}, f32[1,64,1024]{2,1,0:T(8,128)}, u32[]{:S(2)}) copy-start(f32[1,64,1024]{2,1,0:T(8,128)} %param.11) | copy-start | bytes 786436
  73.1 9.0 %collective-permute-start.8 = (bf16[128,1024]{1,0:T(8,128)(2,1)S(1)}, bf16[128,1024]{1,0:T(8,128)(2,1)S(1)}, u32[]{:S(2)}, u32[]{:S(2)}) collective-permute-start(bf16[128,1024]{1,0:T(8,128)(2,1)S(1)} %add_convert_fusion), channel_id=1, source_target_pairs={{0,3},{2,5},{4,7},{6,9},{8,11},{10,13},{12,15},{14,1},{3,0},{5,2},... | collective-permute-start | bytes 786440 | tf_op jit(solution)/shard_map/grad_ring/ppermute | solution.py:93
  82.2 6.8 %collective-permute-start.9 = (bf16[64,1024]{1,0:T(8,128)(2,1)S(1)}, bf16[64,1024]{1,0:T(8,128)(2,1)S(1)}, u32[]{:S(2)}, u32[]{:S(2)}) collective-permute-start(bf16[64,1024]{1,0:T(8,128)(2,1)S(1)} %add_convert_fusion.6), channel_id=1, source_target_pairs={{0,16},{16,0},{1,17},{17,1},{2,18},{18,2},{3,19},{19,3},{4,20},{20... | collective-permute-start | bytes 393224 | tf_op jit(solution)/shard_map/grad_pair/ppermute | solution.py:96
  112.5 0.7 copy-start.6
  112.5 0.7 copy-start.7

commit v6 on v5

--- a/solution.py
+++ b/solution.py
@@ -13,16 +13,14 @@
 RING = 8
 
 
-def product_kernel(steps, pairs, place, *refs):
+def product_kernel(offsets, pairs, place, *refs):
     xl, y, core = place[0], place[1], place[2]
-    before, outs = refs[2 * pairs : -len(steps)], refs[-len(steps) :]
+    before, outs = refs[2 * pairs : -len(offsets)], refs[-len(offsets) :]
     lane = lax.broadcasted_iota(jnp.int32, (1, 128), 1)
 
-    for i, step in enumerate(steps):
-        to_core = core if step % 2 else 1 - core
-        ahead = RING - 1 - step
-        target = lax.rem(y + jnp.where(to_core == 1, ahead, RING - ahead), RING)
-        own_side = (lane < 64) == (to_core == 0)
+    own_side = (lane < 64) == (core == 0)
+    for i, offset in enumerate(offsets):
+        target = lax.rem(y + RING + jnp.where(core == 0, offset, -offset), RING)
 
         def columns(ref):
             def block(side):
@@ -30,8 +28,8 @@
                 return ref[:, pl.ds(start, 128)].astype(jnp.float32)
 
             near, far = block(xl), block(1 - xl)
-            still = jnp.where(to_core == 0, near, far)
-            moved = pltpu.roll(jnp.where(to_core == 0, far, near), 64, 1)
+            still = jnp.where(core == 0, near, far)
+            moved = pltpu.roll(jnp.where(core == 0, far, near), 64, 1)
             return jnp.where(own_side, still, moved).astype(jnp.bfloat16)
 
         def times(lhs, rhs):
@@ -43,18 +41,18 @@
         outs[i][...] = total.astype(outs[i].dtype)
 
 
-def product(steps, dtype, place, pairs, before=()):
+def product(offsets, dtype, place, pairs, before=()):
     vmem = pl.BlockSpec(memory_space=pltpu.VMEM)
     operands = [x for pair in pairs for x in pair] + list(before)
     tokens, cols = pairs[0][1].shape
     return pl.pallas_call(
-        lambda *refs: product_kernel(steps, len(pairs), *refs),
-        out_shape=[jax.ShapeDtypeStruct((128, cols), dtype) for _ in steps],
+        lambda *refs: product_kernel(offsets, len(pairs), *refs),
+        out_shape=[jax.ShapeDtypeStruct((128, cols), dtype) for _ in offsets],
         in_specs=[pl.BlockSpec(memory_space=pltpu.SMEM)] + [vmem] * len(operands),
-        out_specs=[vmem for _ in steps],
+        out_specs=[vmem for _ in offsets],
         compiler_params=pltpu.CompilerParams(vmem_limit_bytes=24 * 1024 * 1024),
         cost_estimate=pl.CostEstimate(
-            flops=2 * 128 * len(steps) * len(pairs) * tokens * cols,
+            flops=2 * 128 * len(offsets) * len(pairs) * tokens * cols,
             bytes_accessed=2 * len(pairs) * tokens * (pairs[0][0].shape[1] + cols),
             transcendentals=0,
         ),
@@ -78,23 +76,22 @@
         cot_peer = lax.ppermute(grad_out[0], "core", swap)
     with jax.named_scope("grad_product"):
         here, peer = (acts[0], grad_out[0]), (acts_peer, cot_peer)
-        first_here = product((0,), jnp.float32, place, [here])
-        blocks = product((0,), bf16, place, [peer], first_here)
-        blocks = [*blocks, *product((1, 2), bf16, place, [here, peer])]
-        blocks = [*blocks, *product((3, 4, 5, 6, 7), bf16, place, [here, peer])]
+        early = product((-3, 4, 3), bf16, place, [peer], product((-3, 4, 3), jnp.float32, place, [here]))
+        late = product((-2, 2, 1, -1, 0), bf16, place, [here, peer])
     with jax.named_scope("grad_ring"):
-        links = []
-        for core in range(2):
-            ends = [(2 * y + core, 2 * ((y + 1) % RING) + 1 - core) for y in range(RING)]
-            links.append(ends + [(b, a) for a, b in ends])
-        running = blocks[0]
-        for step in range(1, RING - 1):
-            running = add(blocks[step], lax.ppermute(running, ("y", "core"), links[(step - 1) % 2])).astype(bf16)
-        running = lax.ppermute(running, ("y", "core"), links[(RING - 2) % 2])
+
+        def hop(block, k):
+            ends = [(2 * y, 2 * ((y + k) % RING)) for y in range(RING)]
+            ends += [(2 * y + 1, 2 * ((y - k) % RING) + 1) for y in range(RING)]
+            return lax.ppermute(block, ("y", "core"), ends)
+
+        back_3, four, ahead_3 = hop(early[0], -1), hop(early[1], 2), hop(early[2], 1)
+        back_2 = hop(add(late[0], back_3).astype(bf16), -2)
+        ahead_2 = hop(add(late[1], four, ahead_3).astype(bf16), 2)
+        terms = (late[4], back_2, ahead_2, hop(late[2], 1), hop(late[3], -1))
     with jax.named_scope("grad_pair"):
-        other = add(blocks[-1][rows:], running[rows:]).astype(bf16)
-        other = lax.ppermute(other, "xl", swap)
-        grad = add(blocks[-1][:rows], running[:rows], other)
+        other = lax.ppermute(add(*(t[rows:] for t in terms)).astype(bf16), "xl", swap)
+        grad = add(other, *(t[:rows] for t in terms))
 
     with jax.named_scope("adamw"):
         first = 0.9 * first_moment[0] + 0.1 * grad

time: 133 us -> 112 us (0.84)
  the two profiles are of different devices: /device:TPU:1 before, /device:TPU:32 now
where the time goes in v6:
time: 112 us; the launch traced here: 111 us
  blocking collectives  46.8 us (42%)
  starting transfers between devices  37.8 us (34%)
  waiting for transfers between devices  16.1 us (14%)
  Pallas kernels  4.4 us (4%)
  local copies, waits for them, and re-layouts  3.8 us (3%)
  other arithmetic  1.35 us (1%)
    ppermute x7, starting transfers between devices, hop(): return lax.ppermute(block, ('y', 'core'), ends)  31.4 us
    all_to_all x1, blocking collectives, shards(): lax.all_to_all(inner_new.reshape(replicas, own, cols), REP, 0, 0, tiled=T...  29.8 us
    all_to_all x1, blocking collectives, shards(): lax.all_to_all(copies, REP, 0, 0, tiled=True).reshape(rows, cols)  17 us
    ppermute x7, waiting for transfers between devices, hop(): return lax.ppermute(block, ('y', 'core'), ends)  9.96 us
    ppermute x1, waiting for transfers between devices, shards(): lax.ppermute(add(*(t[rows:] for t in terms)).astype(bf16), 'xl', swap)  6.15 us
    pallas_call x3, Pallas kernels, product(): pl.pallas_call(lambda *refs: product_kernel(offsets, len(pairs), *refs),...  4.4 us
    unnamed x18, local copies, waits for them, and re-layouts  2.91 us
    ppermute x1, starting transfers between devices, shards(): cot_peer = lax.ppermute(grad_out[0], 'core', swap)  2.41 us
  transfers between devices with their start and end apart: 10, of which 3 were waited for; matrix products, arithmetic and copies ran while one was open for 0% of the time, Pallas kernels for 3%

profile of v6, /device:TPU:32, one launch (start us, length us, event | category | flops | bytes accessed | tf_op | source)
XLA Modules:
  0.0 111.1 jit_solution(5131452009039544758)
XLA Ops:
  0.6 1.9 %collective-permute-start = (bf16[256,2048]{1,0:T(8,128)(2,1)}, bf16[256,2048]{1,0:T(8,128)(2,1)S(1)}, u32[]{:S(2)}, u32[]{:S(2)}) collective-permute-start(bf16[256,2048]{1,0:T(8,128)(2,1)} %bitcast.15), channel_id=1, source_target_pairs={{0,1},{1,0},{2,3},{3,2},{4,5},{5,4},{6,7},{7,6},{8,9},{9,8},{10,11... | collective-permute-start | bytes 3145736 | tf_op jit(solution)/shard_map/core_swap/ppermute | solution.py:75
  2.6 2.4 %collective-permute-start.1 = (bf16[256,1024]{1,0:T(8,128)(2,1)}, bf16[256,1024]{1,0:T(8,128)(2,1)S(1)}, u32[]{:S(2)}, u32[]{:S(2)}) collective-permute-start(bf16[256,1024]{1,0:T(8,128)(2,1)} %bitcast.18), channel_id=1, source_target_pairs={{0,1},{1,0},{2,3},{3,2},{4,5},{5,4},{6,7},{7,6},{8,9},{9,8},{10,11... | collective-permute-start | bytes 1572872 | tf_op jit(solution)/shard_map/core_swap/ppermute | solution.py:76
  5.0 0.1 pad_add_fusion.refs_0_
  5.1 1.2 %copy-done = bf16[1,256,2048]{2,1,0:T(8,128)(2,1)S(1)} copy-done((bf16[1,256,2048]{2,1,0:T(8,128)(2,1)S(1)}, bf16[1,256,2048]{2,1,0:T(8,128)(2,1)}, u32[]{:S(2)}) %copy-start) | copy-done | bytes 1048600
  6.3 1.0 copy-done.2
  7.3 1.1 %grad_product.4 = (f32[128,1024]{1,0:T(8,128)S(1)}, f32[128,1024]{1,0:T(8,128)S(1)}, f32[128,1024]{1,0:T(8,128)S(1)}) custom-call(s32[3]{0:T(128)S(1)} %pad_add_fusion.refs_0_, bf16[256,2048]{1,0:T(8,128)(2,1)S(1)} %bitcast.16, bf16[256,1024]{1,0:T(8,128)(2,1)S(1)} %bitcast.19), custom_call_target="tpu_custom_call" | custom-call | flops 201326592 | bytes 1572864 | tf_op jit(solution)/shard_map/grad_product/pallas_call | solution.py:48
  8.5 0.0 copy-start.1
  8.5 1.2 %grad_product.5 = (bf16[128,1024]{1,0:T(8,128)(2,1)S(1)}, bf16[128,1024]{1,0:T(8,128)(2,1)S(1)}, bf16[128,1024]{1,0:T(8,128)(2,1)S(1)}) custom-call(s32[3]{0:T(128)S(1)} %pad_add_fusion.refs_0_, bf16[256,2048]{1,0:T(8,128)(2,1)S(1)} %collective-permute-done.refs_3_.refs_1_, bf16[256,1024]{1,0:T(8,128)(2,1)S(1)} %collective-permute-done.1.refs_4_.refs_2_, ...), custom_call_target="tpu_custom_call" | custom-call | flops 201326592 | bytes 1572864 | tf_op jit(solution)/shard_map/grad_product/pallas_call | solution.py:48
  9.7 2.2 %collective-permute-start.2 = (bf16[128,1024]{1,0:T(8,128)(2,1)S(1)}, bf16[128,1024]{1,0:T(8,128)(2,1)S(1)}, u32[]{:S(2)}, u32[]{:S(2)}) collective-permute-start(bf16[128,1024]{1,0:T(8,128)(2,1)S(1)} %get-tuple-element.19), channel_id=1, source_target_pairs={{0,14},{2,0},{4,2},{6,4},{8,6},{10,8},{12,10},{14,12},{1,3},{3,5},... | collective-permute-start | bytes 786440 | tf_op jit(solution)/shard_map/grad_ring/ppermute | solution.py:86
  11.9 5.9 %collective-permute-start.4 = (bf16[128,1024]{1,0:T(8,128)(2,1)S(1)}, bf16[128,1024]{1,0:T(8,128)(2,1)S(1)}, u32[]{:S(2)}, u32[]{:S(2)}) collective-permute-start(bf16[128,1024]{1,0:T(8,128)(2,1)S(1)} %get-tuple-element.21), channel_id=1, source_target_pairs={{0,4},{2,6},{4,8},{6,10},{8,12},{10,14},{12,0},{14,2},{1,13},{3,15... | collective-permute-start | bytes 786440 | tf_op jit(solution)/shard_map/grad_ring/ppermute | solution.py:86
  17.9 3.6 %collective-permute-start.5 = (bf16[128,1024]{1,0:T(8,128)(2,1)S(1)}, bf16[128,1024]{1,0:T(8,128)(2,1)S(1)}, u32[]{:S(2)}, u32[]{:S(2)}) collective-permute-start(bf16[128,1024]{1,0:T(8,128)(2,1)S(1)} %get-tuple-element.22), channel_id=1, source_target_pairs={{0,2},{2,4},{4,6},{6,8},{8,10},{10,12},{12,14},{14,0},{1,15},{3,1}... | collective-permute-start | bytes 786440 | tf_op jit(solution)/shard_map/grad_ring/ppermute | solution.py:86
  21.5 2.1 %grad_product.3 = (bf16[128,1024]{1,0:T(8,128)(2,1)S(1)}, bf16[128,1024]{1,0:T(8,128)(2,1)S(1)}, bf16[128,1024]{1,0:T(8,128)(2,1)S(1)}, bf16[128,1024]{1,0:T(8,128)(2,1)S(1)}, bf16[128,1024]{1,0:T(8,128)(2,1)S(1)}) custom-call(s32[3]{0:T(128)S(1)} %pad_add_fusion.refs_0_, bf16[256,2048]{1,0:T(8,128)(2,1)S(1)} %bitcast.17, bf16[256,1024]{1,0:T(8,128)(2,1)S(1)} %bitcast.20, ...), custom_call_target="tpu_custom_call" | custom-call | flops 671088640 | bytes 3145728 | tf_op jit(solution)/shard_map/grad_product/pallas_call | solution.py:48
  23.6 2.7 %collective-permute-start.7 = (bf16[128,1024]{1,0:T(8,128)(2,1)S(1)}, bf16[128,1024]{1,0:T(8,128)(2,1)S(1)}, u32[]{:S(2)}, u32[]{:S(2)}) collective-permute-start(bf16[128,1024]{1,0:T(8,128)(2,1)S(1)} %get-tuple-element.23), channel_id=1, source_target_pairs={{0,2},{2,4},{4,6},{6,8},{8,10},{10,12},{12,14},{14,0},{1,15},{3,1}... | collective-permute-start | bytes 786440 | tf_op jit(solution)/shard_map/grad_ring/ppermute | solution.py:86
  26.3 8.4 %collective-permute-start.8 = (bf16[128,1024]{1,0:T(8,128)(2,1)S(1)}, bf16[128,1024]{1,0:T(8,128)(2,1)S(1)}, u32[]{:S(2)}, u32[]{:S(2)}) collective-permute-start(bf16[128,1024]{1,0:T(8,128)(2,1)S(1)} %get-tuple-element.24), channel_id=1, source_target_pairs={{0,14},{2,0},{4,2},{6,4},{8,6},{10,8},{12,10},{14,12},{1,3},{3,5},... | collective-permute-start | bytes 786440 | tf_op jit(solution)/shard_map/grad_ring/ppermute | solution.py:86
  34.8 0.1 add_convert_fusion.1
  34.8 6.6 %collective-permute-start.3 = (bf16[128,1024]{1,0:T(8,128)(2,1)S(1)}, bf16[128,1024]{1,0:T(8,128)(2,1)S(1)}, u32[]{:S(2)}, u32[]{:S(2)}) collective-permute-start(bf16[128,1024]{1,0:T(8,128)(2,1)S(1)} %add_convert_fusion.1), channel_id=1, source_target_pairs={{0,12},{2,14},{4,0},{6,2},{8,4},{10,6},{12,8},{14,10},{1,5},{3,7},... | collective-permute-start | bytes 786440 | tf_op jit(solution)/shard_map/grad_ring/ppermute | solution.py:86
  41.4 0.1 add_convert_fusion
  41.6 1.9 %collective-permute-start.6 = (bf16[128,1024]{1,0:T(8,128)(2,1)S(1)}, bf16[128,1024]{1,0:T(8,128)(2,1)S(1)}, u32[]{:S(2)}, u32[]{:S(2)}) collective-permute-start(bf16[128,1024]{1,0:T(8,128)(2,1)S(1)} %add_convert_fusion), channel_id=1, source_target_pairs={{0,4},{2,6},{4,8},{6,10},{8,12},{10,14},{12,0},{14,2},{1,13},{3,15... | collective-permute-start | bytes 786440 | tf_op jit(solution)/shard_map/grad_ring/ppermute | solution.py:86
  43.5 9.1 %collective-permute-done.3 = bf16[128,1024]{1,0:T(8,128)(2,1)S(1)} collective-permute-done((bf16[128,1024]{1,0:T(8,128)(2,1)S(1)}, bf16[128,1024]{1,0:T(8,128)(2,1)S(1)}, u32[]{:S(2)}, u32[]{:S(2)}) %collective-permute-start.3) | collective-permute-done | bytes 262176 | tf_op jit(solution)/shard_map/grad_ring/ppermute | solution.py:86
  52.6 0.8 collective-permute-done.6
  53.5 0.1 add_convert_fusion.2
  53.6 2.1 %collective-permute-start.9 = (bf16[64,1024]{1,0:T(8,128)(2,1)S(1)}, bf16[64,1024]{1,0:T(8,128)(2,1)S(1)}, u32[]{:S(2)}, u32[]{:S(2)}) collective-permute-start(bf16[64,1024]{1,0:T(8,128)(2,1)S(1)} %add_convert_fusion.2), channel_id=1, source_target_pairs={{0,16},{16,0},{1,17},{17,1},{2,18},{18,2},{3,19},{19,3},{4,20},{20... | collective-permute-start | bytes 393224 | tf_op jit(solution)/shard_map/grad_pair/ppermute | solution.py:93
  55.6 6.2 %collective-permute-done.9 = bf16[64,1024]{1,0:T(8,128)(2,1)S(1)} collective-permute-done((bf16[64,1024]{1,0:T(8,128)(2,1)S(1)}, bf16[64,1024]{1,0:T(8,128)(2,1)S(1)}, u32[]{:S(2)}, u32[]{:S(2)}) %collective-permute-start.9) | collective-permute-done | bytes 131104 | tf_op jit(solution)/shard_map/grad_pair/ppermute | solution.py:93
  61.8 0.3 fusion.4
  62.1 0.1 reshape.20
  62.2 29.8 %all_to_all.10 = f32[32,2,1024]{2,1,0:T(2,128)S(1)} all-to-all(f32[32,2,1024]{2,1,0:T(2,128)S(1)} %reshape.20), channel_id=1, replica_groups=mesh['xh'=4,'z'=8,'xl'=2,'y'=8,'core'=2] {'xh','z'}, dimensions={0} | all-to-all | bytes 524288 | tf_op jit(solution)/shard_map/replica_sum/all_to_all | solution.py:106
  92.0 0.1 reduce_sum.9
  92.1 0.6 copy-done.7
  92.7 0.0 copy-done.8
  92.7 0.6 fusion.6
  93.4 17.0 %all_to_all.11 = bf16[32,16,128]{2,1,0:T(8,128)(2,1)S(1)} all-to-all(bf16[32,16,128]{2,1,0:T(8,128)(2,1)S(1)} %broadcast_in_dim.8), channel_id=1, replica_groups=mesh['xh'=4,'z'=8,'xl'=2,'y'=8,'core'=2] {'xh','z'}, dimensions={0} | all-to-all | bytes 262144 | tf_op jit(solution)/shard_map/row_gather/all_to_all | solution.py:115
  110.4 0.7 reshape.21
  (22 shorter events, 0.1 us)
Async XLA Ops:
  0.6 7.9 %collective-permute-start = (bf16[256,2048]{1,0:T(8,128)(2,1)}, bf16[256,2048]{1,0:T(8,128)(2,1)S(1)}, u32[]{:S(2)}, u32[]{:S(2)}) collective-permute-start(bf16[256,2048]{1,0:T(8,128)(2,1)} %bitcast.15), channel_id=1, source_target_pairs={{0,1},{1,0},{2,3},{3,2},{4,5},{5,4},{6,7},{7,6},{8,9},{9,8},{10,11... | collective-permute-start | bytes 3145736 | tf_op jit(solution)/shard_map/core_swap/ppermute | solution.py:75
  2.6 5.9 %collective-permute-start.1 = (bf16[256,1024]{1,0:T(8,128)(2,1)}, bf16[256,1024]{1,0:T(8,128)(2,1)S(1)}, u32[]{:S(2)}, u32[]{:S(2)}) collective-permute-start(bf16[256,1024]{1,0:T(8,128)(2,1)} %bitcast.18), channel_id=1, source_target_pairs={{0,1},{1,0},{2,3},{3,2},{4,5},{5,4},{6,7},{7,6},{8,9},{9,8},{10,11... | collective-permute-start | bytes 1572872 | tf_op jit(solution)/shard_map/core_swap/ppermute | solution.py:76
  5.1 1.2 %copy-start = (bf16[1,256,2048]{2,1,0:T(8,128)(2,1)S(1)}, bf16[1,256,2048]{2,1,0:T(8,128)(2,1)}, u32[]{:S(2)}) copy-start(bf16[1,256,2048]{2,1,0:T(8,128)(2,1)} %param.7) | copy-start | bytes 3145732
  6.3 1.0 copy-start.2
  8.5 13.0 %copy-start.1 = (bf16[1,256,2048]{2,1,0:T(8,128)(2,1)S(1)}, bf16[1,256,2048]{2,1,0:T(8,128)(2,1)}, u32[]{:S(2)}) copy-start(bf16[1,256,2048]{2,1,0:T(8,128)(2,1)} %param.7) | copy-start | bytes 3145732
  8.5 13.0 %copy-start.3 = (bf16[1,256,1024]{2,1,0:T(8,128)(2,1)S(1)}, bf16[1,256,1024]{2,1,0:T(8,128)(2,1)}, u32[]{:S(2)}) copy-start(bf16[1,256,1024]{2,1,0:T(8,128)(2,1)} %param.8) | copy-start | bytes 1572868
  9.7 25.1 %collective-permute-start.2 = (bf16[128,1024]{1,0:T(8,128)(2,1)S(1)}, bf16[128,1024]{1,0:T(8,128)(2,1)S(1)}, u32[]{:S(2)}, u32[]{:S(2)}) collective-permute-start(bf16[128,1024]{1,0:T(8,128)(2,1)S(1)} %get-tuple-element.19), channel_id=1, source_target_pairs={{0,14},{2,0},{4,2},{6,4},{8,6},{10,8},{12,10},{14,12},{1,3},{3,5},... | collective-permute-start | bytes 786440 | tf_op jit(solution)/shard_map/grad_ring/ppermute | solution.py:86
  11.9 29.5 %collective-permute-start.4 = (bf16[128,1024]{1,0:T(8,128)(2,1)S(1)}, bf16[128,1024]{1,0:T(8,128)(2,1)S(1)}, u32[]{:S(2)}, u32[]{:S(2)}) collective-permute-start(bf16[128,1024]{1,0:T(8,128)(2,1)S(1)} %get-tuple-element.21), channel_id=1, source_target_pairs={{0,4},{2,6},{4,8},{6,10},{8,12},{10,14},{12,0},{14,2},{1,13},{3,15... | collective-permute-start | bytes 786440 | tf_op jit(solution)/shard_map/grad_ring/ppermute | solution.py:86
  17.9 23.6 %collective-permute-start.5 = (bf16[128,1024]{1,0:T(8,128)(2,1)S(1)}, bf16[128,1024]{1,0:T(8,128)(2,1)S(1)}, u32[]{:S(2)}, u32[]{:S(2)}) collective-permute-start(bf16[128,1024]{1,0:T(8,128)(2,1)S(1)} %get-tuple-element.22), channel_id=1, source_target_pairs={{0,2},{2,4},{4,6},{6,8},{8,10},{10,12},{12,14},{14,0},{1,15},{3,1}... | collective-permute-start | bytes 786440 | tf_op jit(solution)/shard_map/grad_ring/ppermute | solution.py:86
  23.6 19.9 %collective-permute-start.7 = (bf16[128,1024]{1,0:T(8,128)(2,1)S(1)}, bf16[128,1024]{1,0:T(8,128)(2,1)S(1)}, u32[]{:S(2)}, u32[]{:S(2)}) collective-permute-start(bf16[128,1024]{1,0:T(8,128)(2,1)S(1)} %get-tuple-element.23), channel_id=1, source_target_pairs={{0,2},{2,4},{4,6},{6,8},{8,10},{10,12},{12,14},{14,0},{1,15},{3,1}... | collective-permute-start | bytes 786440 | tf_op jit(solution)/shard_map/grad_ring/ppermute | solution.py:86
  26.3 17.2 %collective-permute-start.8 = (bf16[128,1024]{1,0:T(8,128)(2,1)S(1)}, bf16[128,1024]{1,0:T(8,128)(2,1)S(1)}, u32[]{:S(2)}, u32[]{:S(2)}) collective-permute-start(bf16[128,1024]{1,0:T(8,128)(2,1)S(1)} %get-tuple-element.24), channel_id=1, source_target_pairs={{0,14},{2,0},{4,2},{6,4},{8,6},{10,8},{12,10},{14,12},{1,3},{3,5},... | collective-permute-start | bytes 786440 | tf_op jit(solution)/shard_map/grad_ring/ppermute | solution.py:86
  34.8 17.8 %collective-permute-start.3 = (bf16[128,1024]{1,0:T(8,128)(2,1)S(1)}, bf16[128,1024]{1,0:T(8,128)(2,1)S(1)}, u32[]{:S(2)}, u32[]{:S(2)}) collective-permute-start(bf16[128,1024]{1,0:T(8,128)(2,1)S(1)} %add_convert_fusion.1), channel_id=1, source_target_pairs={{0,12},{2,14},{4,0},{6,2},{8,4},{10,6},{12,8},{14,10},{1,5},{3,7},... | collective-permute-start | bytes 786440 | tf_op jit(solution)/shard_map/grad_ring/ppermute | solution.py:86
  41.6 11.9 %collective-permute-start.6 = (bf16[128,1024]{1,0:T(8,128)(2,1)S(1)}, bf16[128,1024]{1,0:T(8,128)(2,1)S(1)}, u32[]{:S(2)}, u32[]{:S(2)}) collective-permute-start(bf16[128,1024]{1,0:T(8,128)(2,1)S(1)} %add_convert_fusion), channel_id=1, source_target_pairs={{0,4},{2,6},{4,8},{6,10},{8,12},{10,14},{12,0},{14,2},{1,13},{3,15... | collective-permute-start | bytes 786440 | tf_op jit(solution)/shard_map/grad_ring/ppermute | solution.py:86
  53.5 8.3 %copy-start.4 = (f32[1,64,1024]{2,1,0:T(8,128)S(1)}, f32[1,64,1024]{2,1,0:T(8,128)}, u32[]{:S(2)}) copy-start(f32[1,64,1024]{2,1,0:T(8,128)} %param.11) | copy-start | bytes 786436
  53.5 8.3 %copy-start.5 = (f32[1,64,1024]{2,1,0:T(8,128)S(1)}, f32[1,64,1024]{2,1,0:T(8,128)}, u32[]{:S(2)}) copy-start(f32[1,64,1024]{2,1,0:T(8,128)} %param.10) | copy-start | bytes 786436
  53.5 8.3 %copy-start.6 = (f32[1,64,1024]{2,1,0:T(8,128)S(1)}, f32[1,64,1024]{2,1,0:T(8,128)}, u32[]{:S(2)}) copy-start(f32[1,64,1024]{2,1,0:T(8,128)} %param.9) | copy-start | bytes 786436
  53.6 8.2 %collective-permute-start.9 = (bf16[64,1024]{1,0:T(8,128)(2,1)S(1)}, bf16[64,1024]{1,0:T(8,128)(2,1)S(1)}, u32[]{:S(2)}, u32[]{:S(2)}) collective-permute-start(bf16[64,1024]{1,0:T(8,128)(2,1)S(1)} %add_convert_fusion.2), channel_id=1, source_target_pairs={{0,16},{16,0},{1,17},{17,1},{2,18},{18,2},{3,19},{19,3},{4,20},{20... | collective-permute-start | bytes 393224 | tf_op jit(solution)/shard_map/grad_pair/ppermute | solution.py:93
  92.0 0.7 copy-start.7
  92.0 0.7 copy-start.8

commit v7 on v6

--- a/solution.py
+++ b/solution.py
@@ -17,7 +17,6 @@
     xl, y, core = place[0], place[1], place[2]
     before, outs = refs[2 * pairs : -len(offsets)], refs[-len(offsets) :]
     lane = lax.broadcasted_iota(jnp.int32, (1, 128), 1)
-
     own_side = (lane < 64) == (core == 0)
     for i, offset in enumerate(offsets):
         target = lax.rem(y + RING + jnp.where(core == 0, offset, -offset), RING)
@@ -86,11 +85,16 @@
             return lax.ppermute(block, ("y", "core"), ends)
 
         back_3, four, ahead_3 = hop(early[0], -1), hop(early[1], 2), hop(early[2], 1)
-        back_2 = hop(add(late[0], back_3).astype(bf16), -2)
-        ahead_2 = hop(add(late[1], four, ahead_3).astype(bf16), 2)
-        terms = (late[4], back_2, ahead_2, hop(late[2], 1), hop(late[3], -1))
+        back_2 = add(late[0], back_3).astype(bf16)
+        ahead_2 = add(late[1], four, ahead_3).astype(bf16)
+        back_2, ahead_1 = lax.optimization_barrier((back_2, late[2]))
+        ahead_2, back_1 = lax.optimization_barrier((ahead_2, late[3]))
+        terms = (late[4], hop(back_2, -2), hop(ahead_2, 2), hop(ahead_1, 1), hop(back_1, -1))
     with jax.named_scope("grad_pair"):
-        other = lax.ppermute(add(*(t[rows:] for t in terms)).astype(bf16), "xl", swap)
+        other = add(*(t[rows:] for t in terms)).astype(bf16)
+        other, weight = lax.optimization_barrier((other, inner_weight[0].reshape(replicas, own, cols)))
+        other = lax.ppermute(other, "xl", swap)
+        weight_sum = jnp.sum(lax.all_to_all(weight, REP, 0, 0, tiled=True), axis=0)
         grad = add(other, *(t[:rows] for t in terms))
 
     with jax.named_scope("adamw"):
@@ -98,13 +102,12 @@
         second = 0.95 * second_moment[0] + 0.05 * grad * grad
         first_hat = first / (1.0 - 0.9**INNER_STEP)
         second_hat = second / (1.0 - 0.95**INNER_STEP)
-        inner_new = inner_weight[0] * (1.0 - 0.0004 * 0.1) - 0.0004 * first_hat / (
-            jnp.sqrt(second_hat) + 1e-08
-        )
-        inner_new = lax.optimization_barrier(inner_new)
+        update = (first_hat / (jnp.sqrt(second_hat) + 1e-08)).astype(bf16)
+        update = lax.optimization_barrier(update)
     with jax.named_scope("replica_sum"):
-        pieces = lax.all_to_all(inner_new.reshape(replicas, own, cols), REP, 0, 0, tiled=True)
-        summed = jnp.sum(pieces, axis=0)
+        pieces = lax.all_to_all(update.reshape(replicas, own, cols), REP, 0, 0, tiled=True)
+        update_sum = jnp.sum(pieces.astype(jnp.float32), axis=0)
+        summed = weight_sum * (1.0 - 0.0004 * 0.1) - 0.0004 * update_sum
     with jax.named_scope("outer_step"):
         pseudo = outer_weight - summed / replicas
         momentum_next = 0.9 * outer_momentum + pseudo

time: 112 us -> 130 us (1.16)
  the two profiles are of different devices: /device:TPU:32 before, /device:TPU:2 now
where the time goes in v7:
time: 130 us
  starting transfers between devices  45.1 us (35%)
  blocking collectives  42.6 us (33%)
  waiting for transfers between devices  31.2 us (24%)
  Pallas kernels  4.42 us (3%)
  local copies, waits for them, and re-layouts  3.95 us (3%)
  other arithmetic  1.5 us (1%)
    all_to_all x1, blocking collectives, shards(): lax.all_to_all(update.reshape(replicas, own, cols), REP, 0, 0, tiled=True)  25.7 us
    ppermute x7, starting transfers between devices, hop(): return lax.ppermute(block, ('y', 'core'), ends)  24.9 us
    all_to_all x1, blocking collectives, shards(): lax.all_to_all(copies, REP, 0, 0, tiled=True).reshape(rows, cols)  16.9 us
    ppermute x7, waiting for transfers between devices, hop(): return lax.ppermute(block, ('y', 'core'), ends)  15.4 us
    all_to_all x1, waiting for transfers between devices, shards(): weight_sum = jnp.sum(lax.all_to_all(weight, REP, 0, 0, tiled=True), axis=0)  12.9 us
    ppermute x1, starting transfers between devices, shards(): other = lax.ppermute(other, 'xl', swap)  12 us
    pallas_call x3, Pallas kernels, product(): pl.pallas_call(lambda *refs: product_kernel(offsets, len(pairs), *refs),...  4.42 us
    all_to_all x1, starting transfers between devices, shards(): weight_sum = jnp.sum(lax.all_to_all(weight, REP, 0, 0, tiled=True), axis=0)  3.87 us
  transfers between devices with their start and end apart: 11, of which 6 were waited for; matrix products, arithmetic and copies ran while one was open for 1% of the time, Pallas kernels for 3%

profile of v7, /device:TPU:2, one launch (start us, length us, event | category | flops | bytes accessed | tf_op | source)
XLA Modules:
  0.0 129.6 jit_solution(4469039869558301910)
XLA Ops:
  0.6 1.9 %collective-permute-start = (bf16[256,2048]{1,0:T(8,128)(2,1)}, bf16[256,2048]{1,0:T(8,128)(2,1)S(1)}, u32[]{:S(2)}, u32[]{:S(2)}) collective-permute-start(bf16[256,2048]{1,0:T(8,128)(2,1)} %bitcast.15), channel_id=1, source_target_pairs={{0,1},{1,0},{2,3},{3,2},{4,5},{5,4},{6,7},{7,6},{8,9},{9,8},{10,11... | collective-permute-start | bytes 3145736 | tf_op jit(solution)/shard_map/core_swap/ppermute | solution.py:74
  2.6 2.4 %collective-permute-start.1 = (bf16[256,1024]{1,0:T(8,128)(2,1)}, bf16[256,1024]{1,0:T(8,128)(2,1)S(1)}, u32[]{:S(2)}, u32[]{:S(2)}) collective-permute-start(bf16[256,1024]{1,0:T(8,128)(2,1)} %bitcast.18), channel_id=1, source_target_pairs={{0,1},{1,0},{2,3},{3,2},{4,5},{5,4},{6,7},{7,6},{8,9},{9,8},{10,11... | collective-permute-start | bytes 1572872 | tf_op jit(solution)/shard_map/core_swap/ppermute | solution.py:75
  5.1 1.2 copy-done
  6.3 1.0 copy-done.2
  7.3 1.1 grad_product.4
  8.5 1.2 grad_product.5
  9.7 6.2 %collective-permute-start.2 = (bf16[128,1024]{1,0:T(8,128)(2,1)S(1)}, bf16[128,1024]{1,0:T(8,128)(2,1)S(1)}, u32[]{:S(2)}, u32[]{:S(2)}) collective-permute-start(bf16[128,1024]{1,0:T(8,128)(2,1)S(1)} %get-tuple-element.25), channel_id=1, source_target_pairs={{0,14},{2,0},{4,2},{6,4},{8,6},{10,8},{12,10},{14,12},{1,3},{3,5},... | collective-permute-start | bytes 786440 | tf_op jit(solution)/shard_map/grad_ring/ppermute | solution.py:85
  15.9 1.9 %collective-permute-start.4 = (bf16[128,1024]{1,0:T(8,128)(2,1)S(1)}, bf16[128,1024]{1,0:T(8,128)(2,1)S(1)}, u32[]{:S(2)}, u32[]{:S(2)}) collective-permute-start(bf16[128,1024]{1,0:T(8,128)(2,1)S(1)} %get-tuple-element.29), channel_id=1, source_target_pairs={{0,4},{2,6},{4,8},{6,10},{8,12},{10,14},{12,0},{14,2},{1,13},{3,15... | collective-permute-start | bytes 786440 | tf_op jit(solution)/shard_map/grad_ring/ppermute | solution.py:85
  17.8 2.5 %collective-permute-start.5 = (bf16[128,1024]{1,0:T(8,128)(2,1)S(1)}, bf16[128,1024]{1,0:T(8,128)(2,1)S(1)}, u32[]{:S(2)}, u32[]{:S(2)}) collective-permute-start(bf16[128,1024]{1,0:T(8,128)(2,1)S(1)} %get-tuple-element.30), channel_id=1, source_target_pairs={{0,2},{2,4},{4,6},{6,8},{8,10},{10,12},{12,14},{14,0},{1,15},{3,1}... | collective-permute-start | bytes 786440 | tf_op jit(solution)/shard_map/grad_ring/ppermute | solution.py:85
  20.3 2.1 %grad_product.3 = (bf16[128,1024]{1,0:T(8,128)(2,1)S(1)}, bf16[128,1024]{1,0:T(8,128)(2,1)S(1)}, bf16[128,1024]{1,0:T(8,128)(2,1)S(1)}, bf16[128,1024]{1,0:T(8,128)(2,1)S(1)}, bf16[128,1024]{1,0:T(8,128)(2,1)S(1)}) custom-call(s32[3]{0:T(128)S(1)} %pad_add_fusion.refs_0_, bf16[256,2048]{1,0:T(8,128)(2,1)S(1)} %bitcast.17, bf16[256,1024]{1,0:T(8,128)(2,1)S(1)} %bitcast.20, ...), custom_call_target="tpu_custom_call" | custom-call | flops 671088640 | bytes 3145728 | tf_op jit(solution)/shard_map/grad_product/pallas_call | solution.py:47
  22.4 6.1 %collective-permute-done.4 = bf16[128,1024]{1,0:T(8,128)(2,1)S(1)} collective-permute-done((bf16[128,1024]{1,0:T(8,128)(2,1)S(1)}, bf16[128,1024]{1,0:T(8,128)(2,1)S(1)}, u32[]{:S(2)}, u32[]{:S(2)}) %collective-permute-start.4) | collective-permute-done | bytes 262176 | tf_op jit(solution)/shard_map/grad_ring/ppermute | solution.py:85
  28.5 0.8 collective-permute-done.5
  29.3 0.2 add_convert_fusion
  29.5 4.5 %collective-permute-start.3 = (bf16[128,1024]{1,0:T(8,128)(2,1)S(1)}, bf16[128,1024]{1,0:T(8,128)(2,1)S(1)}, u32[]{:S(2)}, u32[]{:S(2)}) collective-permute-start(bf16[128,1024]{1,0:T(8,128)(2,1)S(1)} %get-tuple-element.27), channel_id=1, source_target_pairs={{0,12},{2,14},{4,0},{6,2},{8,4},{10,6},{12,8},{14,10},{1,5},{3,7},... | collective-permute-start | bytes 786440 | tf_op jit(solution)/shard_map/grad_ring/ppermute | solution.py:85
  34.1 3.3 %collective-permute-start.7 = (bf16[128,1024]{1,0:T(8,128)(2,1)S(1)}, bf16[128,1024]{1,0:T(8,128)(2,1)S(1)}, u32[]{:S(2)}, u32[]{:S(2)}) collective-permute-start(bf16[128,1024]{1,0:T(8,128)(2,1)S(1)} %get-tuple-element.33), channel_id=1, source_target_pairs={{0,2},{2,4},{4,6},{6,8},{8,10},{10,12},{12,14},{14,0},{1,15},{3,1}... | collective-permute-start | bytes 786440 | tf_op jit(solution)/shard_map/grad_ring/ppermute | solution.py:85
  37.4 1.9 %collective-permute-start.6 = (bf16[128,1024]{1,0:T(8,128)(2,1)S(1)}, bf16[128,1024]{1,0:T(8,128)(2,1)S(1)}, u32[]{:S(2)}, u32[]{:S(2)}) collective-permute-start(bf16[128,1024]{1,0:T(8,128)(2,1)S(1)} %get-tuple-element.32), channel_id=1, source_target_pairs={{0,4},{2,6},{4,8},{6,10},{8,12},{10,14},{12,0},{14,2},{1,13},{3,15... | collective-permute-start | bytes 786440 | tf_op jit(solution)/shard_map/grad_ring/ppermute | solution.py:85
  39.3 4.6 %collective-permute-start.8 = (bf16[128,1024]{1,0:T(8,128)(2,1)S(1)}, bf16[128,1024]{1,0:T(8,128)(2,1)S(1)}, u32[]{:S(2)}, u32[]{:S(2)}) collective-permute-start(bf16[128,1024]{1,0:T(8,128)(2,1)S(1)} %get-tuple-element.34), channel_id=1, source_target_pairs={{0,14},{2,0},{4,2},{6,4},{8,6},{10,8},{12,10},{14,12},{1,3},{3,5},... | collective-permute-start | bytes 786440 | tf_op jit(solution)/shard_map/grad_ring/ppermute | solution.py:85
  43.9 0.8 squeeze.15
  44.8 8.2 %collective-permute-done.6 = bf16[128,1024]{1,0:T(8,128)(2,1)S(1)} collective-permute-done((bf16[128,1024]{1,0:T(8,128)(2,1)S(1)}, bf16[128,1024]{1,0:T(8,128)(2,1)S(1)}, u32[]{:S(2)}, u32[]{:S(2)}) %collective-permute-start.6) | collective-permute-done | bytes 262176 | tf_op jit(solution)/shard_map/grad_ring/ppermute | solution.py:85
  53.0 0.4 collective-permute-done.8
  53.3 0.1 add_convert_fusion.2
  53.4 12.0 %collective-permute-start.9 = (bf16[64,1024]{1,0:T(8,128)(2,1)S(1)}, bf16[64,1024]{1,0:T(8,128)(2,1)S(1)}, u32[]{:S(2)}, u32[]{:S(2)}) collective-permute-start(bf16[64,1024]{1,0:T(8,128)(2,1)S(1)} %add_convert_fusion.2), channel_id=1, source_target_pairs={{0,16},{16,0},{1,17},{17,1},{2,18},{18,2},{3,19},{19,3},{4,20},{20... | collective-permute-start | bytes 393224 | tf_op jit(solution)/shard_map/grad_pair/ppermute | solution.py:96
  65.4 2.9 %collective-permute-done.9 = bf16[64,1024]{1,0:T(8,128)(2,1)S(1)} collective-permute-done((bf16[64,1024]{1,0:T(8,128)(2,1)S(1)}, bf16[64,1024]{1,0:T(8,128)(2,1)S(1)}, u32[]{:S(2)}, u32[]{:S(2)}) %collective-permute-start.9) | collective-permute-done | bytes 131104 | tf_op jit(solution)/shard_map/grad_pair/ppermute | solution.py:96
  68.3 0.3 fusion.4
  68.6 25.7 %all_to_all.15 = bf16[32,2,1024]{2,1,0:T(2,128)(2,1)S(1)} all-to-all(bf16[32,2,1024]{2,1,0:T(2,128)(2,1)S(1)} %reshape.18), channel_id=1, replica_groups=mesh['xh'=4,'z'=8,'xl'=2,'y'=8,'core'=2] {'xh','z'}, dimensions={0} | all-to-all | bytes 262144 | tf_op jit(solution)/shard_map/replica_sum/all_to_all | solution.py:108
  94.4 3.9 %all-to-all-start = ((f32[32,2,1024]{2,1,0:T(2,128)}), f32[32,2,1024]{2,1,0:T(2,128)S(1)}, u32[]{:S(2)}, u32[]{:S(2)}) async-start(f32[32,2,1024]{2,1,0:T(2,128)} %squeeze.15), calls=%async_computation | async-start | bytes 524288 | tf_op jit(solution)/shard_map/grad_pair/all_to_all | solution.py:97
  98.2 0.1 convert_reduce_fusion
  98.4 12.9 %all-to-all-done = f32[32,2,1024]{2,1,0:T(2,128)S(1)} async-done(((f32[32,2,1024]{2,1,0:T(2,128)}), f32[32,2,1024]{2,1,0:T(2,128)S(1)}, u32[]{:S(2)}, u32[]{:S(2)}) %all-to-all-start) | async-done | bytes 262176 | tf_op jit(solution)/shard_map/grad_pair/all_to_all | solution.py:97
  111.3 0.1 reduce_sum.18
  111.4 0.6 fusion.5
  112.1 16.9 %all_to_all.16 = bf16[32,16,128]{2,1,0:T(8,128)(2,1)S(1)} all-to-all(bf16[32,16,128]{2,1,0:T(8,128)(2,1)S(1)} %broadcast_in_dim.8), channel_id=1, replica_groups=mesh['xh'=4,'z'=8,'xl'=2,'y'=8,'core'=2] {'xh','z'}, dimensions={0} | all-to-all | bytes 262144 | tf_op jit(solution)/shard_map/row_gather/all_to_all | solution.py:118
  128.9 0.7 reshape.19
  (25 shorter events, 0.2 us)
Async XLA Ops:
  0.6 7.9 %collective-permute-start = (bf16[256,2048]{1,0:T(8,128)(2,1)}, bf16[256,2048]{1,0:T(8,128)(2,1)S(1)}, u32[]{:S(2)}, u32[]{:S(2)}) collective-permute-start(bf16[256,2048]{1,0:T(8,128)(2,1)} %bitcast.15), channel_id=1, source_target_pairs={{0,1},{1,0},{2,3},{3,2},{4,5},{5,4},{6,7},{7,6},{8,9},{9,8},{10,11... | collective-permute-start | bytes 3145736 | tf_op jit(solution)/shard_map/core_swap/ppermute | solution.py:74
  2.6 5.9 %collective-permute-start.1 = (bf16[256,1024]{1,0:T(8,128)(2,1)}, bf16[256,1024]{1,0:T(8,128)(2,1)S(1)}, u32[]{:S(2)}, u32[]{:S(2)}) collective-permute-start(bf16[256,1024]{1,0:T(8,128)(2,1)} %bitcast.18), channel_id=1, source_target_pairs={{0,1},{1,0},{2,3},{3,2},{4,5},{5,4},{6,7},{7,6},{8,9},{9,8},{10,11... | collective-permute-start | bytes 1572872 | tf_op jit(solution)/shard_map/core_swap/ppermute | solution.py:75
  5.1 1.2 copy-start
  6.3 1.0 copy-start.2
  8.5 11.8 %copy-start.1 = (bf16[1,256,2048]{2,1,0:T(8,128)(2,1)S(1)}, bf16[1,256,2048]{2,1,0:T(8,128)(2,1)}, u32[]{:S(2)}) copy-start(bf16[1,256,2048]{2,1,0:T(8,128)(2,1)} %param.7) | copy-start | bytes 3145732
  8.5 11.8 %copy-start.3 = (bf16[1,256,1024]{2,1,0:T(8,128)(2,1)S(1)}, bf16[1,256,1024]{2,1,0:T(8,128)(2,1)}, u32[]{:S(2)}) copy-start(bf16[1,256,1024]{2,1,0:T(8,128)(2,1)} %param.8) | copy-start | bytes 1572868
  9.7 12.7 %collective-permute-start.2 = (bf16[128,1024]{1,0:T(8,128)(2,1)S(1)}, bf16[128,1024]{1,0:T(8,128)(2,1)S(1)}, u32[]{:S(2)}, u32[]{:S(2)}) collective-permute-start(bf16[128,1024]{1,0:T(8,128)(2,1)S(1)} %get-tuple-element.25), channel_id=1, source_target_pairs={{0,14},{2,0},{4,2},{6,4},{8,6},{10,8},{12,10},{14,12},{1,3},{3,5},... | collective-permute-start | bytes 786440 | tf_op jit(solution)/shard_map/grad_ring/ppermute | solution.py:85
  15.9 12.6 %collective-permute-start.4 = (bf16[128,1024]{1,0:T(8,128)(2,1)S(1)}, bf16[128,1024]{1,0:T(8,128)(2,1)S(1)}, u32[]{:S(2)}, u32[]{:S(2)}) collective-permute-start(bf16[128,1024]{1,0:T(8,128)(2,1)S(1)} %get-tuple-element.29), channel_id=1, source_target_pairs={{0,4},{2,6},{4,8},{6,10},{8,12},{10,14},{12,0},{14,2},{1,13},{3,15... | collective-permute-start | bytes 786440 | tf_op jit(solution)/shard_map/grad_ring/ppermute | solution.py:85
  17.8 11.5 %collective-permute-start.5 = (bf16[128,1024]{1,0:T(8,128)(2,1)S(1)}, bf16[128,1024]{1,0:T(8,128)(2,1)S(1)}, u32[]{:S(2)}, u32[]{:S(2)}) collective-permute-start(bf16[128,1024]{1,0:T(8,128)(2,1)S(1)} %get-tuple-element.30), channel_id=1, source_target_pairs={{0,2},{2,4},{4,6},{6,8},{8,10},{10,12},{12,14},{14,0},{1,15},{3,1}... | collective-permute-start | bytes 786440 | tf_op jit(solution)/shard_map/grad_ring/ppermute | solution.py:85
  29.3 14.6 %copy-start.4 = (f32[1,64,1024]{2,1,0:T(8,128)S(1)}, f32[1,64,1024]{2,1,0:T(8,128)}, u32[]{:S(2)}) copy-start(f32[1,64,1024]{2,1,0:T(8,128)} %param.9) | copy-start | bytes 786436
  29.5 15.3 %collective-permute-start.3 = (bf16[128,1024]{1,0:T(8,128)(2,1)S(1)}, bf16[128,1024]{1,0:T(8,128)(2,1)S(1)}, u32[]{:S(2)}, u32[]{:S(2)}) collective-permute-start(bf16[128,1024]{1,0:T(8,128)(2,1)S(1)} %get-tuple-element.27), channel_id=1, source_target_pairs={{0,12},{2,14},{4,0},{6,2},{8,4},{10,6},{12,8},{14,10},{1,5},{3,7},... | collective-permute-start | bytes 786440 | tf_op jit(solution)/shard_map/grad_ring/ppermute | solution.py:85
  34.1 10.7 %collective-permute-start.7 = (bf16[128,1024]{1,0:T(8,128)(2,1)S(1)}, bf16[128,1024]{1,0:T(8,128)(2,1)S(1)}, u32[]{:S(2)}, u32[]{:S(2)}) collective-permute-start(bf16[128,1024]{1,0:T(8,128)(2,1)S(1)} %get-tuple-element.33), channel_id=1, source_target_pairs={{0,2},{2,4},{4,6},{6,8},{8,10},{10,12},{12,14},{14,0},{1,15},{3,1}... | collective-permute-start | bytes 786440 | tf_op jit(solution)/shard_map/grad_ring/ppermute | solution.py:85
  37.4 15.6 %collective-permute-start.6 = (bf16[128,1024]{1,0:T(8,128)(2,1)S(1)}, bf16[128,1024]{1,0:T(8,128)(2,1)S(1)}, u32[]{:S(2)}, u32[]{:S(2)}) collective-permute-start(bf16[128,1024]{1,0:T(8,128)(2,1)S(1)} %get-tuple-element.32), channel_id=1, source_target_pairs={{0,4},{2,6},{4,8},{6,10},{8,12},{10,14},{12,0},{14,2},{1,13},{3,15... | collective-permute-start | bytes 786440 | tf_op jit(solution)/shard_map/grad_ring/ppermute | solution.py:85
  39.3 14.0 %collective-permute-start.8 = (bf16[128,1024]{1,0:T(8,128)(2,1)S(1)}, bf16[128,1024]{1,0:T(8,128)(2,1)S(1)}, u32[]{:S(2)}, u32[]{:S(2)}) collective-permute-start(bf16[128,1024]{1,0:T(8,128)(2,1)S(1)} %get-tuple-element.34), channel_id=1, source_target_pairs={{0,14},{2,0},{4,2},{6,4},{8,6},{10,8},{12,10},{14,12},{1,3},{3,5},... | collective-permute-start | bytes 786440 | tf_op jit(solution)/shard_map/grad_ring/ppermute | solution.py:85
  53.3 15.0 %copy-start.5 = (f32[1,64,1024]{2,1,0:T(8,128)S(1)}, f32[1,64,1024]{2,1,0:T(8,128)}, u32[]{:S(2)}) copy-start(f32[1,64,1024]{2,1,0:T(8,128)} %param.11) | copy-start | bytes 786436
  53.3 15.0 %copy-start.6 = (f32[1,64,1024]{2,1,0:T(8,128)S(1)}, f32[1,64,1024]{2,1,0:T(8,128)}, u32[]{:S(2)}) copy-start(f32[1,64,1024]{2,1,0:T(8,128)} %param.10) | copy-start | bytes 786436
  53.4 14.9 %collective-permute-start.9 = (bf16[64,1024]{1,0:T(8,128)(2,1)S(1)}, bf16[64,1024]{1,0:T(8,128)(2,1)S(1)}, u32[]{:S(2)}, u32[]{:S(2)}) collective-permute-start(bf16[64,1024]{1,0:T(8,128)(2,1)S(1)} %add_convert_fusion.2), channel_id=1, source_target_pairs={{0,16},{16,0},{1,17},{17,1},{2,18},{18,2},{3,19},{19,3},{4,20},{20... | collective-permute-start | bytes 393224 | tf_op jit(solution)/shard_map/grad_pair/ppermute | solution.py:96
  94.4 16.9 %all-to-all-start = ((f32[32,2,1024]{2,1,0:T(2,128)}), f32[32,2,1024]{2,1,0:T(2,128)S(1)}, u32[]{:S(2)}, u32[]{:S(2)}) async-start(f32[32,2,1024]{2,1,0:T(2,128)} %squeeze.15), calls=%async_computation | async-start | bytes 524288 | tf_op jit(solution)/shard_map/grad_pair/all_to_all | solution.py:97
  98.4 13.0 %copy-start.7 = (f32[2,1024]{1,0:T(2,128)S(1)}, f32[2,1024]{1,0:T(2,128)}, u32[]{:S(2)}) copy-start(f32[2,1024]{1,0:T(2,128)} %param.12) | copy-start | bytes 24580
  98.4 13.0 %copy-start.8 = (f32[2,1024]{1,0:T(2,128)S(1)}, f32[2,1024]{1,0:T(2,128)}, u32[]{:S(2)}) copy-start(f32[2,1024]{1,0:T(2,128)} %param.13) | copy-start | bytes 24580

commit v8 on v6

--- a/solution.py
+++ b/solution.py
@@ -13,11 +13,10 @@
 RING = 8
 
 
-def product_kernel(offsets, pairs, place, *refs):
+def product_kernel(offsets, sources, wide, place, *refs):
     xl, y, core = place[0], place[1], place[2]
-    before, outs = refs[2 * pairs : -len(offsets)], refs[-len(offsets) :]
+    before, outs = refs[sources : -len(offsets)], refs[-len(offsets) :]
     lane = lax.broadcasted_iota(jnp.int32, (1, 128), 1)
-
     own_side = (lane < 64) == (core == 0)
     for i, offset in enumerate(offsets):
         target = lax.rem(y + RING + jnp.where(core == 0, offset, -offset), RING)
@@ -35,25 +34,25 @@
         def times(lhs, rhs):
             return lax.dot_general(lhs, rhs, (((0,), (0,)), ((), ())), preferred_element_type=jnp.float32)
 
-        total = sum(times(columns(refs[2 * k]), refs[2 * k + 1][...]) for k in range(pairs))
+        total = sum(times(columns(ref), ref[:, wide:]) for ref in refs[:sources])
         if before:
             total = total + before[i][...]
         outs[i][...] = total.astype(outs[i].dtype)
 
 
-def product(offsets, dtype, place, pairs, before=()):
+def product(offsets, dtype, place, sources, cols, before=()):
     vmem = pl.BlockSpec(memory_space=pltpu.VMEM)
-    operands = [x for pair in pairs for x in pair] + list(before)
-    tokens, cols = pairs[0][1].shape
+    operands = [*sources, *before]
+    tokens, wide = sources[0].shape
     return pl.pallas_call(
-        lambda *refs: product_kernel(offsets, len(pairs), *refs),
+        lambda *refs: product_kernel(offsets, len(sources), wide - cols, *refs),
         out_shape=[jax.ShapeDtypeStruct((128, cols), dtype) for _ in offsets],
         in_specs=[pl.BlockSpec(memory_space=pltpu.SMEM)] + [vmem] * len(operands),
         out_specs=[vmem for _ in offsets],
         compiler_params=pltpu.CompilerParams(vmem_limit_bytes=24 * 1024 * 1024),
         cost_estimate=pl.CostEstimate(
-            flops=2 * 128 * len(offsets) * len(pairs) * tokens * cols,
-            bytes_accessed=2 * len(pairs) * tokens * (pairs[0][0].shape[1] + cols),
+            flops=2 * 128 * len(offsets) * len(sources) * tokens * cols,
+            bytes_accessed=2 * len(sources) * tokens * wide,
             transcendentals=0,
         ),
     )(place, *operands)
@@ -72,12 +71,12 @@
 
     swap = [(0, 1), (1, 0)]
     with jax.named_scope("core_swap"):
-        acts_peer = lax.ppermute(acts[0], "core", swap)
-        cot_peer = lax.ppermute(grad_out[0], "core", swap)
+        here = jnp.concatenate([acts[0], grad_out[0]], axis=1)
+        peer = lax.ppermute(here, "core", swap)
     with jax.named_scope("grad_product"):
-        here, peer = (acts[0], grad_out[0]), (acts_peer, cot_peer)
-        early = product((-3, 4, 3), bf16, place, [peer], product((-3, 4, 3), jnp.float32, place, [here]))
-        late = product((-2, 2, 1, -1, 0), bf16, place, [here, peer])
+        mine = product((-3, 4, 3), jnp.float32, place, [here], cols)
+        early = product((-3, 4, 3), bf16, place, [peer], cols, mine)
+        late = product((-2, 2, 1, -1, 0), bf16, place, [here, peer], cols)
     with jax.named_scope("grad_ring"):
 
         def hop(block, k):
@@ -86,9 +85,11 @@
             return lax.ppermute(block, ("y", "core"), ends)
 
         back_3, four, ahead_3 = hop(early[0], -1), hop(early[1], 2), hop(early[2], 1)
-        back_2 = hop(add(late[0], back_3).astype(bf16), -2)
-        ahead_2 = hop(add(late[1], four, ahead_3).astype(bf16), 2)
-        terms = (late[4], back_2, ahead_2, hop(late[2], 1), hop(late[3], -1))
+        back_2 = hop(add(late[0], back_3).astype(bf16), -1)
+        ahead_2 = hop(add(late[1], four, ahead_3).astype(bf16), 1)
+        ahead_1 = hop(add(late[2], ahead_2).astype(bf16), 1)
+        back_1 = hop(add(late[3], back_2).astype(bf16), -1)
+        terms = (late[4], ahead_1, back_1)
     with jax.named_scope("grad_pair"):
         other = lax.ppermute(add(*(t[rows:] for t in terms)).astype(bf16), "xl", swap)
         grad = add(other, *(t[:rows] for t in terms))

time: 112 us -> 113 us (level)
  the two profiles are of different devices: /device:TPU:32 before, /device:TPU:1 now
where the time goes in v8:
time: 113 us; the launch traced here: 112 us
  blocking collectives  45.1 us (40%)
  starting transfers between devices  35.6 us (32%)
  waiting for transfers between devices  22.2 us (20%)
  Pallas kernels  4.36 us (4%)
  other arithmetic  2.93 us (3%)
    all_to_all x1, blocking collectives, shards(): lax.all_to_all(inner_new.reshape(replicas, own, cols), REP, 0, 0, tiled=T...  27.6 us
    ppermute x7, starting transfers between devices, hop(): return lax.ppermute(block, ('y', 'core'), ends)  17.7 us
    all_to_all x1, blocking collectives, shards(): lax.all_to_all(copies, REP, 0, 0, tiled=True).reshape(rows, cols)  17.6 us
    ppermute x7, waiting for transfers between devices, hop(): return lax.ppermute(block, ('y', 'core'), ends)  16.7 us
    ppermute x1, starting transfers between devices, shards(): peer = lax.ppermute(here, 'core', swap)  16.1 us
    pallas_call x3, Pallas kernels, product(): pl.pallas_call(lambda *refs: product_kernel(offsets, len(sources), wide -...  4.36 us
    ppermute x1, waiting for transfers between devices, shards(): lax.ppermute(add(*(t[rows:] for t in terms)).astype(bf16), 'xl', swap)  3.78 us
  transfers between devices with their start and end apart: 9, of which 7 were waited for; matrix products, arithmetic and copies ran while one was open for 0% of the time, Pallas kernels for 3%

profile of v8, /device:TPU:1, one launch (start us, length us, event | category | flops | bytes accessed | tf_op | source)
XLA Modules:
  0.0 112.1 jit_solution(18166243560881350771)
XLA Ops:
  0.6 1.5 %pad_maximum_fusion.refs_1_ = bf16[256,3072]{1,0:T(8,128)(2,1)S(1)} fusion(bf16[256,1024]{1,0:T(8,128)(2,1)} %bitcast.16, bf16[256,2048]{1,0:T(8,128)(2,1)} %bitcast.15), kind=kLoop, calls=%fused_computation | loop fusion | flops 3145728 | bytes 3145728 | tf_op jit(solution)/shard_map/core_swap/concatenate | solution.py:74
  2.1 16.1 %collective-permute-start = (bf16[256,3072]{1,0:T(8,128)(2,1)S(1)}, bf16[256,3072]{1,0:T(8,128)(2,1)S(1)}, u32[]{:S(2)}, u32[]{:S(2)}) collective-permute-start(bf16[256,3072]{1,0:T(8,128)(2,1)S(1)} %pad_maximum_fusion.refs_1_), channel_id=1, source_target_pairs={{0,1},{1,0},{2,3},{3,2},{4,5},{5,4},{6,7},{7,6},{8,9},{9,8},{10,11... | collective-permute-start | bytes 4718600 | tf_op jit(solution)/shard_map/core_swap/ppermute | solution.py:75
  18.2 0.1 pad_add_fusion.refs_0_
  18.3 1.1 %grad_product.4 = (f32[128,1024]{1,0:T(8,128)S(1)}, f32[128,1024]{1,0:T(8,128)S(1)}, f32[128,1024]{1,0:T(8,128)S(1)}) custom-call(s32[3]{0:T(128)S(1)} %pad_add_fusion.refs_0_, bf16[256,3072]{1,0:T(8,128)(2,1)S(1)} %pad_maximum_fusion.refs_1_), custom_call_target="tpu_custom_call" | custom-call | flops 201326592 | bytes 1572864 | tf_op jit(solution)/shard_map/grad_product/pallas_call | solution.py:47
  19.4 1.8 %collective-permute-done.refs_2_.refs_1_ = bf16[256,3072]{1,0:T(8,128)(2,1)S(1)} collective-permute-done((bf16[256,3072]{1,0:T(8,128)(2,1)S(1)}, bf16[256,3072]{1,0:T(8,128)(2,1)S(1)}, u32[]{:S(2)}, u32[]{:S(2)}) %collective-permute-start) | collective-permute-done | bytes 1572896 | tf_op jit(solution)/shard_map/core_swap/ppermute | solution.py:75
  21.2 1.2 %grad_product.5 = (bf16[128,1024]{1,0:T(8,128)(2,1)S(1)}, bf16[128,1024]{1,0:T(8,128)(2,1)S(1)}, bf16[128,1024]{1,0:T(8,128)(2,1)S(1)}) custom-call(s32[3]{0:T(128)S(1)} %pad_add_fusion.refs_0_, bf16[256,3072]{1,0:T(8,128)(2,1)S(1)} %collective-permute-done.refs_2_.refs_1_, f32[128,1024]{1,0:T(8,128)S(1)} %get-tuple-element.17.refs_2_, ...), custom_call_target="tpu_custom_call" | custom-call | flops 201326592 | bytes 1572864 | tf_op jit(solution)/shard_map/grad_product/pallas_call | solution.py:47
  22.4 1.9 %collective-permute-start.1 = (bf16[128,1024]{1,0:T(8,128)(2,1)S(1)}, bf16[128,1024]{1,0:T(8,128)(2,1)S(1)}, u32[]{:S(2)}, u32[]{:S(2)}) collective-permute-start(bf16[128,1024]{1,0:T(8,128)(2,1)S(1)} %get-tuple-element.20), channel_id=1, source_target_pairs={{0,4},{2,6},{4,8},{6,10},{8,12},{10,14},{12,0},{14,2},{1,13},{3,15... | collective-permute-start | bytes 786440 | tf_op jit(solution)/shard_map/grad_ring/ppermute | solution.py:85
  24.3 1.9 %collective-permute-start.2 = (bf16[128,1024]{1,0:T(8,128)(2,1)S(1)}, bf16[128,1024]{1,0:T(8,128)(2,1)S(1)}, u32[]{:S(2)}, u32[]{:S(2)}) collective-permute-start(bf16[128,1024]{1,0:T(8,128)(2,1)S(1)} %get-tuple-element.21), channel_id=1, source_target_pairs={{0,2},{2,4},{4,6},{6,8},{8,10},{10,12},{12,14},{14,0},{1,15},{3,1}... | collective-permute-start | bytes 786440 | tf_op jit(solution)/shard_map/grad_ring/ppermute | solution.py:85
  26.2 3.4 %collective-permute-start.5 = (bf16[128,1024]{1,0:T(8,128)(2,1)S(1)}, bf16[128,1024]{1,0:T(8,128)(2,1)S(1)}, u32[]{:S(2)}, u32[]{:S(2)}) collective-permute-start(bf16[128,1024]{1,0:T(8,128)(2,1)S(1)} %get-tuple-element.24), channel_id=1, source_target_pairs={{0,14},{2,0},{4,2},{6,4},{8,6},{10,8},{12,10},{14,12},{1,3},{3,5},... | collective-permute-start | bytes 786440 | tf_op jit(solution)/shard_map/grad_ring/ppermute | solution.py:85
  29.6 2.1 %grad_product.3 = (bf16[128,1024]{1,0:T(8,128)(2,1)S(1)}, bf16[128,1024]{1,0:T(8,128)(2,1)S(1)}, bf16[128,1024]{1,0:T(8,128)(2,1)S(1)}, bf16[128,1024]{1,0:T(8,128)(2,1)S(1)}, bf16[128,1024]{1,0:T(8,128)(2,1)S(1)}) custom-call(s32[3]{0:T(128)S(1)} %pad_add_fusion.refs_0_, bf16[256,3072]{1,0:T(8,128)(2,1)S(1)} %pad_maximum_fusion.refs_1_, ...), custom_call_target="tpu_custom_call" | custom-call | flops 671088640 | bytes 3145728 | tf_op jit(solution)/shard_map/grad_product/pallas_call | solution.py:47
  31.7 4.7 %collective-permute-done.2 = bf16[128,1024]{1,0:T(8,128)(2,1)S(1)} collective-permute-done((bf16[128,1024]{1,0:T(8,128)(2,1)S(1)}, bf16[128,1024]{1,0:T(8,128)(2,1)S(1)}, u32[]{:S(2)}, u32[]{:S(2)}) %collective-permute-start.2) | collective-permute-done | bytes 262176 | tf_op jit(solution)/shard_map/grad_ring/ppermute | solution.py:85
  36.4 0.1 add_convert_fusion.3
  36.5 2.1 %collective-permute-start.3 = (bf16[128,1024]{1,0:T(8,128)(2,1)S(1)}, bf16[128,1024]{1,0:T(8,128)(2,1)S(1)}, u32[]{:S(2)}, u32[]{:S(2)}) collective-permute-start(bf16[128,1024]{1,0:T(8,128)(2,1)S(1)} %add_convert_fusion.3), channel_id=1, source_target_pairs={{0,2},{2,4},{4,6},{6,8},{8,10},{10,12},{12,14},{14,0},{1,15},{3,1}... | collective-permute-start | bytes 786440 | tf_op jit(solution)/shard_map/grad_ring/ppermute | solution.py:85
  38.6 0.1 add_convert_fusion.1
  38.7 3.4 %collective-permute-start.6 = (bf16[128,1024]{1,0:T(8,128)(2,1)S(1)}, bf16[128,1024]{1,0:T(8,128)(2,1)S(1)}, u32[]{:S(2)}, u32[]{:S(2)}) collective-permute-start(bf16[128,1024]{1,0:T(8,128)(2,1)S(1)} %add_convert_fusion.1), channel_id=1, source_target_pairs={{0,14},{2,0},{4,2},{6,4},{8,6},{10,8},{12,10},{14,12},{1,3},{3,5},... | collective-permute-start | bytes 786440 | tf_op jit(solution)/shard_map/grad_ring/ppermute | solution.py:85
  42.0 1.7 %collective-permute-done.3 = bf16[128,1024]{1,0:T(8,128)(2,1)S(1)} collective-permute-done((bf16[128,1024]{1,0:T(8,128)(2,1)S(1)}, bf16[128,1024]{1,0:T(8,128)(2,1)S(1)}, u32[]{:S(2)}, u32[]{:S(2)}) %collective-permute-start.3) | collective-permute-done | bytes 262176 | tf_op jit(solution)/shard_map/grad_ring/ppermute | solution.py:85
  43.8 0.1 add_convert_fusion.2
  43.8 3.1 %collective-permute-start.4 = (bf16[128,1024]{1,0:T(8,128)(2,1)S(1)}, bf16[128,1024]{1,0:T(8,128)(2,1)S(1)}, u32[]{:S(2)}, u32[]{:S(2)}) collective-permute-start(bf16[128,1024]{1,0:T(8,128)(2,1)S(1)} %add_convert_fusion.2), channel_id=1, source_target_pairs={{0,2},{2,4},{4,6},{6,8},{8,10},{10,12},{12,14},{14,0},{1,15},{3,1}... | collective-permute-start | bytes 786440 | tf_op jit(solution)/shard_map/grad_ring/ppermute | solution.py:85
  47.0 2.4 %collective-permute-done.6 = bf16[128,1024]{1,0:T(8,128)(2,1)S(1)} collective-permute-done((bf16[128,1024]{1,0:T(8,128)(2,1)S(1)}, bf16[128,1024]{1,0:T(8,128)(2,1)S(1)}, u32[]{:S(2)}, u32[]{:S(2)}) %collective-permute-start.6) | collective-permute-done | bytes 262176 | tf_op jit(solution)/shard_map/grad_ring/ppermute | solution.py:85
  49.4 0.1 add_convert_fusion
  49.5 1.9 %collective-permute-start.7 = (bf16[128,1024]{1,0:T(8,128)(2,1)S(1)}, bf16[128,1024]{1,0:T(8,128)(2,1)S(1)}, u32[]{:S(2)}, u32[]{:S(2)}) collective-permute-start(bf16[128,1024]{1,0:T(8,128)(2,1)S(1)} %add_convert_fusion), channel_id=1, source_target_pairs={{0,14},{2,0},{4,2},{6,4},{8,6},{10,8},{12,10},{14,12},{1,3},{3,5},... | collective-permute-start | bytes 786440 | tf_op jit(solution)/shard_map/grad_ring/ppermute | solution.py:85
  51.4 1.0 collective-permute-done.4
  52.4 6.8 %collective-permute-done.7 = bf16[128,1024]{1,0:T(8,128)(2,1)S(1)} collective-permute-done((bf16[128,1024]{1,0:T(8,128)(2,1)S(1)}, bf16[128,1024]{1,0:T(8,128)(2,1)S(1)}, u32[]{:S(2)}, u32[]{:S(2)}) %collective-permute-start.7) | collective-permute-done | bytes 262176 | tf_op jit(solution)/shard_map/grad_ring/ppermute | solution.py:85
  59.3 1.9 %collective-permute-start.8 = (bf16[64,1024]{1,0:T(8,128)(2,1)S(1)}, bf16[64,1024]{1,0:T(8,128)(2,1)S(1)}, u32[]{:S(2)}, u32[]{:S(2)}) collective-permute-start(bf16[64,1024]{1,0:T(8,128)(2,1)S(1)} %add_convert_fusion.4), channel_id=1, source_target_pairs={{0,16},{16,0},{1,17},{17,1},{2,18},{18,2},{3,19},{19,3},{4,20},{20... | collective-permute-start | bytes 393224 | tf_op jit(solution)/shard_map/grad_pair/ppermute | solution.py:94
  61.2 3.8 %collective-permute-done.8 = bf16[64,1024]{1,0:T(8,128)(2,1)S(1)} collective-permute-done((bf16[64,1024]{1,0:T(8,128)(2,1)S(1)}, bf16[64,1024]{1,0:T(8,128)(2,1)S(1)}, u32[]{:S(2)}, u32[]{:S(2)}) %collective-permute-start.8) | collective-permute-done | bytes 131104 | tf_op jit(solution)/shard_map/grad_pair/ppermute | solution.py:94
  65.0 0.3 fusion.4
  65.3 0.1 reshape.20
  65.5 27.6 %all_to_all.10 = f32[32,2,1024]{2,1,0:T(2,128)S(1)} all-to-all(f32[32,2,1024]{2,1,0:T(2,128)S(1)} %reshape.20), channel_id=1, replica_groups=mesh['xh'=4,'z'=8,'xl'=2,'y'=8,'core'=2] {'xh','z'}, dimensions={0} | all-to-all | bytes 524288 | tf_op jit(solution)/shard_map/replica_sum/all_to_all | solution.py:107
  93.0 0.1 reduce_sum.9
  93.1 0.6 fusion.6
  93.8 17.6 %all_to_all.11 = bf16[32,16,128]{2,1,0:T(8,128)(2,1)S(1)} all-to-all(bf16[32,16,128]{2,1,0:T(8,128)(2,1)S(1)} %broadcast_in_dim.8), channel_id=1, replica_groups=mesh['xh'=4,'z'=8,'xl'=2,'y'=8,'core'=2] {'xh','z'}, dimensions={0} | all-to-all | bytes 262144 | tf_op jit(solution)/shard_map/row_gather/all_to_all | solution.py:116
  111.4 0.7 reshape.21
  (15 shorter events, 0.1 us)
Async XLA Ops:
  2.1 19.1 %collective-permute-start = (bf16[256,3072]{1,0:T(8,128)(2,1)S(1)}, bf16[256,3072]{1,0:T(8,128)(2,1)S(1)}, u32[]{:S(2)}, u32[]{:S(2)}) collective-permute-start(bf16[256,3072]{1,0:T(8,128)(2,1)S(1)} %pad_maximum_fusion.refs_1_), channel_id=1, source_target_pairs={{0,1},{1,0},{2,3},{3,2},{4,5},{5,4},{6,7},{7,6},{8,9},{9,8},{10,11... | collective-permute-start | bytes 4718600 | tf_op jit(solution)/shard_map/core_swap/ppermute | solution.py:75
  22.4 9.3 %collective-permute-start.1 = (bf16[128,1024]{1,0:T(8,128)(2,1)S(1)}, bf16[128,1024]{1,0:T(8,128)(2,1)S(1)}, u32[]{:S(2)}, u32[]{:S(2)}) collective-permute-start(bf16[128,1024]{1,0:T(8,128)(2,1)S(1)} %get-tuple-element.20), channel_id=1, source_target_pairs={{0,4},{2,6},{4,8},{6,10},{8,12},{10,14},{12,0},{14,2},{1,13},{3,15... | collective-permute-start | bytes 786440 | tf_op jit(solution)/shard_map/grad_ring/ppermute | solution.py:85
  24.3 12.0 %collective-permute-start.2 = (bf16[128,1024]{1,0:T(8,128)(2,1)S(1)}, bf16[128,1024]{1,0:T(8,128)(2,1)S(1)}, u32[]{:S(2)}, u32[]{:S(2)}) collective-permute-start(bf16[128,1024]{1,0:T(8,128)(2,1)S(1)} %get-tuple-element.21), channel_id=1, source_target_pairs={{0,2},{2,4},{4,6},{6,8},{8,10},{10,12},{12,14},{14,0},{1,15},{3,1}... | collective-permute-start | bytes 786440 | tf_op jit(solution)/shard_map/grad_ring/ppermute | solution.py:85
  26.2 12.3 %collective-permute-start.5 = (bf16[128,1024]{1,0:T(8,128)(2,1)S(1)}, bf16[128,1024]{1,0:T(8,128)(2,1)S(1)}, u32[]{:S(2)}, u32[]{:S(2)}) collective-permute-start(bf16[128,1024]{1,0:T(8,128)(2,1)S(1)} %get-tuple-element.24), channel_id=1, source_target_pairs={{0,14},{2,0},{4,2},{6,4},{8,6},{10,8},{12,10},{14,12},{1,3},{3,5},... | collective-permute-start | bytes 786440 | tf_op jit(solution)/shard_map/grad_ring/ppermute | solution.py:85
  36.5 28.6 %copy-start = (f32[1,64,1024]{2,1,0:T(8,128)S(1)}, f32[1,64,1024]{2,1,0:T(8,128)}, u32[]{:S(2)}) copy-start(f32[1,64,1024]{2,1,0:T(8,128)} %param.11) | copy-start | bytes 786436
  36.5 28.5 %copy-start.1 = (f32[1,64,1024]{2,1,0:T(8,128)S(1)}, f32[1,64,1024]{2,1,0:T(8,128)}, u32[]{:S(2)}) copy-start(f32[1,64,1024]{2,1,0:T(8,128)} %param.10) | copy-start | bytes 786436
  36.5 28.5 %copy-start.2 = (f32[1,64,1024]{2,1,0:T(8,128)S(1)}, f32[1,64,1024]{2,1,0:T(8,128)}, u32[]{:S(2)}) copy-start(f32[1,64,1024]{2,1,0:T(8,128)} %param.9) | copy-start | bytes 786436
  36.5 7.2 %collective-permute-start.3 = (bf16[128,1024]{1,0:T(8,128)(2,1)S(1)}, bf16[128,1024]{1,0:T(8,128)(2,1)S(1)}, u32[]{:S(2)}, u32[]{:S(2)}) collective-permute-start(bf16[128,1024]{1,0:T(8,128)(2,1)S(1)} %add_convert_fusion.3), channel_id=1, source_target_pairs={{0,2},{2,4},{4,6},{6,8},{8,10},{10,12},{12,14},{14,0},{1,15},{3,1}... | collective-permute-start | bytes 786440 | tf_op jit(solution)/shard_map/grad_ring/ppermute | solution.py:85
  38.7 10.7 %collective-permute-start.6 = (bf16[128,1024]{1,0:T(8,128)(2,1)S(1)}, bf16[128,1024]{1,0:T(8,128)(2,1)S(1)}, u32[]{:S(2)}, u32[]{:S(2)}) collective-permute-start(bf16[128,1024]{1,0:T(8,128)(2,1)S(1)} %add_convert_fusion.1), channel_id=1, source_target_pairs={{0,14},{2,0},{4,2},{6,4},{8,6},{10,8},{12,10},{14,12},{1,3},{3,5},... | collective-permute-start | bytes 786440 | tf_op jit(solution)/shard_map/grad_ring/ppermute | solution.py:85
  43.8 8.6 %collective-permute-start.4 = (bf16[128,1024]{1,0:T(8,128)(2,1)S(1)}, bf16[128,1024]{1,0:T(8,128)(2,1)S(1)}, u32[]{:S(2)}, u32[]{:S(2)}) collective-permute-start(bf16[128,1024]{1,0:T(8,128)(2,1)S(1)} %add_convert_fusion.2), channel_id=1, source_target_pairs={{0,2},{2,4},{4,6},{6,8},{8,10},{10,12},{12,14},{14,0},{1,15},{3,1}... | collective-permute-start | bytes 786440 | tf_op jit(solution)/shard_map/grad_ring/ppermute | solution.py:85
  49.5 9.8 %collective-permute-start.7 = (bf16[128,1024]{1,0:T(8,128)(2,1)S(1)}, bf16[128,1024]{1,0:T(8,128)(2,1)S(1)}, u32[]{:S(2)}, u32[]{:S(2)}) collective-permute-start(bf16[128,1024]{1,0:T(8,128)(2,1)S(1)} %add_convert_fusion), channel_id=1, source_target_pairs={{0,14},{2,0},{4,2},{6,4},{8,6},{10,8},{12,10},{14,12},{1,3},{3,5},... | collective-permute-start | bytes 786440 | tf_op jit(solution)/shard_map/grad_ring/ppermute | solution.py:85
  59.3 33.8 %copy-start.3 = (f32[2,1024]{1,0:T(2,128)S(1)}, f32[2,1024]{1,0:T(2,128)}, u32[]{:S(2)}) copy-start(f32[2,1024]{1,0:T(2,128)} %param.12) | copy-start | bytes 24580
  59.3 33.8 %copy-start.4 = (f32[2,1024]{1,0:T(2,128)S(1)}, f32[2,1024]{1,0:T(2,128)}, u32[]{:S(2)}) copy-start(f32[2,1024]{1,0:T(2,128)} %param.13) | copy-start | bytes 24580
  59.3 5.7 %collective-permute-start.8 = (bf16[64,1024]{1,0:T(8,128)(2,1)S(1)}, bf16[64,1024]{1,0:T(8,128)(2,1)S(1)}, u32[]{:S(2)}, u32[]{:S(2)}) collective-permute-start(bf16[64,1024]{1,0:T(8,128)(2,1)S(1)} %add_convert_fusion.4), channel_id=1, source_target_pairs={{0,16},{16,0},{1,17},{17,1},{2,18},{18,2},{3,19},{19,3},{4,20},{20... | collective-permute-start | bytes 393224 | tf_op jit(solution)/shard_map/grad_pair/ppermute | solution.py:94

commit v9 on v8

--- a/solution.py
+++ b/solution.py
@@ -78,18 +78,17 @@
         early = product((-3, 4, 3), bf16, place, [peer], cols, mine)
         late = product((-2, 2, 1, -1, 0), bf16, place, [here, peer], cols)
     with jax.named_scope("grad_ring"):
-
         def hop(block, k):
             ends = [(2 * y, 2 * ((y + k) % RING)) for y in range(RING)]
             ends += [(2 * y + 1, 2 * ((y - k) % RING) + 1) for y in range(RING)]
             return lax.ppermute(block, ("y", "core"), ends)
 
         back_3, four, ahead_3 = hop(early[0], -1), hop(early[1], 2), hop(early[2], 1)
+        ahead_1 = hop(late[2], 1)
         back_2 = hop(add(late[0], back_3).astype(bf16), -1)
-        ahead_2 = hop(add(late[1], four, ahead_3).astype(bf16), 1)
-        ahead_1 = hop(add(late[2], ahead_2).astype(bf16), 1)
+        ahead_2 = hop(add(late[1], four, ahead_3).astype(bf16), 2)
         back_1 = hop(add(late[3], back_2).astype(bf16), -1)
-        terms = (late[4], ahead_1, back_1)
+        terms = (late[4], ahead_1, ahead_2, back_1)
     with jax.named_scope("grad_pair"):
         other = lax.ppermute(add(*(t[rows:] for t in terms)).astype(bf16), "xl", swap)
         grad = add(other, *(t[:rows] for t in terms))

time: 113 us -> 107 us (0.947)
  waiting for transfers between devices: 22.2 us -> 17 us
  blocking collectives: 45.1 us -> 42.7 us
  starting transfers between devices: 35.6 us -> 37.3 us
    ppermute x7, waiting for transfers between devices: 16.7 us -> 10.6 us  [hop(): return lax.ppermute(block, ('y', 'core'), ends)]
    all_to_all x1, blocking collectives: 27.6 us -> 25 us  [shards(): lax.all_to_all(inner_new.reshape(replicas, own, cols), REP, 0, 0, tiled=T...]
    ppermute x7, starting transfers between devices: 17.7 us -> 19.3 us  [hop(): return lax.ppermute(block, ('y', 'core'), ends)]
  transfers between devices with their start and end apart: 9 -> 9, of which waited for: 7 -> 6; matrix products, arithmetic and copies ran while one was open for 0% -> 0% of each run, Pallas kernels for 3% -> 3%
where the time goes in v9:
time: 107 us; the launch traced here: 106 us
  blocking collectives  42.7 us (40%)
  starting transfers between devices  37.3 us (35%)
  waiting for transfers between devices  17 us (16%)
  Pallas kernels  4.37 us (4%)
  other arithmetic  2.9 us (3%)
    all_to_all x1, blocking collectives, shards(): lax.all_to_all(inner_new.reshape(replicas, own, cols), REP, 0, 0, tiled=T...  25 us
    ppermute x7, starting transfers between devices, hop(): return lax.ppermute(block, ('y', 'core'), ends)  19.3 us
    all_to_all x1, blocking collectives, shards(): lax.all_to_all(copies, REP, 0, 0, tiled=True).reshape(rows, cols)  17.7 us
    ppermute x1, starting transfers between devices, shards(): peer = lax.ppermute(here, 'core', swap)  16.1 us
    ppermute x7, waiting for transfers between devices, hop(): return lax.ppermute(block, ('y', 'core'), ends)  10.6 us
    ppermute x1, waiting for transfers between devices, shards(): lax.ppermute(add(*(t[rows:] for t in terms)).astype(bf16), 'xl', swap)  4.69 us
    pallas_call x3, Pallas kernels, product(): pl.pallas_call(lambda *refs: product_kernel(offsets, len(sources), wide -...  4.37 us
  transfers between devices with their start and end apart: 9, of which 6 were waited for; matrix products, arithmetic and copies ran while one was open for 0% of the time, Pallas kernels for 3%

profile of v9, /device:TPU:1, one launch (start us, length us, event | category | flops | bytes accessed | tf_op | source)
XLA Modules:
  0.0 106.1 jit_solution(17373570144271622676)
XLA Ops:
  0.6 1.5 %pad_maximum_fusion.refs_1_ = bf16[256,3072]{1,0:T(8,128)(2,1)S(1)} fusion(bf16[256,1024]{1,0:T(8,128)(2,1)} %bitcast.16, bf16[256,2048]{1,0:T(8,128)(2,1)} %bitcast.15), kind=kLoop, calls=%fused_computation | loop fusion | flops 3145728 | bytes 3145728 | tf_op jit(solution)/shard_map/core_swap/concatenate | solution.py:74
  2.1 16.1 %collective-permute-start = (bf16[256,3072]{1,0:T(8,128)(2,1)S(1)}, bf16[256,3072]{1,0:T(8,128)(2,1)S(1)}, u32[]{:S(2)}, u32[]{:S(2)}) collective-permute-start(bf16[256,3072]{1,0:T(8,128)(2,1)S(1)} %pad_maximum_fusion.refs_1_), channel_id=1, source_target_pairs={{0,1},{1,0},{2,3},{3,2},{4,5},{5,4},{6,7},{7,6},{8,9},{9,8},{10,11... | collective-permute-start | bytes 4718600 | tf_op jit(solution)/shard_map/core_swap/ppermute | solution.py:75
  18.2 0.1 pad_add_fusion.refs_0_
  18.3 1.1 %grad_product.4 = (f32[128,1024]{1,0:T(8,128)S(1)}, f32[128,1024]{1,0:T(8,128)S(1)}, f32[128,1024]{1,0:T(8,128)S(1)}) custom-call(s32[3]{0:T(128)S(1)} %pad_add_fusion.refs_0_, bf16[256,3072]{1,0:T(8,128)(2,1)S(1)} %pad_maximum_fusion.refs_1_), custom_call_target="tpu_custom_call" | custom-call | flops 201326592 | bytes 1572864 | tf_op jit(solution)/shard_map/grad_product/pallas_call | solution.py:47
  19.4 1.8 %collective-permute-done.refs_2_.refs_1_ = bf16[256,3072]{1,0:T(8,128)(2,1)S(1)} collective-permute-done((bf16[256,3072]{1,0:T(8,128)(2,1)S(1)}, bf16[256,3072]{1,0:T(8,128)(2,1)S(1)}, u32[]{:S(2)}, u32[]{:S(2)}) %collective-permute-start) | collective-permute-done | bytes 1572896 | tf_op jit(solution)/shard_map/core_swap/ppermute | solution.py:75
  21.2 1.2 %grad_product.5 = (bf16[128,1024]{1,0:T(8,128)(2,1)S(1)}, bf16[128,1024]{1,0:T(8,128)(2,1)S(1)}, bf16[128,1024]{1,0:T(8,128)(2,1)S(1)}) custom-call(s32[3]{0:T(128)S(1)} %pad_add_fusion.refs_0_, bf16[256,3072]{1,0:T(8,128)(2,1)S(1)} %collective-permute-done.refs_2_.refs_1_, f32[128,1024]{1,0:T(8,128)S(1)} %get-tuple-element.17.refs_2_, ...), custom_call_target="tpu_custom_call" | custom-call | flops 201326592 | bytes 1572864 | tf_op jit(solution)/shard_map/grad_product/pallas_call | solution.py:47
  22.4 1.9 %collective-permute-start.5 = (bf16[128,1024]{1,0:T(8,128)(2,1)S(1)}, bf16[128,1024]{1,0:T(8,128)(2,1)S(1)}, u32[]{:S(2)}, u32[]{:S(2)}) collective-permute-start(bf16[128,1024]{1,0:T(8,128)(2,1)S(1)} %get-tuple-element.24), channel_id=1, source_target_pairs={{0,14},{2,0},{4,2},{6,4},{8,6},{10,8},{12,10},{14,12},{1,3},{3,5},... | collective-permute-start | bytes 786440 | tf_op jit(solution)/shard_map/grad_ring/ppermute | solution.py:84
  24.3 1.9 %collective-permute-start.2 = (bf16[128,1024]{1,0:T(8,128)(2,1)S(1)}, bf16[128,1024]{1,0:T(8,128)(2,1)S(1)}, u32[]{:S(2)}, u32[]{:S(2)}) collective-permute-start(bf16[128,1024]{1,0:T(8,128)(2,1)S(1)} %get-tuple-element.20), channel_id=1, source_target_pairs={{0,4},{2,6},{4,8},{6,10},{8,12},{10,14},{12,0},{14,2},{1,13},{3,15... | collective-permute-start | bytes 786440 | tf_op jit(solution)/shard_map/grad_ring/ppermute | solution.py:84
  26.2 4.6 %collective-permute-start.3 = (bf16[128,1024]{1,0:T(8,128)(2,1)S(1)}, bf16[128,1024]{1,0:T(8,128)(2,1)S(1)}, u32[]{:S(2)}, u32[]{:S(2)}) collective-permute-start(bf16[128,1024]{1,0:T(8,128)(2,1)S(1)} %get-tuple-element.21), channel_id=1, source_target_pairs={{0,2},{2,4},{4,6},{6,8},{8,10},{10,12},{12,14},{14,0},{1,15},{3,1}... | collective-permute-start | bytes 786440 | tf_op jit(solution)/shard_map/grad_ring/ppermute | solution.py:84
  30.8 2.1 %grad_product.3 = (bf16[128,1024]{1,0:T(8,128)(2,1)S(1)}, bf16[128,1024]{1,0:T(8,128)(2,1)S(1)}, bf16[128,1024]{1,0:T(8,128)(2,1)S(1)}, bf16[128,1024]{1,0:T(8,128)(2,1)S(1)}, bf16[128,1024]{1,0:T(8,128)(2,1)S(1)}) custom-call(s32[3]{0:T(128)S(1)} %pad_add_fusion.refs_0_, bf16[256,3072]{1,0:T(8,128)(2,1)S(1)} %pad_maximum_fusion.refs_1_, ...), custom_call_target="tpu_custom_call" | custom-call | flops 671088640 | bytes 3145728 | tf_op jit(solution)/shard_map/grad_product/pallas_call | solution.py:47
  32.9 0.0 copy-start
  32.9 0.1 add_convert_fusion.1
  33.0 3.2 %collective-permute-start.6 = (bf16[128,1024]{1,0:T(8,128)(2,1)S(1)}, bf16[128,1024]{1,0:T(8,128)(2,1)S(1)}, u32[]{:S(2)}, u32[]{:S(2)}) collective-permute-start(bf16[128,1024]{1,0:T(8,128)(2,1)S(1)} %add_convert_fusion.1), channel_id=1, source_target_pairs={{0,14},{2,0},{4,2},{6,4},{8,6},{10,8},{12,10},{14,12},{1,3},{3,5},... | collective-permute-start | bytes 786440 | tf_op jit(solution)/shard_map/grad_ring/ppermute | solution.py:84
  36.3 3.4 %collective-permute-start.1 = (bf16[128,1024]{1,0:T(8,128)(2,1)S(1)}, bf16[128,1024]{1,0:T(8,128)(2,1)S(1)}, u32[]{:S(2)}, u32[]{:S(2)}) collective-permute-start(bf16[128,1024]{1,0:T(8,128)(2,1)S(1)} %get-tuple-element.15), channel_id=1, source_target_pairs={{0,2},{2,4},{4,6},{6,8},{8,10},{10,12},{12,14},{14,0},{1,15},{3,1}... | collective-permute-start | bytes 786440 | tf_op jit(solution)/shard_map/grad_ring/ppermute | solution.py:84
  39.7 0.1 add_convert_fusion.2
  39.8 1.9 %collective-permute-start.4 = (bf16[128,1024]{1,0:T(8,128)(2,1)S(1)}, bf16[128,1024]{1,0:T(8,128)(2,1)S(1)}, u32[]{:S(2)}, u32[]{:S(2)}) collective-permute-start(bf16[128,1024]{1,0:T(8,128)(2,1)S(1)} %add_convert_fusion.2), channel_id=1, source_target_pairs={{0,4},{2,6},{4,8},{6,10},{8,12},{10,14},{12,0},{14,2},{1,13},{3,15... | collective-permute-start | bytes 786440 | tf_op jit(solution)/shard_map/grad_ring/ppermute | solution.py:84
  41.7 1.1 %collective-permute-done.6 = bf16[128,1024]{1,0:T(8,128)(2,1)S(1)} collective-permute-done((bf16[128,1024]{1,0:T(8,128)(2,1)S(1)}, bf16[128,1024]{1,0:T(8,128)(2,1)S(1)}, u32[]{:S(2)}, u32[]{:S(2)}) %collective-permute-start.6) | collective-permute-done | bytes 262176 | tf_op jit(solution)/shard_map/grad_ring/ppermute | solution.py:84
  42.9 0.1 add_convert_fusion
  42.9 2.3 %collective-permute-start.7 = (bf16[128,1024]{1,0:T(8,128)(2,1)S(1)}, bf16[128,1024]{1,0:T(8,128)(2,1)S(1)}, u32[]{:S(2)}, u32[]{:S(2)}) collective-permute-start(bf16[128,1024]{1,0:T(8,128)(2,1)S(1)} %add_convert_fusion), channel_id=1, source_target_pairs={{0,14},{2,0},{4,2},{6,4},{8,6},{10,8},{12,10},{14,12},{1,3},{3,5},... | collective-permute-start | bytes 786440 | tf_op jit(solution)/shard_map/grad_ring/ppermute | solution.py:84
  45.3 0.1 collective-permute-done.1
  45.4 6.8 %collective-permute-done.4 = bf16[128,1024]{1,0:T(8,128)(2,1)S(1)} collective-permute-done((bf16[128,1024]{1,0:T(8,128)(2,1)S(1)}, bf16[128,1024]{1,0:T(8,128)(2,1)S(1)}, u32[]{:S(2)}, u32[]{:S(2)}) %collective-permute-start.4) | collective-permute-done | bytes 262176 | tf_op jit(solution)/shard_map/grad_ring/ppermute | solution.py:84
  52.2 2.6 %collective-permute-done.7 = bf16[128,1024]{1,0:T(8,128)(2,1)S(1)} collective-permute-done((bf16[128,1024]{1,0:T(8,128)(2,1)S(1)}, bf16[128,1024]{1,0:T(8,128)(2,1)S(1)}, u32[]{:S(2)}, u32[]{:S(2)}) %collective-permute-start.7) | collective-permute-done | bytes 262176 | tf_op jit(solution)/shard_map/grad_ring/ppermute | solution.py:84
  54.7 0.1 add_convert_fusion.3
  54.8 1.9 %collective-permute-start.8 = (bf16[64,1024]{1,0:T(8,128)(2,1)S(1)}, bf16[64,1024]{1,0:T(8,128)(2,1)S(1)}, u32[]{:S(2)}, u32[]{:S(2)}) collective-permute-start(bf16[64,1024]{1,0:T(8,128)(2,1)S(1)} %add_convert_fusion.3), channel_id=1, source_target_pairs={{0,16},{16,0},{1,17},{17,1},{2,18},{18,2},{3,19},{19,3},{4,20},{20... | collective-permute-start | bytes 393224 | tf_op jit(solution)/shard_map/grad_pair/ppermute | solution.py:93
  56.8 4.7 %collective-permute-done.8 = bf16[64,1024]{1,0:T(8,128)(2,1)S(1)} collective-permute-done((bf16[64,1024]{1,0:T(8,128)(2,1)S(1)}, bf16[64,1024]{1,0:T(8,128)(2,1)S(1)}, u32[]{:S(2)}, u32[]{:S(2)}) %collective-permute-start.8) | collective-permute-done | bytes 131104 | tf_op jit(solution)/shard_map/grad_pair/ppermute | solution.py:93
  61.5 0.3 fusion.4
  61.7 0.1 reshape.20
  61.9 25.0 %all_to_all.10 = f32[32,2,1024]{2,1,0:T(2,128)S(1)} all-to-all(f32[32,2,1024]{2,1,0:T(2,128)S(1)} %reshape.20), channel_id=1, replica_groups=mesh['xh'=4,'z'=8,'xl'=2,'y'=8,'core'=2] {'xh','z'}, dimensions={0} | all-to-all | bytes 524288 | tf_op jit(solution)/shard_map/replica_sum/all_to_all | solution.py:106
  86.9 0.1 reduce_sum.9
  87.0 0.6 fusion.6
  87.7 17.7 %all_to_all.11 = bf16[32,16,128]{2,1,0:T(8,128)(2,1)S(1)} all-to-all(bf16[32,16,128]{2,1,0:T(8,128)(2,1)S(1)} %broadcast_in_dim.8), channel_id=1, replica_groups=mesh['xh'=4,'z'=8,'xl'=2,'y'=8,'core'=2] {'xh','z'}, dimensions={0} | all-to-all | bytes 262144 | tf_op jit(solution)/shard_map/row_gather/all_to_all | solution.py:115
  105.4 0.7 reshape.21
  (14 shorter events, 0.1 us)
Async XLA Ops:
  2.1 19.1 %collective-permute-start = (bf16[256,3072]{1,0:T(8,128)(2,1)S(1)}, bf16[256,3072]{1,0:T(8,128)(2,1)S(1)}, u32[]{:S(2)}, u32[]{:S(2)}) collective-permute-start(bf16[256,3072]{1,0:T(8,128)(2,1)S(1)} %pad_maximum_fusion.refs_1_), channel_id=1, source_target_pairs={{0,1},{1,0},{2,3},{3,2},{4,5},{5,4},{6,7},{7,6},{8,9},{9,8},{10,11... | collective-permute-start | bytes 4718600 | tf_op jit(solution)/shard_map/core_swap/ppermute | solution.py:75
  22.4 10.5 %collective-permute-start.5 = (bf16[128,1024]{1,0:T(8,128)(2,1)S(1)}, bf16[128,1024]{1,0:T(8,128)(2,1)S(1)}, u32[]{:S(2)}, u32[]{:S(2)}) collective-permute-start(bf16[128,1024]{1,0:T(8,128)(2,1)S(1)} %get-tuple-element.24), channel_id=1, source_target_pairs={{0,14},{2,0},{4,2},{6,4},{8,6},{10,8},{12,10},{14,12},{1,3},{3,5},... | collective-permute-start | bytes 786440 | tf_op jit(solution)/shard_map/grad_ring/ppermute | solution.py:84
  24.3 15.3 %collective-permute-start.2 = (bf16[128,1024]{1,0:T(8,128)(2,1)S(1)}, bf16[128,1024]{1,0:T(8,128)(2,1)S(1)}, u32[]{:S(2)}, u32[]{:S(2)}) collective-permute-start(bf16[128,1024]{1,0:T(8,128)(2,1)S(1)} %get-tuple-element.20), channel_id=1, source_target_pairs={{0,4},{2,6},{4,8},{6,10},{8,12},{10,14},{12,0},{14,2},{1,13},{3,15... | collective-permute-start | bytes 786440 | tf_op jit(solution)/shard_map/grad_ring/ppermute | solution.py:84
  26.2 13.4 %collective-permute-start.3 = (bf16[128,1024]{1,0:T(8,128)(2,1)S(1)}, bf16[128,1024]{1,0:T(8,128)(2,1)S(1)}, u32[]{:S(2)}, u32[]{:S(2)}) collective-permute-start(bf16[128,1024]{1,0:T(8,128)(2,1)S(1)} %get-tuple-element.21), channel_id=1, source_target_pairs={{0,2},{2,4},{4,6},{6,8},{8,10},{10,12},{12,14},{14,0},{1,15},{3,1}... | collective-permute-start | bytes 786440 | tf_op jit(solution)/shard_map/grad_ring/ppermute | solution.py:84
  32.9 28.5 %copy-start = (f32[1,64,1024]{2,1,0:T(8,128)S(1)}, f32[1,64,1024]{2,1,0:T(8,128)}, u32[]{:S(2)}) copy-start(f32[1,64,1024]{2,1,0:T(8,128)} %param.11) | copy-start | bytes 786436
  32.9 28.5 %copy-start.1 = (f32[1,64,1024]{2,1,0:T(8,128)S(1)}, f32[1,64,1024]{2,1,0:T(8,128)}, u32[]{:S(2)}) copy-start(f32[1,64,1024]{2,1,0:T(8,128)} %param.10) | copy-start | bytes 786436
  32.9 28.5 %copy-start.2 = (f32[1,64,1024]{2,1,0:T(8,128)S(1)}, f32[1,64,1024]{2,1,0:T(8,128)}, u32[]{:S(2)}) copy-start(f32[1,64,1024]{2,1,0:T(8,128)} %param.9) | copy-start | bytes 786436
  33.0 9.8 %collective-permute-start.6 = (bf16[128,1024]{1,0:T(8,128)(2,1)S(1)}, bf16[128,1024]{1,0:T(8,128)(2,1)S(1)}, u32[]{:S(2)}, u32[]{:S(2)}) collective-permute-start(bf16[128,1024]{1,0:T(8,128)(2,1)S(1)} %add_convert_fusion.1), channel_id=1, source_target_pairs={{0,14},{2,0},{4,2},{6,4},{8,6},{10,8},{12,10},{14,12},{1,3},{3,5},... | collective-permute-start | bytes 786440 | tf_op jit(solution)/shard_map/grad_ring/ppermute | solution.py:84
  36.3 9.1 %collective-permute-start.1 = (bf16[128,1024]{1,0:T(8,128)(2,1)S(1)}, bf16[128,1024]{1,0:T(8,128)(2,1)S(1)}, u32[]{:S(2)}, u32[]{:S(2)}) collective-permute-start(bf16[128,1024]{1,0:T(8,128)(2,1)S(1)} %get-tuple-element.15), channel_id=1, source_target_pairs={{0,2},{2,4},{4,6},{6,8},{8,10},{10,12},{12,14},{14,0},{1,15},{3,1}... | collective-permute-start | bytes 786440 | tf_op jit(solution)/shard_map/grad_ring/ppermute | solution.py:84
  39.8 12.3 %collective-permute-start.4 = (bf16[128,1024]{1,0:T(8,128)(2,1)S(1)}, bf16[128,1024]{1,0:T(8,128)(2,1)S(1)}, u32[]{:S(2)}, u32[]{:S(2)}) collective-permute-start(bf16[128,1024]{1,0:T(8,128)(2,1)S(1)} %add_convert_fusion.2), channel_id=1, source_target_pairs={{0,4},{2,6},{4,8},{6,10},{8,12},{10,14},{12,0},{14,2},{1,13},{3,15... | collective-permute-start | bytes 786440 | tf_op jit(solution)/shard_map/grad_ring/ppermute | solution.py:84
  42.9 11.8 %collective-permute-start.7 = (bf16[128,1024]{1,0:T(8,128)(2,1)S(1)}, bf16[128,1024]{1,0:T(8,128)(2,1)S(1)}, u32[]{:S(2)}, u32[]{:S(2)}) collective-permute-start(bf16[128,1024]{1,0:T(8,128)(2,1)S(1)} %add_convert_fusion), channel_id=1, source_target_pairs={{0,14},{2,0},{4,2},{6,4},{8,6},{10,8},{12,10},{14,12},{1,3},{3,5},... | collective-permute-start | bytes 786440 | tf_op jit(solution)/shard_map/grad_ring/ppermute | solution.py:84
  54.8 32.2 %copy-start.3 = (f32[2,1024]{1,0:T(2,128)S(1)}, f32[2,1024]{1,0:T(2,128)}, u32[]{:S(2)}) copy-start(f32[2,1024]{1,0:T(2,128)} %param.12) | copy-start | bytes 24580
  54.8 32.2 %copy-start.4 = (f32[2,1024]{1,0:T(2,128)S(1)}, f32[2,1024]{1,0:T(2,128)}, u32[]{:S(2)}) copy-start(f32[2,1024]{1,0:T(2,128)} %param.13) | copy-start | bytes 24580
  54.8 6.6 %collective-permute-start.8 = (bf16[64,1024]{1,0:T(8,128)(2,1)S(1)}, bf16[64,1024]{1,0:T(8,128)(2,1)S(1)}, u32[]{:S(2)}, u32[]{:S(2)}) collective-permute-start(bf16[64,1024]{1,0:T(8,128)(2,1)S(1)} %add_convert_fusion.3), channel_id=1, source_target_pairs={{0,16},{16,0},{1,17},{17,1},{2,18},{18,2},{3,19},{19,3},{4,20},{20... | collective-permute-start | bytes 393224 | tf_op jit(solution)/shard_map/grad_pair/ppermute | solution.py:93

commit v10 on v9

--- a/solution.py
+++ b/solution.py
@@ -83,15 +83,22 @@
             ends += [(2 * y + 1, 2 * ((y - k) % RING) + 1) for y in range(RING)]
             return lax.ppermute(block, ("y", "core"), ends)
 
+        def across(block, k):
+            ends = []
+            for xl in range(2):
+                ends += [(16 * xl + 2 * y, 16 * (1 - xl) + 2 * ((y + k) % RING)) for y in range(RING)]
+                ends += [(16 * xl + 2 * y + 1, 16 * (1 - xl) + 2 * ((y - k) % RING) + 1) for y in range(RING)]
+            return lax.ppermute(block, FSDP, ends)
+
         back_3, four, ahead_3 = hop(early[0], -1), hop(early[1], 2), hop(early[2], 1)
         ahead_1 = hop(late[2], 1)
         back_2 = hop(add(late[0], back_3).astype(bf16), -1)
-        ahead_2 = hop(add(late[1], four, ahead_3).astype(bf16), 2)
-        back_1 = hop(add(late[3], back_2).astype(bf16), -1)
-        terms = (late[4], ahead_1, ahead_2, back_1)
-    with jax.named_scope("grad_pair"):
-        other = lax.ppermute(add(*(t[rows:] for t in terms)).astype(bf16), "xl", swap)
-        grad = add(other, *(t[:rows] for t in terms))
+        ahead_2 = add(late[1], four, ahead_3).astype(bf16)
+        back_1 = add(late[3], back_2).astype(bf16)
+        ahead_2, ahead_2_far = hop(ahead_2[:rows], 2), across(ahead_2[rows:], 2)
+        back_1, back_1_far = hop(back_1[:rows], -1), across(back_1[rows:], -1)
+        far = across(add(late[4][rows:], ahead_1[rows:]).astype(bf16), 0)
+        grad = add(late[4][:rows], ahead_1[:rows], ahead_2, back_1, ahead_2_far, back_1_far, far)
 
     with jax.named_scope("adamw"):
         first = 0.9 * first_moment[0] + 0.1 * grad

time: 107 us -> 106 us (level)
  the two profiles are of different devices: /device:TPU:1 before, /device:TPU:2 now
where the time goes in v10:
time: 106 us; the launch traced here: 105 us
  starting transfers between devices  46.1 us (43%)
  blocking collectives  45.1 us (43%)
  waiting for transfers between devices  4.63 us (4%)
  Pallas kernels  4.41 us (4%)
  other arithmetic  2.9 us (3%)
    all_to_all x1, blocking collectives, shards(): lax.all_to_all(inner_new.reshape(replicas, own, cols), REP, 0, 0, tiled=T...  28.2 us
    ppermute x7, starting transfers between devices, hop(): return lax.ppermute(block, ('y', 'core'), ends)  25 us
    ppermute x3, starting transfers between devices, across(): return lax.ppermute(block, FSDP, ends)  19.1 us
    all_to_all x1, blocking collectives, shards(): lax.all_to_all(copies, REP, 0, 0, tiled=True).reshape(rows, cols)  16.9 us
    pallas_call x3, Pallas kernels, product(): pl.pallas_call(lambda *refs: product_kernel(offsets, len(sources), wide -...  4.41 us
    ppermute x3, waiting for transfers between devices, across(): return lax.ppermute(block, FSDP, ends)  2.46 us
    ppermute x1, waiting for transfers between devices, shards(): peer = lax.ppermute(here, 'core', swap)  2.14 us
  transfers between devices with their start and end apart: 11, of which 2 were waited for; matrix products, arithmetic and copies ran while one was open for 0% of the time, Pallas kernels for 3%

profile of v10, /device:TPU:2, one launch (start us, length us, event | category | flops | bytes accessed | tf_op | source)
XLA Modules:
  0.0 105.0 jit_solution(14472621270163119821)
XLA Ops:
  0.6 1.5 %pad_maximum_fusion.refs_1_ = bf16[256,3072]{1,0:T(8,128)(2,1)S(1)} fusion(bf16[256,1024]{1,0:T(8,128)(2,1)} %bitcast.16, bf16[256,2048]{1,0:T(8,128)(2,1)} %bitcast.15), kind=kLoop, calls=%fused_computation | loop fusion | flops 3145728 | bytes 3145728 | tf_op jit(solution)/shard_map/core_swap/concatenate | solution.py:74
  2.1 1.9 %collective-permute-start = (bf16[256,3072]{1,0:T(8,128)(2,1)S(1)}, bf16[256,3072]{1,0:T(8,128)(2,1)S(1)}, u32[]{:S(2)}, u32[]{:S(2)}) collective-permute-start(bf16[256,3072]{1,0:T(8,128)(2,1)S(1)} %pad_maximum_fusion.refs_1_), channel_id=1, source_target_pairs={{0,1},{1,0},{2,3},{3,2},{4,5},{5,4},{6,7},{7,6},{8,9},{9,8},{10,11... | collective-permute-start | bytes 4718600 | tf_op jit(solution)/shard_map/core_swap/ppermute | solution.py:75
  4.1 0.1 pad_add_fusion.refs_0_
  4.2 1.1 %grad_product.4 = (f32[128,1024]{1,0:T(8,128)S(1)}, f32[128,1024]{1,0:T(8,128)S(1)}, f32[128,1024]{1,0:T(8,128)S(1)}) custom-call(s32[3]{0:T(128)S(1)} %pad_add_fusion.refs_0_, bf16[256,3072]{1,0:T(8,128)(2,1)S(1)} %pad_maximum_fusion.refs_1_), custom_call_target="tpu_custom_call" | custom-call | flops 201326592 | bytes 1572864 | tf_op jit(solution)/shard_map/grad_product/pallas_call | solution.py:47
  5.3 2.1 %collective-permute-done.refs_2_.refs_1_ = bf16[256,3072]{1,0:T(8,128)(2,1)S(1)} collective-permute-done((bf16[256,3072]{1,0:T(8,128)(2,1)S(1)}, bf16[256,3072]{1,0:T(8,128)(2,1)S(1)}, u32[]{:S(2)}, u32[]{:S(2)}) %collective-permute-start) | collective-permute-done | bytes 1572896 | tf_op jit(solution)/shard_map/core_swap/ppermute | solution.py:75
  7.5 1.2 %grad_product.5 = (bf16[128,1024]{1,0:T(8,128)(2,1)S(1)}, bf16[128,1024]{1,0:T(8,128)(2,1)S(1)}, bf16[128,1024]{1,0:T(8,128)(2,1)S(1)}) custom-call(s32[3]{0:T(128)S(1)} %pad_add_fusion.refs_0_, bf16[256,3072]{1,0:T(8,128)(2,1)S(1)} %collective-permute-done.refs_2_.refs_1_, f32[128,1024]{1,0:T(8,128)S(1)} %get-tuple-element.17.refs_2_, ...), custom_call_target="tpu_custom_call" | custom-call | flops 201326592 | bytes 1572864 | tf_op jit(solution)/shard_map/grad_product/pallas_call | solution.py:47
  8.6 6.2 %collective-permute-start.5 = (bf16[128,1024]{1,0:T(8,128)(2,1)S(1)}, bf16[128,1024]{1,0:T(8,128)(2,1)S(1)}, u32[]{:S(2)}, u32[]{:S(2)}) collective-permute-start(bf16[128,1024]{1,0:T(8,128)(2,1)S(1)} %get-tuple-element.24), channel_id=1, source_target_pairs={{0,14},{2,0},{4,2},{6,4},{8,6},{10,8},{12,10},{14,12},{1,3},{3,5},... | collective-permute-start | bytes 786440 | tf_op jit(solution)/shard_map/grad_ring/ppermute | solution.py:84
  14.8 1.9 %collective-permute-start.2 = (bf16[128,1024]{1,0:T(8,128)(2,1)S(1)}, bf16[128,1024]{1,0:T(8,128)(2,1)S(1)}, u32[]{:S(2)}, u32[]{:S(2)}) collective-permute-start(bf16[128,1024]{1,0:T(8,128)(2,1)S(1)} %get-tuple-element.20), channel_id=1, source_target_pairs={{0,4},{2,6},{4,8},{6,10},{8,12},{10,14},{12,0},{14,2},{1,13},{3,15... | collective-permute-start | bytes 786440 | tf_op jit(solution)/shard_map/grad_ring/ppermute | solution.py:84
  16.7 2.5 %collective-permute-start.3 = (bf16[128,1024]{1,0:T(8,128)(2,1)S(1)}, bf16[128,1024]{1,0:T(8,128)(2,1)S(1)}, u32[]{:S(2)}, u32[]{:S(2)}) collective-permute-start(bf16[128,1024]{1,0:T(8,128)(2,1)S(1)} %get-tuple-element.21), channel_id=1, source_target_pairs={{0,2},{2,4},{4,6},{6,8},{8,10},{10,12},{12,14},{14,0},{1,15},{3,1}... | collective-permute-start | bytes 786440 | tf_op jit(solution)/shard_map/grad_ring/ppermute | solution.py:84
  19.2 2.1 %grad_product.3 = (bf16[128,1024]{1,0:T(8,128)(2,1)S(1)}, bf16[128,1024]{1,0:T(8,128)(2,1)S(1)}, bf16[128,1024]{1,0:T(8,128)(2,1)S(1)}, bf16[128,1024]{1,0:T(8,128)(2,1)S(1)}, bf16[128,1024]{1,0:T(8,128)(2,1)S(1)}) custom-call(s32[3]{0:T(128)S(1)} %pad_add_fusion.refs_0_, bf16[256,3072]{1,0:T(8,128)(2,1)S(1)} %pad_maximum_fusion.refs_1_, ...), custom_call_target="tpu_custom_call" | custom-call | flops 671088640 | bytes 3145728 | tf_op jit(solution)/shard_map/grad_product/pallas_call | solution.py:47
  21.3 4.8 %collective-permute-start.1 = (bf16[128,1024]{1,0:T(8,128)(2,1)S(1)}, bf16[128,1024]{1,0:T(8,128)(2,1)S(1)}, u32[]{:S(2)}, u32[]{:S(2)}) collective-permute-start(bf16[128,1024]{1,0:T(8,128)(2,1)S(1)} %get-tuple-element.15), channel_id=1, source_target_pairs={{0,2},{2,4},{4,6},{6,8},{8,10},{10,12},{12,14},{14,0},{1,15},{3,1}... | collective-permute-start | bytes 786440 | tf_op jit(solution)/shard_map/grad_ring/ppermute | solution.py:84
  26.1 0.1 add_convert_fusion.1
  26.2 2.2 %collective-permute-start.6 = (bf16[128,1024]{1,0:T(8,128)(2,1)S(1)}, bf16[128,1024]{1,0:T(8,128)(2,1)S(1)}, u32[]{:S(2)}, u32[]{:S(2)}) collective-permute-start(bf16[128,1024]{1,0:T(8,128)(2,1)S(1)} %add_convert_fusion.1), channel_id=1, source_target_pairs={{0,14},{2,0},{4,2},{6,4},{8,6},{10,8},{12,10},{14,12},{1,3},{3,5},... | collective-permute-start | bytes 786440 | tf_op jit(solution)/shard_map/grad_ring/ppermute | solution.py:84
  28.5 0.0 copy-start
  28.5 0.0 copy-start.1
  28.5 0.0 copy-start.2
  28.5 0.1 add_convert_fusion.2
  28.7 4.9 %collective-permute-start.4 = (bf16[64,1024]{1,0:T(8,128)(2,1)S(1)}, bf16[64,1024]{1,0:T(8,128)(2,1)S(1)}, u32[]{:S(2)}, u32[]{:S(2)}) collective-permute-start(bf16[64,1024]{1,0:T(8,128)(2,1)S(1)} %get-tuple-element.28), channel_id=1, source_target_pairs={{0,4},{2,6},{4,8},{6,10},{8,12},{10,14},{12,0},{14,2},{1,13},{3,15... | collective-permute-start | bytes 393224 | tf_op jit(solution)/shard_map/grad_ring/ppermute | solution.py:84
  33.5 11.3 %collective-permute-start.8 = (bf16[64,1024]{1,0:T(8,128)(2,1)S(1)}, bf16[64,1024]{1,0:T(8,128)(2,1)S(1)}, u32[]{:S(2)}, u32[]{:S(2)}) collective-permute-start(bf16[64,1024]{1,0:T(8,128)(2,1)S(1)} %get-tuple-element.29), channel_id=1, source_target_pairs={{0,20},{2,22},{4,24},{6,26},{8,28},{10,30},{12,16},{14,18},{1,29},... | collective-permute-start | bytes 393224 | tf_op jit(solution)/shard_map/grad_ring/ppermute | solution.py:91
  44.9 2.0 %collective-permute-start.10 = (bf16[64,1024]{1,0:T(8,128)(2,1)S(1)}, bf16[64,1024]{1,0:T(8,128)(2,1)S(1)}, u32[]{:S(2)}, u32[]{:S(2)}) collective-permute-start(bf16[64,1024]{1,0:T(8,128)(2,1)S(1)} %add_convert_fusion.3), channel_id=1, source_target_pairs={{0,16},{2,18},{4,20},{6,22},{8,24},{10,26},{12,28},{14,30},{1,17},... | collective-permute-start | bytes 393224 | tf_op jit(solution)/shard_map/grad_ring/ppermute | solution.py:91
  46.9 0.1 add_convert_fusion
  47.0 2.6 %collective-permute-start.7 = (bf16[64,1024]{1,0:T(8,128)(2,1)S(1)}, bf16[64,1024]{1,0:T(8,128)(2,1)S(1)}, u32[]{:S(2)}, u32[]{:S(2)}) collective-permute-start(bf16[64,1024]{1,0:T(8,128)(2,1)S(1)} %get-tuple-element.30), channel_id=1, source_target_pairs={{0,14},{2,0},{4,2},{6,4},{8,6},{10,8},{12,10},{14,12},{1,3},{3,5},... | collective-permute-start | bytes 393224 | tf_op jit(solution)/shard_map/grad_ring/ppermute | solution.py:84
  49.6 0.0 copy-start.4
  49.6 5.9 %collective-permute-start.9 = (bf16[64,1024]{1,0:T(8,128)(2,1)S(1)}, bf16[64,1024]{1,0:T(8,128)(2,1)S(1)}, u32[]{:S(2)}, u32[]{:S(2)}) collective-permute-start(bf16[64,1024]{1,0:T(8,128)(2,1)S(1)} %get-tuple-element.31), channel_id=1, source_target_pairs={{0,30},{2,16},{4,18},{6,20},{8,22},{10,24},{12,26},{14,28},{1,19},... | collective-permute-start | bytes 393224 | tf_op jit(solution)/shard_map/grad_ring/ppermute | solution.py:91
  55.5 2.5 %collective-permute-done.9 = bf16[64,1024]{1,0:T(8,128)(2,1)S(1)} collective-permute-done((bf16[64,1024]{1,0:T(8,128)(2,1)S(1)}, bf16[64,1024]{1,0:T(8,128)(2,1)S(1)}, u32[]{:S(2)}, u32[]{:S(2)}) %collective-permute-start.9) | collective-permute-done | bytes 131104 | tf_op jit(solution)/shard_map/grad_ring/ppermute | solution.py:91
  58.0 0.3 fusion.4
  58.3 0.1 reshape.20
  58.4 28.2 %all_to_all.10 = f32[32,2,1024]{2,1,0:T(2,128)S(1)} all-to-all(f32[32,2,1024]{2,1,0:T(2,128)S(1)} %reshape.20), channel_id=1, replica_groups=mesh['xh'=4,'z'=8,'xl'=2,'y'=8,'core'=2] {'xh','z'}, dimensions={0} | all-to-all | bytes 524288 | tf_op jit(solution)/shard_map/replica_sum/all_to_all | solution.py:113
  86.6 0.1 reduce_sum.9
  86.7 0.6 fusion.6
  87.4 16.9 %all_to_all.11 = bf16[32,16,128]{2,1,0:T(8,128)(2,1)S(1)} all-to-all(bf16[32,16,128]{2,1,0:T(8,128)(2,1)S(1)} %broadcast_in_dim.8), channel_id=1, replica_groups=mesh['xh'=4,'z'=8,'xl'=2,'y'=8,'core'=2] {'xh','z'}, dimensions={0} | all-to-all | bytes 262144 | tf_op jit(solution)/shard_map/row_gather/all_to_all | solution.py:122
  104.2 0.7 reshape.21
  (20 shorter events, 0.1 us)
Async XLA Ops:
  2.1 5.3 %collective-permute-start = (bf16[256,3072]{1,0:T(8,128)(2,1)S(1)}, bf16[256,3072]{1,0:T(8,128)(2,1)S(1)}, u32[]{:S(2)}, u32[]{:S(2)}) collective-permute-start(bf16[256,3072]{1,0:T(8,128)(2,1)S(1)} %pad_maximum_fusion.refs_1_), channel_id=1, source_target_pairs={{0,1},{1,0},{2,3},{3,2},{4,5},{5,4},{6,7},{7,6},{8,9},{9,8},{10,11... | collective-permute-start | bytes 4718600 | tf_op jit(solution)/shard_map/core_swap/ppermute | solution.py:75
  8.6 17.5 %collective-permute-start.5 = (bf16[128,1024]{1,0:T(8,128)(2,1)S(1)}, bf16[128,1024]{1,0:T(8,128)(2,1)S(1)}, u32[]{:S(2)}, u32[]{:S(2)}) collective-permute-start(bf16[128,1024]{1,0:T(8,128)(2,1)S(1)} %get-tuple-element.24), channel_id=1, source_target_pairs={{0,14},{2,0},{4,2},{6,4},{8,6},{10,8},{12,10},{14,12},{1,3},{3,5},... | collective-permute-start | bytes 786440 | tf_op jit(solution)/shard_map/grad_ring/ppermute | solution.py:84
  14.8 13.7 %collective-permute-start.2 = (bf16[128,1024]{1,0:T(8,128)(2,1)S(1)}, bf16[128,1024]{1,0:T(8,128)(2,1)S(1)}, u32[]{:S(2)}, u32[]{:S(2)}) collective-permute-start(bf16[128,1024]{1,0:T(8,128)(2,1)S(1)} %get-tuple-element.20), channel_id=1, source_target_pairs={{0,4},{2,6},{4,8},{6,10},{8,12},{10,14},{12,0},{14,2},{1,13},{3,15... | collective-permute-start | bytes 786440 | tf_op jit(solution)/shard_map/grad_ring/ppermute | solution.py:84
  16.7 11.7 %collective-permute-start.3 = (bf16[128,1024]{1,0:T(8,128)(2,1)S(1)}, bf16[128,1024]{1,0:T(8,128)(2,1)S(1)}, u32[]{:S(2)}, u32[]{:S(2)}) collective-permute-start(bf16[128,1024]{1,0:T(8,128)(2,1)S(1)} %get-tuple-element.21), channel_id=1, source_target_pairs={{0,2},{2,4},{4,6},{6,8},{8,10},{10,12},{12,14},{14,0},{1,15},{3,1}... | collective-permute-start | bytes 786440 | tf_op jit(solution)/shard_map/grad_ring/ppermute | solution.py:84
  21.3 23.5 %collective-permute-start.1 = (bf16[128,1024]{1,0:T(8,128)(2,1)S(1)}, bf16[128,1024]{1,0:T(8,128)(2,1)S(1)}, u32[]{:S(2)}, u32[]{:S(2)}) collective-permute-start(bf16[128,1024]{1,0:T(8,128)(2,1)S(1)} %get-tuple-element.15), channel_id=1, source_target_pairs={{0,2},{2,4},{4,6},{6,8},{8,10},{10,12},{12,14},{14,0},{1,15},{3,1}... | collective-permute-start | bytes 786440 | tf_op jit(solution)/shard_map/grad_ring/ppermute | solution.py:84
  26.2 20.7 %collective-permute-start.6 = (bf16[128,1024]{1,0:T(8,128)(2,1)S(1)}, bf16[128,1024]{1,0:T(8,128)(2,1)S(1)}, u32[]{:S(2)}, u32[]{:S(2)}) collective-permute-start(bf16[128,1024]{1,0:T(8,128)(2,1)S(1)} %add_convert_fusion.1), channel_id=1, source_target_pairs={{0,14},{2,0},{4,2},{6,4},{8,6},{10,8},{12,10},{14,12},{1,3},{3,5},... | collective-permute-start | bytes 786440 | tf_op jit(solution)/shard_map/grad_ring/ppermute | solution.py:84
  28.5 29.5 %copy-start = (f32[1,64,1024]{2,1,0:T(8,128)S(1)}, f32[1,64,1024]{2,1,0:T(8,128)}, u32[]{:S(2)}) copy-start(f32[1,64,1024]{2,1,0:T(8,128)} %param.11) | copy-start | bytes 786436
  28.5 29.5 %copy-start.1 = (f32[1,64,1024]{2,1,0:T(8,128)S(1)}, f32[1,64,1024]{2,1,0:T(8,128)}, u32[]{:S(2)}) copy-start(f32[1,64,1024]{2,1,0:T(8,128)} %param.10) | copy-start | bytes 786436
  28.5 29.4 %copy-start.2 = (f32[1,64,1024]{2,1,0:T(8,128)S(1)}, f32[1,64,1024]{2,1,0:T(8,128)}, u32[]{:S(2)}) copy-start(f32[1,64,1024]{2,1,0:T(8,128)} %param.9) | copy-start | bytes 786436
  28.7 26.8 %collective-permute-start.4 = (bf16[64,1024]{1,0:T(8,128)(2,1)S(1)}, bf16[64,1024]{1,0:T(8,128)(2,1)S(1)}, u32[]{:S(2)}, u32[]{:S(2)}) collective-permute-start(bf16[64,1024]{1,0:T(8,128)(2,1)S(1)} %get-tuple-element.28), channel_id=1, source_target_pairs={{0,4},{2,6},{4,8},{6,10},{8,12},{10,14},{12,0},{14,2},{1,13},{3,15... | collective-permute-start | bytes 393224 | tf_op jit(solution)/shard_map/grad_ring/ppermute | solution.py:84
  33.5 21.9 %collective-permute-start.8 = (bf16[64,1024]{1,0:T(8,128)(2,1)S(1)}, bf16[64,1024]{1,0:T(8,128)(2,1)S(1)}, u32[]{:S(2)}, u32[]{:S(2)}) collective-permute-start(bf16[64,1024]{1,0:T(8,128)(2,1)S(1)} %get-tuple-element.29), channel_id=1, source_target_pairs={{0,20},{2,22},{4,24},{6,26},{8,28},{10,30},{12,16},{14,18},{1,29},... | collective-permute-start | bytes 393224 | tf_op jit(solution)/shard_map/grad_ring/ppermute | solution.py:91
  44.9 10.6 %collective-permute-start.10 = (bf16[64,1024]{1,0:T(8,128)(2,1)S(1)}, bf16[64,1024]{1,0:T(8,128)(2,1)S(1)}, u32[]{:S(2)}, u32[]{:S(2)}) collective-permute-start(bf16[64,1024]{1,0:T(8,128)(2,1)S(1)} %add_convert_fusion.3), channel_id=1, source_target_pairs={{0,16},{2,18},{4,20},{6,22},{8,24},{10,26},{12,28},{14,30},{1,17},... | collective-permute-start | bytes 393224 | tf_op jit(solution)/shard_map/grad_ring/ppermute | solution.py:91
  47.0 8.5 %collective-permute-start.7 = (bf16[64,1024]{1,0:T(8,128)(2,1)S(1)}, bf16[64,1024]{1,0:T(8,128)(2,1)S(1)}, u32[]{:S(2)}, u32[]{:S(2)}) collective-permute-start(bf16[64,1024]{1,0:T(8,128)(2,1)S(1)} %get-tuple-element.30), channel_id=1, source_target_pairs={{0,14},{2,0},{4,2},{6,4},{8,6},{10,8},{12,10},{14,12},{1,3},{3,5},... | collective-permute-start | bytes 393224 | tf_op jit(solution)/shard_map/grad_ring/ppermute | solution.py:84
  49.6 37.2 %copy-start.3 = (f32[2,1024]{1,0:T(2,128)S(1)}, f32[2,1024]{1,0:T(2,128)}, u32[]{:S(2)}) copy-start(f32[2,1024]{1,0:T(2,128)} %param.12) | copy-start | bytes 24580
  49.6 37.2 %copy-start.4 = (f32[2,1024]{1,0:T(2,128)S(1)}, f32[2,1024]{1,0:T(2,128)}, u32[]{:S(2)}) copy-start(f32[2,1024]{1,0:T(2,128)} %param.13) | copy-start | bytes 24580
  49.6 8.4 %collective-permute-start.9 = (bf16[64,1024]{1,0:T(8,128)(2,1)S(1)}, bf16[64,1024]{1,0:T(8,128)(2,1)S(1)}, u32[]{:S(2)}, u32[]{:S(2)}) collective-permute-start(bf16[64,1024]{1,0:T(8,128)(2,1)S(1)} %get-tuple-element.31), channel_id=1, source_target_pairs={{0,30},{2,16},{4,18},{6,20},{8,22},{10,24},{12,26},{14,28},{1,19},... | collective-permute-start | bytes 393224 | tf_op jit(solution)/shard_map/grad_ring/ppermute | solution.py:91
